TPU v7x, 32 devices: a whole 2x2x4 slice. The times are simulated.
32 devices in a mesh: group: 2 (over x), tm: 16 (over z, y, core).
Axes of the slice: x: 2, y: 2, z: 4, core: 2. Of those that a mesh axis runs over, the one named last changes fastest.
Arguments:
- noise: float32 [8, 4096], P('group'), parts along dimension 0, may hold values from -6 to 6
- labels: int32 [8], P('group'), parts along dimension 0, may hold values from 0 to 1000
- timesteps: int32 [25], replicated, may hold values from 0 to 399, as said below
- window_start: int32 [1], replicated, may hold values from 0 to 8
- time_weight_in: bfloat16 [256, 768], replicated, may hold values from -0.375 to 0.375
- time_weight_out: bfloat16 [768, 768], replicated, may hold values from -0.21875 to 0.21875
- class_table: bfloat16 [1001, 768], replicated, may hold values from -6 to 6
- patch_weight: bfloat16 [64, 768], replicated, may hold values from -0.75 to 0.75
- query_key_value: bfloat16 [1, 768, 2304], P(None, None, 'tm'), may hold values from -0.21875 to 0.21875
- mix_weight: bfloat16 [1, 768, 768], P(None, None, 'tm'), may hold values from -0.21875 to 0.21875
- expand_weight: bfloat16 [1, 768, 3072], P(None, None, 'tm'), may hold values from -0.21875 to 0.21875
- shrink_weight: bfloat16 [1, 3072, 768], P(None, None, 'tm'), may hold values from -0.109375 to 0.109375
- block_modulation: bfloat16 [1, 768, 4608], P(None, None, 'tm'), may hold values from -0.21875 to 0.21875
- final_modulation: bfloat16 [768, 1536], P(None, 'tm'), may hold values from -0.21875 to 0.21875
- output_weight: bfloat16 [768, 64], replicated, may hold values from -0.21875 to 0.21875
Outputs:
- trajectory: float32 [16, 8, 4096], P('tm', 'group'), parts along dimension 1
There are 2 independent parts, one for each index of `group`. A program takes and returns all parts, laid end to end along the dimension named above; an argument that names none is the same for every part. Nothing has to cross between parts.
Inputs may be any that keep to these rules, and one draw needn't show every extreme that they name: `timesteps`: strictly decreasing; the first entry is 399 and the last is 0.
All inputs are finite; a program needn't handle non-finite values.
Results may differ from a plain program's by a relative error of at most 0.0025.
Values may be sent and summed in bfloat16 or wider, within the bound.
No kernel may reach another device: no remote copies, remote signals or barrier semaphores. Data moves between devices by JAX's collectives and lax.ppermute only.
A program may use at most 128 MiB of HBM per device.

v0:
```python
import math

import jax
import jax.numpy as jnp
from jax import lax
from jax.sharding import PartitionSpec as P

HEADS = 12
ITERS = 2
TRAIN_T = 1000


def carried_in(x, axis, combine, identity):
    count, index = (lax.axis_size(axis), lax.axis_index(axis))
    everything = lax.all_gather(x.astype(jnp.bfloat16), axis)
    start = jnp.broadcast_to(jnp.asarray(identity, x.dtype), x.shape)

    def hop(k, before):
        reached = k < index
        new = combine(before, everything[k].astype(x.dtype))
        return jnp.where(reached, new, before)

    return lax.fori_loop(0, count, hop, start)


def layer_norm(values):
    average = jnp.mean(values, axis=-1, keepdims=True)
    centered = values - average
    variance = jnp.mean(centered * centered, axis=-1, keepdims=True)
    return centered / jnp.sqrt(variance + 1e-06)


def position_table(count, width):
    side = math.isqrt(count)
    quarter = width // 4
    omega = 1.0 / 10000.0 ** (jnp.arange(quarter, dtype=jnp.float32) / quarter)
    index = jnp.arange(count, dtype=jnp.int32)
    first = (index // side).astype(jnp.float32)[:, None] * omega[None, :]
    second = (index % side).astype(jnp.float32)[:, None] * omega[None, :]
    return jnp.concatenate(
        [jnp.sin(first), jnp.cos(first), jnp.sin(second), jnp.cos(second)], axis=1
    )


def plan_terms(timesteps, window_start, step_index, train_steps):
    levels = jnp.arange(train_steps, dtype=jnp.float32)
    betas = 0.0001 + (0.02 - 0.0001) * levels / (train_steps - 1)
    alpha_bar = jnp.cumprod(1.0 - betas)
    current = jnp.take(timesteps, window_start[0] + step_index)
    following = jnp.take(timesteps, window_start[0] + step_index + 1)
    bar_current = jnp.take(alpha_bar, current)
    bar_following = jnp.take(alpha_bar, following)
    scale_state = jnp.sqrt(bar_following / bar_current)
    scale_noise = jnp.sqrt(1.0 - bar_following) - scale_state * jnp.sqrt(1.0 - bar_current)
    return (current, scale_state, scale_noise)


def conditioning(current, labels, time_weight_in, time_weight_out, class_table):
    half = time_weight_in.shape[0] // 2
    rates = jnp.exp(-math.log(10000.0) * jnp.arange(half, dtype=jnp.float32) / half)
    angles = current.astype(jnp.float32)[:, None] * rates[None, :]
    features = jnp.concatenate([jnp.cos(angles), jnp.sin(angles)], axis=1).astype(jnp.bfloat16)
    time_hidden = jax.nn.silu(
        jnp.dot(features, time_weight_in, preferred_element_type=jnp.float32)
    ).astype(jnp.bfloat16)
    time_embed = jnp.dot(time_hidden, time_weight_out, preferred_element_type=jnp.float32)
    selector = (
        labels[:, None] == jnp.arange(class_table.shape[0], dtype=jnp.int32)[None, :]
    ).astype(jnp.bfloat16)
    class_embed = jnp.dot(selector, class_table, preferred_element_type=jnp.float32)
    return jax.nn.silu(time_embed[:, None, :] + class_embed[None, :, :]).astype(jnp.bfloat16)


def network(
    states,
    block_terms,
    final_terms,
    patch_weight,
    query_key_value,
    mix_weight,
    expand_weight,
    shrink_weight,
    output_weight,
    heads,
):
    count = states.shape[0]
    patch = patch_weight.shape[0]
    width = patch_weight.shape[1]
    tokens = states.shape[1] // patch
    head_dim = width // heads
    patches = states.reshape(count * tokens, patch).astype(jnp.bfloat16)
    hidden = jnp.dot(patches, patch_weight, preferred_element_type=jnp.float32).reshape(
        count, tokens, width
    )
    hidden = hidden + position_table(tokens, width)[None]
    blocks = block_terms[0].reshape(count, 6, 1, width)
    normed = (layer_norm(hidden) * (1.0 + blocks[:, 1]) + blocks[:, 0]).astype(jnp.bfloat16)
    projected = jnp.dot(
        normed.reshape(count * tokens, width),
        query_key_value[0],
        preferred_element_type=jnp.float32,
    ).astype(jnp.bfloat16)
    projected = projected.reshape(count, tokens, 3, heads, head_dim)
    scores = jnp.einsum(
        "rqhd,rkhd->rhqk",
        projected[:, :, 0],
        projected[:, :, 1],
        preferred_element_type=jnp.float32,
    ) / math.sqrt(head_dim)
    raised = jnp.exp(scores)
    weights = (raised / jnp.sum(raised, axis=-1, keepdims=True)).astype(jnp.bfloat16)
    attended = jnp.einsum(
        "rhqk,rkhd->rqhd", weights, projected[:, :, 2], preferred_element_type=jnp.float32
    ).astype(jnp.bfloat16)
    mixed = jnp.dot(
        attended.reshape(count * tokens, width), mix_weight[0], preferred_element_type=jnp.float32
    )
    hidden = hidden + blocks[:, 2] * mixed.reshape(count, tokens, width)
    normed = (layer_norm(hidden) * (1.0 + blocks[:, 4]) + blocks[:, 3]).astype(jnp.bfloat16)
    expanded = jax.nn.gelu(
        jnp.dot(
            normed.reshape(count * tokens, width),
            expand_weight[0],
            preferred_element_type=jnp.float32,
        ),
        approximate=True,
    ).astype(jnp.bfloat16)
    shrunk = jnp.dot(expanded, shrink_weight[0], preferred_element_type=jnp.float32)
    hidden = hidden + blocks[:, 5] * shrunk.reshape(count, tokens, width)
    final = final_terms.reshape(count, 2, 1, width)
    normed = (layer_norm(hidden) * (1.0 + final[:, 1]) + final[:, 0]).astype(jnp.bfloat16)
    return jnp.dot(
        normed.reshape(count * tokens, width), output_weight, preferred_element_type=jnp.float32
    ).reshape(count, tokens * patch)


def add_terms(earlier, later):
    return earlier + later


def body(
    noise,
    labels,
    timesteps,
    window_start,
    time_weight_in,
    time_weight_out,
    class_table,
    patch_weight,
    query_key_value,
    mix_weight,
    expand_weight,
    shrink_weight,
    block_modulation,
    final_modulation,
    output_weight,
):
    position = lax.axis_index("tm")
    current, scale_state, scale_noise = plan_terms(timesteps, window_start, position[None], TRAIN_T)
    condition = conditioning(current, labels, time_weight_in, time_weight_out, class_table)[0]
    full_query, full_mix, full_expand, full_shrink = (
        lax.all_gather(query_key_value, "tm", axis=2, tiled=True),
        lax.all_gather(mix_weight, "tm", axis=2, tiled=True),
        lax.all_gather(expand_weight, "tm", axis=2, tiled=True),
        lax.all_gather(shrink_weight, "tm", axis=2, tiled=True),
    )
    everyone = lax.all_gather(condition, "tm", axis=0, tiled=True)
    block_part = jnp.einsum(
        "rd,ldc->lrc", everyone, block_modulation, preferred_element_type=jnp.float32
    )
    final_part = jnp.dot(everyone, final_modulation, preferred_element_type=jnp.float32)[None]
    block_terms, final_both = (
        lax.all_to_all(
            block_part.astype(jnp.bfloat16), "tm", split_axis=1, concat_axis=2, tiled=True
        ).astype(block_part.dtype),
        lax.all_to_all(
            final_part.astype(jnp.bfloat16), "tm", split_axis=1, concat_axis=2, tiled=True
        ).astype(final_part.dtype),
    )
    final_terms = final_both[0]
    states = noise
    running = noise
    for sweep in range(ITERS):
        predicted = network(
            states,
            block_terms,
            final_terms,
            patch_weight,
            full_query,
            full_mix,
            full_expand,
            full_shrink,
            output_weight,
            HEADS,
        )
        drift = (scale_state[0] - 1.0) * states + scale_noise[0] * predicted
        before = carried_in(drift, "tm", add_terms, jnp.zeros_like(drift))
        running = before + drift
        states = noise + before
    return (noise + running)[None]


def solution(mesh):
    return jax.shard_map(
        body,
        mesh=mesh,
        in_specs=(
            P("group", None),
            P("group"),
            P(),
            P(),
            P(),
            P(),
            P(),
            P(),
            P(None, None, "tm"),
            P(None, None, "tm"),
            P(None, None, "tm"),
            P(None, None, "tm"),
            P(None, None, "tm"),
            P(None, "tm"),
            P(),
        ),
        out_specs=P("tm", "group", None),
        check_vma=False,
    )
```

profile of v0, /device:TPU:0, one launch (start us, length us, event | category | flops | bytes accessed | tf_op | source)
XLA Modules:
  0.0 296.3 jit_solution(10705091431752967225)
XLA Ops:
  15.3 23.5 %all-gather.2 = bf16[16,4,768]{2,1,0:T(4,128)(2,1)S(1)} all-gather(bf16[1,4,768]{2,1,0:T(4,128)(2,1)S(1)} %fusion.65), channel_id=1, replica_groups=mesh['group'=2,'tm'=16] {'tm'}, dimensions={0}, use_global_device_ids=true | all-gather | bytes 104448 | tf_op jit(solution)/shard_map/all_gather | solution.py:167
  41.0 3.5 %all-to-all-start.1 = ((bf16[16,2,192]{2,1,0:T(2,128)(2,1)}), bf16[16,2,192]{2,1,0:T(2,128)(2,1)S(1)}, u32[]{:S(2)}, u32[]{:S(2)}) async-start(bf16[16,2,192]{2,1,0:T(2,128)(2,1)} %reshape.443), calls=%async_computation.1 | async-start | bytes 32768 | tf_op jit(solution)/shard_map/all_to_all | solution.py:176
  52.0 6.0 %all-to-all-start = ((bf16[16,2,576]{2,1,0:T(2,128)(2,1)}), bf16[16,2,576]{2,1,0:T(2,128)(2,1)S(1)}, u32[]{:S(2)}, u32[]{:S(2)}) async-start(bf16[16,2,576]{2,1,0:T(2,128)(2,1)} %reshape.441), calls=%async_computation | async-start | bytes 81920 | tf_op jit(solution)/shard_map/all_to_all | solution.py:173
  58.3 6.4 %all-to-all-done = bf16[16,2,576]{2,1,0:T(2,128)(2,1)S(1)} async-done(((bf16[16,2,576]{2,1,0:T(2,128)(2,1)}), bf16[16,2,576]{2,1,0:T(2,128)(2,1)S(1)}, u32[]{:S(2)}, u32[]{:S(2)}) %all-to-all-start) | async-done | bytes 36896 | tf_op jit(solution)/shard_map/all_to_all | solution.py:173
  67.1 4.3 %convolution_convert_fusion.1 = bf16[256,2304]{1,0:T(8,128)(2,1)} fusion(bf16[256,768]{1,0:T(8,128)(2,1)S(1)} %bitcast.222, bf16[1,768,2304]{1,2,0:T(8,128)(2,1)} %all-gather.10.cloned.1.call-done), kind=kOutput, calls=%fused_computation.13 | convolution fusion | flops 906559488 | bytes 5111808 | tf_op jit(solution)/shard_map/dot_general | solution.py:98
  73.0 2.6 reshape.298
  75.5 4.0 %fusion.84 = (bf16[4,64,1,12,64]{1,0,4,3,2:T(4,128)(2,1)}, bf16[4,64,1,12,64]{1,0,4,3,2:T(4,128)(2,1)S(1)}, bf16[4,64,1,12,64]{1,0,4,3,2:T(4,128)(2,1)}) fusion(bf16[4,64,3,12,64]{1,0,4,3,2:T(4,128)(2,1)} %reshape.298), kind=kLoop, calls=%fused_computation.147 | loop fusion | bytes 2359296 | tf_op jit(solution)/shard_map/slice | solution.py:113
  83.0 3.2 %multiply_exponential_fusion.1 = f32[4,12,64,64]{2,3,1,0:T(8,128)} fusion(bf16[4,64,1,12,64]{4,1,3,0,2:T(8,128)(2,1)} %copy.80, bf16[4,64,1,12,64]{4,1,3,0,2:T(8,128)(2,1)} %copy.79), kind=kOutput, calls=%fused_computation.35 | convolution fusion | flops 25362432 | bytes 1572864 | tf_op jit(solution)/shard_map/rqhd,rkhd->rhqk/dot_general | solution.py:104
  86.2 3.3 %convolution_convert_fusion.3 = bf16[4,12,64,64]{3,2,1,0:T(8,128)(2,1)} fusion(f32[4,12,64,64]{2,3,1,0:T(8,128)} %multiply_exponential_fusion.1, bf16[4,64,1,12,64]{1,0,4,3,2:T(4,128)(2,1)S(1)} %copy-done.11), kind=kOutput, calls=%fused_computation.37 | convolution fusion | flops 25758784 | bytes 1572864 | tf_op jit(solution)/shard_map/rhqk,rkhd->rqhd/dot_general | solution.py:112
  89.6 9.8 %all-gather.12.cloned.1.call-done = bf16[1,768,768]{1,2,0:T(8,128)(2,1)} async-done(((bf16[1,768,48]{1,2,0:T(8,128)(2,1)}), bf16[1,768,768]{1,2,0:T(8,128)(2,1)}) %all-gather.12.cloned.1.call-update) | async-done | bytes 1179664 | tf_op jit(solution)/shard_map/all_gather | solution.py:163
  99.3 2.4 fusion.89
  102.2 51.8 %all-gather.14.cloned.1.call-done = bf16[1,768,3072]{1,2,0:T(8,128)(2,1)} async-done(((bf16[1,768,192]{1,2,0:T(8,128)(2,1)}), bf16[1,768,3072]{1,2,0:T(8,128)(2,1)}) %all-gather.14.cloned.1.call-update) | async-done | bytes 4718608 | tf_op jit(solution)/shard_map/all_gather | solution.py:164
  154.0 5.3 %fusion.19 = bf16[256,3072]{1,0:T(8,128)(2,1)} fusion(bf16[256,768]{1,0:T(8,128)(2,1)S(1)} %bitcast.223, bf16[1,768,3072]{1,2,0:T(8,128)(2,1)} %all-gather.14.cloned.1.call-done), kind=kOutput, calls=%fused_computation.23 | convolution fusion | flops 1215037440 | bytes 6684672 | tf_op jit(solution)/shard_map/dot_general | solution.py:121
  159.3 48.8 %all-gather.16.cloned.1.call-done = bf16[1,3072,768]{1,2,0:T(8,128)(2,1)} async-done(((bf16[1,3072,48]{1,2,0:T(8,128)(2,1)}), bf16[1,3072,768]{1,2,0:T(8,128)(2,1)}) %all-gather.16.cloned.1.call-update) | async-done | bytes 4718608 | tf_op jit(solution)/shard_map/all_gather | solution.py:165
  208.1 4.4 %fusion.90 = (f32[4,64]{1,0:T(4,128)S(1)}, f32[4,64,768]{2,1,0:T(8,128)S(1)}) fusion(f32[4,64,768]{2,1,0:T(8,128)S(1)} %get-tuple-element.282, bf16[4,64,3072]{2,1,0:T(8,128)(2,1)} %bitcast.248, bf16[1,3072,768]{1,2,0:T(8,128)(2,1)} %all-gather.16.cloned.1.call-done, f32[4,768]{1,0:T(4,128)S(1)} %bitcast.243), kind=kOutput, calls=%fused_computation.153 | convolution fusion | flops 1208549120 | bytes 7877632 | tf_op jit(solution)/shard_map/dot_general | solution.py:128
  213.6 20.6 %all-gather.3 = bf16[16,4,4096]{2,1,0:T(4,128)(2,1)S(1)} all-gather(bf16[1,4,4096]{2,1,0:T(4,128)(2,1)S(1)} %fusion.63), channel_id=2, replica_groups=mesh['group'=2,'tm'=16] {'tm'}, dimensions={0}, use_global_device_ids=true | all-gather | bytes 557056 | tf_op jit(solution)/shard_map/all_gather | solution.py:15
  237.0 4.2 %convolution_convert_fusion = bf16[256,2304]{1,0:T(8,128)(2,1)} fusion(bf16[256,768]{1,0:T(8,128)(2,1)S(1)} %bitcast.224, bf16[1,768,2304]{1,2,0:T(8,128)(2,1)} %all-gather.10.cloned.1.call-done), kind=kOutput, calls=%fused_computation.12 | convolution fusion | flops 906559488 | bytes 5111808 | tf_op jit(solution)/shard_map/dot_general | solution.py:98
  242.8 2.5 reshape.302
  245.3 4.1 %fusion.83 = (bf16[4,64,1,12,64]{1,0,4,3,2:T(4,128)(2,1)}, bf16[4,64,1,12,64]{1,0,4,3,2:T(4,128)(2,1)S(1)}, bf16[4,64,1,12,64]{1,0,4,3,2:T(4,128)(2,1)}) fusion(bf16[4,64,3,12,64]{1,0,4,3,2:T(4,128)(2,1)} %reshape.302), kind=kLoop, calls=%fused_computation.146 | loop fusion | bytes 2359296 | tf_op jit(solution)/shard_map/slice | solution.py:113
  249.4 2.2 copy.82
  252.9 3.1 %multiply_exponential_fusion = f32[4,12,64,64]{2,3,1,0:T(8,128)} fusion(bf16[4,64,1,12,64]{4,1,3,0,2:T(8,128)(2,1)} %copy.83, bf16[4,64,1,12,64]{4,1,3,0,2:T(8,128)(2,1)} %copy.82), kind=kOutput, calls=%fused_computation.33 | convolution fusion | flops 25362432 | bytes 1572864 | tf_op jit(solution)/shard_map/rqhd,rkhd->rhqk/dot_general | solution.py:104
  256.0 3.5 %convolution_convert_fusion.2 = bf16[4,12,64,64]{3,2,1,0:T(8,128)(2,1)} fusion(f32[4,12,64,64]{2,3,1,0:T(8,128)} %multiply_exponential_fusion, bf16[4,64,1,12,64]{1,0,4,3,2:T(4,128)(2,1)} %get-tuple-element.255), kind=kOutput, calls=%fused_computation.36 | convolution fusion | flops 25758784 | bytes 1572864 | tf_op jit(solution)/shard_map/rhqk,rkhd->rqhd/dot_general | solution.py:112
  262.1 4.3 %fusion.31 = bf16[256,3072]{1,0:T(8,128)(2,1)S(1)} fusion(bf16[256,768]{1,0:T(8,128)(2,1)S(1)} %bitcast.225, bf16[1,768,3072]{1,2,0:T(8,128)(2,1)} %all-gather.14.cloned.1.call-done), kind=kOutput, calls=%fused_computation.31 | convolution fusion | flops 1215037440 | bytes 6684672 | tf_op jit(solution)/shard_map/dot_general | solution.py:121
  269.0 18.9 %all-gather.4 = bf16[16,4,4096]{2,1,0:T(4,128)(2,1)S(1)} all-gather(bf16[1,4,4096]{2,1,0:T(4,128)(2,1)S(1)} %convert_bitcast_fusion), channel_id=3, replica_groups=mesh['group'=2,'tm'=16] {'tm'}, dimensions={0}, use_global_device_ids=true | all-gather | bytes 557056 | tf_op jit(solution)/shard_map/all_gather | solution.py:15
  (201 shorter events, 38.2 us)
Async XLA Ops:
  6.5 8.4 %copy-start = (bf16[1001,768]{1,0:T(8,128)(2,1)S(1)}, bf16[1001,768]{1,0:T(8,128)(2,1)}, u32[]{:S(2)}) copy-start(bf16[1001,768]{1,0:T(8,128)(2,1)} %param.25) | copy-start | bytes 4612612
  6.5 8.4 %copy-start.27 = (s32[4]{0:T(128)S(1)}, s32[4]{0:T(128)}, u32[]{:S(2)}) copy-start(s32[4]{0:T(128)} %param.20) | copy-start | bytes 52
  6.5 32.3 %copy-start.17 = (bf16[768,96]{0,1:T(8,128)(2,1)S(1)}, bf16[768,96]{0,1:T(8,128)(2,1)}, u32[]{:S(2)}) copy-start(bf16[768,96]{0,1:T(8,128)(2,1)} %param.32) | copy-start | bytes 442372
  6.5 37.9 %copy-start.8 = (f32[4,4096]{1,0:T(4,128)S(1)}, f32[4,4096]{1,0:T(4,128)}, u32[]{:S(2)}) copy-start(f32[4,4096]{1,0:T(4,128)} %param.19) | copy-start | bytes 196612
  6.5 60.6 %all-gather.10.cloned.1.call-start = ((), (), s32[]{:S(2)}) async-start(), calls=%async_computation.2 | async-start | bytes 3760128 | tf_op jit(solution)/shard_map/all_gather | solution.py:162
  7.3 92.1 %all-gather.12.cloned.1.call-start = ((), (), s32[]{:S(2)}) async-start(), calls=%async_computation.3 | async-start | bytes 1253376 | tf_op jit(solution)/shard_map/all_gather | solution.py:163
  8.0 146.0 %all-gather.14.cloned.1.call-start = ((), (), s32[]{:S(2)}) async-start(), calls=%async_computation.4 | async-start | bytes 5013504 | tf_op jit(solution)/shard_map/all_gather | solution.py:164
  8.8 199.4 %all-gather.16.cloned.1.call-start = ((), (), s32[]{:S(2)}) async-start(), calls=%async_computation.5 | async-start | bytes 5013504 | tf_op jit(solution)/shard_map/all_gather | solution.py:165
  12.1 34.4 %copy-start.13 = (bf16[64,768]{1,0:T(8,128)(2,1)S(1)}, bf16[64,768]{1,0:T(8,128)(2,1)}, u32[]{:S(2)}) copy-start(bf16[64,768]{1,0:T(8,128)(2,1)} %param.26) | copy-start | bytes 294916
  14.9 32.2 %copy-start.12 = (bf16[1,768,288]{1,2,0:T(8,128)(2,1)S(1)}, bf16[1,768,288]{1,2,0:T(8,128)(2,1)}, u32[]{:S(2)}) copy-start(bf16[1,768,288]{1,2,0:T(8,128)(2,1)} %param.31) | copy-start | bytes 1327108
  41.0 11.0 %all-to-all-start.1 = ((bf16[16,2,192]{2,1,0:T(2,128)(2,1)}), bf16[16,2,192]{2,1,0:T(2,128)(2,1)S(1)}, u32[]{:S(2)}, u32[]{:S(2)}) async-start(bf16[16,2,192]{2,1,0:T(2,128)(2,1)} %reshape.443), calls=%async_computation.1 | async-start | bytes 32768 | tf_op jit(solution)/shard_map/all_to_all | solution.py:176
  52.0 12.7 %all-to-all-start = ((bf16[16,2,576]{2,1,0:T(2,128)(2,1)}), bf16[16,2,576]{2,1,0:T(2,128)(2,1)S(1)}, u32[]{:S(2)}, u32[]{:S(2)}) async-start(bf16[16,2,576]{2,1,0:T(2,128)(2,1)} %reshape.441), calls=%async_computation | async-start | bytes 81920 | tf_op jit(solution)/shard_map/all_to_all | solution.py:173
  86.2 13.1 %copy-start.24 = (f32[4,1,1,768]{3,0,1,2:T(4,128)S(1)}, f32[4,1,1,768]{3,0,1,2:T(4,128)}, u32[]{:S(2)}) copy-start(f32[4,1,1,768]{3,0,1,2:T(4,128)} %copy.109) | copy-start | bytes 36868
  89.6 12.5 %copy-start.18 = (f32[4,1,1,768]{3,0,1,2:T(4,128)S(1)}, f32[4,1,1,768]{3,0,1,2:T(4,128)}, u32[]{:S(2)}) copy-start(f32[4,1,1,768]{3,0,1,2:T(4,128)} %copy.105) | copy-start | bytes 36868
  154.0 54.1 %copy-start.25 = (f32[4,1,1,768]{3,0,1,2:T(4,128)S(1)}, f32[4,1,1,768]{3,0,1,2:T(4,128)}, u32[]{:S(2)}) copy-start(f32[4,1,1,768]{3,0,1,2:T(4,128)} %copy.106) | copy-start | bytes 36868
  208.1 4.9 %copy-start.15 = (bf16[768,64]{0,1:T(8,128)(2,1)S(1)}, bf16[768,64]{0,1:T(8,128)(2,1)}, u32[]{:S(2)}) copy-start(bf16[768,64]{0,1:T(8,128)(2,1)} %param.33) | copy-start | bytes 294916
  212.5 21.7 %copy-start.2 = (f32[4,4096]{1,0:T(4,128)S(1)}, f32[4,4096]{1,0:T(4,128)}, u32[]{:S(2)}) copy-start(f32[4,4096]{1,0:T(4,128)} %custom-call) | copy-start | bytes 196612
  212.5 23.6 %copy-start.7 = (f32[64,768]{1,0:T(8,128)S(1)}, f32[64,768]{1,0:T(8,128)}, u32[]{:S(2)}) copy-start(f32[64,768]{1,0:T(8,128)} %copy-done.6) | copy-start | bytes 589828
  212.5 23.6 %copy-start.14 = (bf16[64,768]{1,0:T(8,128)(2,1)S(1)}, bf16[64,768]{1,0:T(8,128)(2,1)}, u32[]{:S(2)}) copy-start(bf16[64,768]{1,0:T(8,128)(2,1)} %param.26) | copy-start | bytes 294916
  213.0 23.7 %copy-start.21 = (f32[4,1,1,768]{3,0,1,2:T(4,128)S(1)}, f32[4,1,1,768]{3,0,1,2:T(4,128)}, u32[]{:S(2)}) copy-start(f32[4,1,1,768]{3,0,1,2:T(4,128)} %copy-done.20) | copy-start | bytes 36868
  213.0 23.7 %copy-start.23 = (f32[4,1,1,768]{3,0,1,2:T(4,128)S(1)}, f32[4,1,1,768]{3,0,1,2:T(4,128)}, u32[]{:S(2)}) copy-start(f32[4,1,1,768]{3,0,1,2:T(4,128)} %copy-done.22) | copy-start | bytes 36868
  261.9 4.5 %slice-start = ((s8[4718592]{0:T(1024)(128)(4,1)}), s8[4194304]{0:T(1024)(128)(4,1)S(1)}, s32[]{:S(2)}) async-start(s8[4718592]{0:T(1024)(128)(4,1)} %bitcast.246), calls=%async_computation.6 | async-start | bytes 8388608
  262.1 4.3 %copy-start.26 = (f32[4,1,1,768]{3,0,1,2:T(4,128)S(1)}, f32[4,1,1,768]{3,0,1,2:T(4,128)}, u32[]{:S(2)}) copy-start(f32[4,1,1,768]{3,0,1,2:T(4,128)} %copy.106) | copy-start | bytes 36868
  268.0 19.9 %copy-start.5 = (f32[4,4096]{1,0:T(4,128)S(1)}, f32[4,4096]{1,0:T(4,128)}, u32[]{:S(2)}) copy-start(f32[4,4096]{1,0:T(4,128)} %custom-call.1) | copy-start | bytes 196612
  (12 other events, 23.9 us)
Sparse Core Ops, SparseCore 0:
  9.7 49.9 all-gather.9
  62.0 37.3 all-gather.11
  101.6 52.3 all-gather.13
  156.2 51.9 all-gather.15
where the time goes:
time: 297 us; the launch traced here: 296 us
  waiting for transfers between devices  119 us (40%)
  blocking collectives  63 us (21%)
  matrix products  46.3 us (16%)
  local copies, waits for them, and re-layouts  31.9 us (11%)
  between operations  17.4 us (6%)
  starting transfers between devices  9.61 us (3%)
  other arithmetic  8.2 us (3%)
    all_gather x1, waiting for transfers between devices, body(): lax.all_gather(expand_weight, 'tm', axis=2, tiled=True)  51.8 us
    all_gather x1, waiting for transfers between devices, body(): lax.all_gather(shrink_weight, 'tm', axis=2, tiled=True)  48.8 us
    all_gather x2, blocking collectives, carried_in(): everything = lax.all_gather(x.astype(jnp.bfloat16), axis)  39.5 us
    all_gather x1, blocking collectives, body(): everyone = lax.all_gather(condition, 'tm', axis=0, tiled=True)  23.5 us
    unnamed x78, local copies, waits for them, and re-layouts  12.4 us
    all_gather x1, waiting for transfers between devices, body(): lax.all_gather(mix_weight, 'tm', axis=2, tiled=True)  9.78 us
    dot_general x2, matrix products, network(): jnp.dot(normed.reshape(count * tokens, width), expand_weight[0], preferre...  9.56 us
    dot_general x2, matrix products, network(): jnp.dot(normed.reshape(count * tokens, width), query_key_value[0], prefer...  8.47 us
  transfers between devices with their start and end apart: 6, of which 4 were waited for; matrix products, arithmetic and copies ran while one was open for 15% of the time, Pallas kernels for 0%

commit v1 on v0

v1 whole, which is shorter than its diff:
```python
import functools
import math

import jax
import jax.numpy as jnp
from jax import lax
from jax.experimental import pallas as pl
from jax.experimental.pallas import tpu as pltpu
from jax.sharding import PartitionSpec as P

HEADS = 12
ITERS = 2
TRAIN_T = 1000
WINDOW = 5
BF16 = jnp.bfloat16
F32 = jnp.float32


def plan_terms(timesteps, window_start, step_index, train_steps):
    levels = jnp.arange(train_steps, dtype=F32)
    betas = 0.0001 + (0.02 - 0.0001) * levels / (train_steps - 1)
    alpha_bar = jnp.cumprod(1.0 - betas)
    current = jnp.take(timesteps, window_start[0] + step_index)
    following = jnp.take(timesteps, window_start[0] + step_index + 1)
    bar_current = jnp.take(alpha_bar, current)
    bar_following = jnp.take(alpha_bar, following)
    scale_state = jnp.sqrt(bar_following / bar_current)
    scale_noise = jnp.sqrt(1.0 - bar_following) - scale_state * jnp.sqrt(1.0 - bar_current)
    return (current, scale_state, scale_noise)


def conditioning(current, labels, time_weight_in, time_weight_out, class_table):
    half = time_weight_in.shape[0] // 2
    rates = jnp.exp(-math.log(10000.0) * jnp.arange(half, dtype=F32) / half)
    angles = current.astype(F32)[:, None] * rates[None, :]
    features = jnp.concatenate([jnp.cos(angles), jnp.sin(angles)], axis=1).astype(BF16)
    time_hidden = jax.nn.silu(
        jnp.dot(features, time_weight_in, preferred_element_type=F32)
    ).astype(BF16)
    time_embed = jnp.dot(time_hidden, time_weight_out, preferred_element_type=F32)
    selector = (
        labels[:, None] == jnp.arange(class_table.shape[0], dtype=jnp.int32)[None, :]
    ).astype(BF16)
    class_embed = jnp.dot(selector, class_table, preferred_element_type=F32)
    return jax.nn.silu(time_embed[:, None, :] + class_embed[None, :, :]).astype(BF16)


def position_columns(count, width):
    side = math.isqrt(count)
    quarter = width // 4
    omega = 1.0 / 10000.0 ** (jnp.arange(quarter, dtype=F32) / quarter)
    index = jnp.arange(count, dtype=jnp.int32)
    first = omega[:, None] * (index // side).astype(F32)[None, :]
    second = omega[:, None] * (index % side).astype(F32)[None, :]
    return jnp.concatenate(
        [jnp.sin(first), jnp.cos(first), jnp.sin(second), jnp.cos(second)], axis=0
    )


def ring_order(count):
    return list(range(0, count, 2)) + list(range(1, count, 2))[::-1]


class Mover:
    def __init__(self, groups, count):
        self.groups, self.count, self.sent = groups, count, []

    def swap(self, value, distance):
        return self._send(value, lambda i: i ^ distance, lambda g: g)

    def across(self, value):
        return self._send(value, lambda i: i, lambda g: g ^ 1)

    def ring(self, value):
        order = ring_order(self.count // 4)
        after = {z: order[(k + 1) % len(order)] for k, z in enumerate(order)}
        return self._send(value, lambda i: after[i // 4] * 4 + i % 4, lambda g: g)

    def _send(self, value, target, side):
        if len(self.sent) >= WINDOW:
            value, _ = lax.optimization_barrier((value, self.sent[-WINDOW]))
        pairs = [
            (g * self.count + i, side(g) * self.count + target(i))
            for g in range(self.groups)
            for i in range(self.count)
        ]
        value = lax.ppermute(value, ("group", "tm"), pairs)
        self.sent.append(value)
        return value


def spread_weights(first, second, groups, count):
    mover = Mover(groups, count)
    depth = count // 4
    p, h = first.shape[0], second.shape[1]
    side = lax.axis_index("group")
    mine = jnp.where(side == 0, second[0], second[1])
    held = {("p", 0, 0): first, ("h", 0, 0): mine}
    first_out, second_out = [], []
    everything = jnp.concatenate([first, second[0], second[1]], axis=0)

    def z(kind, r):
        held[kind, r, 0] = mover.ring(held[kind, r - 1, 0])

    def y(kind, r):
        held[kind, r, 1] = mover.swap(held[kind, r, 0], 2)

    stacks = {}

    def x(j, keys):
        stack = jnp.concatenate([held[k] for k in keys], axis=0)
        stacks[j] = (keys, stack, mover.across(stack))

    def core_second(j):
        keys, stack, other = stacks[j]
        buffer = jnp.concatenate([stack, other], axis=0)
        received = mover.swap(buffer, 1)
        for core, data in ((0, buffer), (1, received)):
            pieces = []
            for half in range(2):
                for k, (_, r, dy) in enumerate(keys):
                    pieces.append(((half * len(keys) + k) * h, r, dy, core, half))
            second_out.append((data, pieces))

    def core_first(keys):
        buffer = jnp.concatenate([held[k] for k in keys], axis=0)
        received = mover.swap(buffer, 1)
        for core, data in ((0, buffer), (1, received)):
            pieces = [(k * p, r, dy, core, 0) for k, (_, r, dy) in enumerate(keys)]
            first_out.append((data, pieces))

    def core_own():
        received = mover.swap(everything, 1)
        for core, data in ((0, everything), (1, received)):
            first_out.append((data, [(0, 0, 0, core, 0)]))
            second_out.append((data, [(p, 0, 0, core, "lo"), (p + h, 0, 0, core, "hi")]))

    group = lambda j: [("h", j + 1, 0), ("h", j, 1)] if j + 1 < depth else [("h", j, 1)]
    z("p", 1), y("p", 0), z("h", 1), y("h", 0), core_own()
    z("p", 2), x(0, group(0)), y("p", 1), z("h", 2), y("h", 1)
    z("p", 3), y("p", 2), x(1, group(1)), z("h", 3)
    core_first([("p", 1, 0), ("p", 0, 1), ("p", 1, 1)])
    y("h", 2), y("p", 3), core_second(0), x(2, group(2))
    core_first([("p", 2, 0), ("p", 3, 0), ("p", 2, 1), ("p", 3, 1)])
    y("h", 3), core_second(1), x(3, group(3)), core_second(2), core_second(3)
    return first_out, second_out


def piece_owners(count):
    position = lax.axis_index("tm")
    depth = count // 4
    order = ring_order(depth)
    place = jnp.asarray([order.index(z) for z in range(depth)], jnp.int32)[position // 4]
    rows = []
    for r in range(depth):
        z = jnp.asarray(order, jnp.int32)[(place - r + depth) % depth]
        for dy in range(2):
            for core in range(2):
                rows.append(z * 4 + ((position % 4) ^ (2 * dy + core)))
    return jnp.stack(rows).astype(jnp.int32)


def norm(hidden, shift, scale):
    average = jnp.mean(hidden, axis=0, keepdims=True)
    centered = hidden - average
    variance = jnp.mean(centered * centered, axis=0, keepdims=True)
    return (centered * lax.rsqrt(variance + 1e-06) * (1.0 + scale) + shift).astype(BF16)


def dims_of(terms, tokens, samples):
    return samples, tokens // samples


def spread_terms(terms_ref, which, width, tokens, samples):
    each = tokens // samples
    rows = terms_ref.shape[0]
    own = lax.broadcasted_iota(jnp.int32, (rows, tokens), 0)
    of = lax.broadcasted_iota(jnp.int32, (rows, tokens), 1) // each
    pick = jnp.where(own == of, 1.0, 0.0).astype(BF16)
    return lax.dot_general(
        terms_ref[:, which * width : (which + 1) * width],
        pick,
        (((0,), (0,)), ((), ())),
        preferred_element_type=F32,
    )


def attention_part(state_ref, patch_ref, place_ref, terms_ref, wq, wm, qkv, att, ready, heads, samples):
    width, tokens = place_ref.shape
    each = tokens // samples
    size = width // heads
    terms = lambda k: spread_terms(terms_ref, k, width, tokens, samples)
    hidden = (
        jnp.dot(patch_ref[...], state_ref[...].astype(BF16), preferred_element_type=F32)
        + place_ref[...]
    )
    normed = norm(hidden, terms(0), terms(1))
    ready[0]()
    for k in range(3):
        rows = pl.ds(k * width, width)
        qkv[rows, :] = jnp.dot(wq[rows, :], normed, preferred_element_type=F32).astype(BF16)
    sample_of = lax.broadcasted_iota(jnp.int32, (each, tokens), 1) // each
    scale = 1.0 / math.sqrt(size)
    for k in range(heads):
        query = qkv[pl.ds(k * size, size), :]
        key = qkv[pl.ds(width + k * size, size), :]
        value = qkv[pl.ds(2 * width + k * size, size), :]
        scores = lax.dot_general(
            key, query, (((0,), (0,)), ((), ())), preferred_element_type=F32
        )
        mine = scores[0:each]
        for s in range(1, samples):
            mine = jnp.where(sample_of == s, scores[s * each : (s + 1) * each], mine)
        raised = jnp.exp(mine * scale)
        weights = (raised / jnp.sum(raised, axis=0, keepdims=True)).astype(F32)
        spread = jnp.concatenate(
            [jnp.where(sample_of == s, weights, 0.0).astype(BF16) for s in range(samples)], axis=0
        )
        att[pl.ds(k * size, size), :] = jnp.dot(
            value, spread, preferred_element_type=F32
        ).astype(BF16)
    ready[1]()
    mixed = jnp.dot(wm[...], att[...], preferred_element_type=F32)
    return hidden + terms(2) * mixed


def feed_part(hidden, state_ref, terms_ref, out_ref, scalars_ref, we, ws, mid, ready, samples):
    width, tokens = hidden.shape
    terms = lambda k: spread_terms(terms_ref, k, width, tokens, samples)
    normed = norm(hidden, terms(3), terms(4))
    ready[2]()
    for k in range(we.shape[0] // width):
        rows = pl.ds(k * width, width)
        mid[rows, :] = jax.nn.gelu(
            jnp.dot(we[rows, :], normed, preferred_element_type=F32), approximate=True
        ).astype(BF16)
    ready[3]()
    shrunk = jnp.zeros_like(hidden)
    for k in range(we.shape[0] // width):
        rows = pl.ds(k * width, width)
        shrunk = shrunk + jnp.dot(ws[rows, :], mid[rows, :], preferred_element_type=F32)
    hidden = hidden + terms(5) * shrunk
    normed = norm(hidden, terms(6), terms(7))
    predicted = jnp.dot(out_ref[...], normed, preferred_element_type=F32)
    return (scalars_ref[0] - 1.0) * state_ref[...] + scalars_ref[1] * predicted


def network_kernel(parts, sources, sizes, heads, samples, *refs):
    nq, nm, ne, ns, width = sizes
    refs = list(refs)
    take = lambda: refs.pop(0)
    owners, scalars, state, patch, place, terms, out_weight = (take() for _ in range(7))
    before = None if 0 in parts else take()
    buffers = [take() for _ in sources]
    results = [take() for _ in range(1 if 1 not in parts else 2)]
    if 0 in parts:
        wq, wm, qkv, att = (take() for _ in range(4))
    if 1 in parts:
        we, ws, mid = (take() for _ in range(3))
    sems = take()

    def copy(src, dst, k):
        pltpu.make_async_copy(src, dst, sems.at[k]).start()

    def at(ref, start, rows):
        return ref.at[pl.ds(pl.multiple_of(start, 16), rows), :]

    half_e, halves = ne // 2, ns // 2
    for stage in range(2):
        if stage not in parts:
            continue
        for ref, (stages, pieces) in zip(buffers, sources):
            if stages != stage:
                continue
            if pieces is None:
                continue
            for row, r, dy, core, half in pieces:
                shard = owners[(r * 2 + dy) * 2 + core]
                if stage == 0:
                    copy(ref.at[pl.ds(row, nq), :], at(wq, shard * nq, nq), 0)
                    copy(ref.at[pl.ds(row + nq, nm), :], at(wm, shard * nm, nm), 1)
                else:
                    side = owners[owners.shape[0] - 1]
                    side = {0: side, 1: 1 - side, "lo": 0, "hi": 1}[half]
                    copy(
                        ref.at[pl.ds(row, half_e), :], at(we, shard * ne + side * half_e, half_e), 2
                    )
                    for k in range(halves):
                        copy(
                            ref.at[pl.ds(row + half_e + k * nm, nm), :],
                            at(ws, (side * halves + k) * width + shard * nm, nm),
                            3,
                        )
    whole = [pieces for _, pieces in sources]
    if all(p is None for p in whole):
        targets = ([wq, wm] if 0 in parts else []) + ([we, ws] if 1 in parts else [])
        first = 0 if 0 in parts else 2
        for k, (ref, dst) in enumerate(zip(buffers, targets)):
            copy(ref, dst, first + k)

    def waiter(ref, k):
        return lambda: pltpu.make_async_copy(ref, ref, sems.at[k]).wait()

    ready = {}
    if 0 in parts:
        ready[0], ready[1] = waiter(wq, 0), waiter(wm, 1)
    if 1 in parts:
        ready[2], ready[3] = waiter(we, 2), waiter(ws, 3)
    if 0 in parts:
        hidden = attention_part(
            state, patch, place, terms, wq, wm, qkv, att, ready, heads, samples
        )
    else:
        hidden = before[...]
    if 1 not in parts:
        results[0][...] = hidden
        return
    drift = feed_part(hidden, state, terms, out_weight, scalars, we, ws, mid, ready, samples)
    results[0][...] = drift
    results[1][...] = drift.astype(BF16)


def run_network(parts, fixed, before, buffers, sizes, heads, samples):
    width, tokens = fixed[4].shape
    patch = fixed[2].shape[0]
    nq, nm, ne, ns, _ = sizes
    ff = ns * width
    smem = pl.BlockSpec(memory_space=pltpu.SMEM)
    vmem = pl.BlockSpec(memory_space=pltpu.VMEM)
    anywhere = pl.BlockSpec(memory_space=pl.ANY)
    scratch = []
    if 0 in parts:
        scratch += [
            pltpu.VMEM((3 * width, width), BF16),
            pltpu.VMEM((width, width), BF16),
            pltpu.VMEM((3 * width, tokens), BF16),
            pltpu.VMEM((width, tokens), BF16),
        ]
    if 1 in parts:
        scratch += [
            pltpu.VMEM((ff, width), BF16),
            pltpu.VMEM((ff, width), BF16),
            pltpu.VMEM((ff, tokens), BF16),
        ]
    scratch.append(pltpu.SemaphoreType.DMA((4,)))
    if 1 in parts:
        out_shape = [
            jax.ShapeDtypeStruct((patch, tokens), F32),
            jax.ShapeDtypeStruct((patch, tokens), BF16),
        ]
    else:
        out_shape = [jax.ShapeDtypeStruct((width, tokens), F32)]
    rows = (4 * width if 0 in parts else 0) + (2 * ff if 1 in parts else 0)
    extra = [] if before is None else [before]
    return pl.pallas_call(
        functools.partial(
            network_kernel, parts, [(s, p) for s, _, p in buffers], sizes, heads, samples
        ),
        out_shape=out_shape,
        in_specs=[smem, smem] + [vmem] * (len(fixed) - 2 + len(extra)) + [anywhere] * len(buffers),
        out_specs=[vmem] * len(out_shape),
        scratch_shapes=scratch,
        compiler_params=pltpu.CompilerParams(vmem_limit_bytes=40 * 1024 * 1024),
        cost_estimate=pl.CostEstimate(
            flops=2 * rows * width * tokens, bytes_accessed=2 * rows * width, transcendentals=0
        ),
    )(*fixed, *extra, *[b for _, b, _ in buffers])


def earlier_sum(value, narrow, count):
    position = lax.axis_index("tm")
    total = value
    before = jnp.zeros_like(value)
    distance = 1
    while distance < count:
        pairs = [(i, i ^ distance) for i in range(count)]
        other = lax.ppermute(narrow, "tm", pairs).astype(value.dtype)
        before = jnp.where((position & distance) != 0, before + other, before)
        total = total + other
        narrow = total.astype(BF16)
        distance *= 2
    return before


def body(
    noise,
    labels,
    timesteps,
    window_start,
    time_weight_in,
    time_weight_out,
    class_table,
    patch_weight,
    query_key_value,
    mix_weight,
    expand_weight,
    shrink_weight,
    block_modulation,
    final_modulation,
    output_weight,
):
    groups, count = lax.axis_size("group"), lax.axis_size("tm")
    samples, latent = noise.shape
    patch, width = patch_weight.shape
    each = latent // patch
    tokens = samples * each
    position = lax.axis_index("tm")

    nq, nm, ne = query_key_value.shape[2], mix_weight.shape[2], expand_weight.shape[2]
    ns = shrink_weight.shape[1] // width
    sizes = (nq, nm, ne, ns, width)
    q_rows, m_rows, e_rows = query_key_value[0].T, mix_weight[0].T, expand_weight[0].T
    s_rows = shrink_weight[0].reshape(ns, width, nm).transpose(0, 2, 1)
    short = (
        groups == 2
        and count == 16
        and ns % 2 == 0
        and all(v % 16 == 0 for v in (nq, nm, ne // 2))
    )
    if short:
        half_e, half_s = ne // 2, ns // 2
        first = jnp.concatenate([q_rows, m_rows], axis=0)
        second = jnp.stack(
            [
                jnp.concatenate(
                    [e_rows[k * half_e : (k + 1) * half_e]]
                    + [s_rows[k * half_s + j] for j in range(half_s)],
                    axis=0,
                )
                for k in range(2)
            ]
        )
        first_out, second_out = spread_weights(first, second, groups, count)
        owners = jnp.concatenate(
            [piece_owners(count), lax.axis_index("group").astype(jnp.int32)[None]]
        )
        first_buffers = [(0, data, pieces) for data, pieces in first_out]
        second_buffers = [(1, data, pieces) for data, pieces in second_out]
    else:
        whole = lambda rows, axis: lax.all_gather(rows, "tm", axis=axis, tiled=True)
        owners = jnp.zeros((1,), jnp.int32)
        first_buffers = [(0, whole(q_rows, 0), None), (0, whole(m_rows, 0), None)]
        second_buffers = [
            (1, whole(e_rows, 0), None),
            (1, whole(s_rows, 1).reshape(ns * width, width), None),
        ]

    steps = jnp.arange(count, dtype=jnp.int32)
    current, scale_state, scale_noise = plan_terms(timesteps, window_start, steps, TRAIN_T)
    scalars = jnp.stack([scale_state[position], scale_noise[position]])
    condition = conditioning(current, labels, time_weight_in, time_weight_out, class_table)
    rows = condition.reshape(count * samples, width)
    block_part = jnp.dot(rows, block_modulation[0], preferred_element_type=F32).astype(BF16)
    final_part = jnp.dot(rows, final_modulation, preferred_element_type=F32).astype(BF16)
    nb = block_part.shape[1]
    both = jnp.concatenate([block_part, final_part], axis=1).reshape(count, samples, -1)
    both = lax.all_to_all(both, "tm", split_axis=0, concat_axis=0, tiled=True)
    unfold = lambda t: t.transpose(1, 0, 2).reshape(samples, -1)
    terms = jnp.concatenate([unfold(both[:, :, :nb]), unfold(both[:, :, nb:])], axis=1)
    terms = jnp.pad(terms, ((0, -samples % 16), (0, 0)))

    start = noise.reshape(samples, each, patch).transpose(2, 0, 1).reshape(patch, tokens)
    place = jnp.tile(position_columns(each, width), (1, samples))
    patch_rows, out_rows = patch_weight.T, output_weight.T

    states = start
    for sweep in range(ITERS):
        fixed = (owners, scalars, states, patch_rows, place, terms, out_rows)
        if sweep == 0:
            (hidden,) = run_network((0,), fixed, None, first_buffers, sizes, HEADS, samples)
            drift, narrow = run_network(
                (1,), fixed, hidden, second_buffers, sizes, HEADS, samples
            )
        else:
            drift, narrow = run_network(
                (0, 1), fixed, None, first_buffers + second_buffers, sizes, HEADS, samples
            )
        before = earlier_sum(drift, narrow, count)
        running = before + drift
        states = start + before
    result = (start + running).reshape(patch, samples, each).transpose(1, 2, 0)
    return result.reshape(1, samples, latent)


def solution(mesh):
    return jax.shard_map(
        body,
        mesh=mesh,
        in_specs=(
            P("group", None),
            P("group"),
            P(),
            P(),
            P(),
            P(),
            P(),
            P(),
            P(None, None, "tm"),
            P(None, None, "tm"),
            P(None, None, "tm"),
            P(None, None, "tm"),
            P(None, None, "tm"),
            P(None, "tm"),
            P(),
        ),
        out_specs=P("tm", "group", None),
        check_vma=False,
    )
```

time: 297 us -> 204 us (0.69)
  waiting for transfers between devices: 119 us -> 46.2 us
  blocking collectives: 63 us -> 0 us
  Pallas kernels: 0 us -> 45.3 us
  matrix products: 46.3 us -> 4.58 us
  starting transfers between devices: 9.61 us -> 43 us
  local copies, waits for them, and re-layouts: 31.9 us -> 47.5 us
  between operations: 17.4 us -> 6.56 us
    all_gather x4 -> x0, waiting for transfers between devices: 110 us -> none  [the longest x1 51.8 us: body(): lax.all_gather(expand_weight, 'tm', axis=2, tiled=True)]
    all_gather x3 -> x0, blocking collectives: 63 us -> none  [the longest x2 39.5 us: carried_in(): everything = lax.all_gather(x.astype(jnp.bfloat16), axis)]
    ppermute x0 -> x33, waiting for transfers between devices: none -> 46.2 us  [the longest x25 26.6 us: _send(): value = lax.ppermute(value, ('group', 'tm'), pairs)]
    pallas_call x0 -> x3, Pallas kernels: none -> 45.3 us  [run_network(): pl.pallas_call(functools.partial(network_kernel, parts, [(s, p) for s, _,...]
    dot_general x21 -> x4, matrix products: 46.3 us -> 4.58 us  [the longest x1 1.84 us: conditioning(): jnp.dot(time_hidden, time_weight_out, preferred_element_type=F32)]
    ppermute x0 -> x33, starting transfers between devices: none -> 38.8 us  [the longest x25 29.7 us: _send(): value = lax.ppermute(value, ('group', 'tm'), pairs)]
    unnamed x78 -> x87, local copies, waits for them, and re-layouts: 12.4 us -> 27 us
    slice x3 -> x2, local copies, waits for them, and re-layouts: 8.25 us -> 0.11 us  [the longest x2 8.18 us: network(): projected[:, :, 2]]
  transfers between devices with their start and end apart: 6 -> 34, of which waited for: 4 -> 17; matrix products, arithmetic and copies ran while one was open for 15% -> 21% of each run, Pallas kernels for 0% -> 5%
where the time goes in v1:
time: 204 us; the launch traced here: 202 us
  local copies, waits for them, and re-layouts  47.5 us (23%)
  waiting for transfers between devices  46.2 us (23%)
  Pallas kernels  45.3 us (22%)
  starting transfers between devices  43 us (21%)
  other arithmetic  9 us (4%)
  between operations  6.56 us (3%)
  matrix products  4.58 us (2%)
    pallas_call x3, Pallas kernels, run_network(): pl.pallas_call(functools.partial(network_kernel, parts, [(s, p) for s, _,...  45.3 us
    ppermute x25, starting transfers between devices, _send(): value = lax.ppermute(value, ('group', 'tm'), pairs)  29.7 us
    unnamed x87, local copies, waits for them, and re-layouts  27 us
    ppermute x25, waiting for transfers between devices, _send(): value = lax.ppermute(value, ('group', 'tm'), pairs)  26.6 us
    ppermute x8, waiting for transfers between devices, earlier_sum(): other = lax.ppermute(narrow, 'tm', pairs).astype(value.dtype)  19.5 us
    ppermute x8, starting transfers between devices, earlier_sum(): other = lax.ppermute(narrow, 'tm', pairs).astype(value.dtype)  9.05 us
    all_to_all x1, starting transfers between devices, body(): both = lax.all_to_all(both, 'tm', split_axis=0, concat_axis=0, tiled=True)  4.26 us
  transfers between devices with their start and end apart: 34, of which 17 were waited for; matrix products, arithmetic and copies ran while one was open for 21% of the time, Pallas kernels for 5%

profile of v1, /device:TPU:0, one launch (start us, length us, event | category | flops | bytes accessed | tf_op | source)
XLA Modules:
  0.0 202.2 jit_solution(15033130578636726864)
XLA Ops:
  1.9 3.0 %collective-permute-start.2 = (bf16[192,768]{1,0:T(8,128)(2,1)}, bf16[192,768]{1,0:T(8,128)(2,1)}, u32[]{:S(2)}, u32[]{:S(2)}) collective-permute-start(bf16[192,768]{1,0:T(8,128)(2,1)} %pad_maximum_fusion.3), channel_id=1, source_target_pairs={{0,2},{1,3},{2,0},{3,1},{4,6},{5,7},{6,4},{7,5},{8,10},{9,11},{10,... | collective-permute-start | bytes 884744 | tf_op jit(solution)/shard_map/ppermute | solution.py:87
  4.8 2.6 %collective-permute-start.1 = (bf16[192,768]{1,0:T(8,128)(2,1)}, bf16[192,768]{1,0:T(8,128)(2,1)}, u32[]{:S(2)}, u32[]{:S(2)}) collective-permute-start(bf16[192,768]{1,0:T(8,128)(2,1)} %pad_maximum_fusion.3), channel_id=1, source_target_pairs={{0,8},{1,9},{2,10},{3,11},{4,0},{5,1},{6,2},{7,3},{8,12},{9,13},{1... | collective-permute-start | bytes 884744 | tf_op jit(solution)/shard_map/ppermute | solution.py:87
  20.3 4.3 %all-to-all-start = ((bf16[16,4,384]{2,1,0:T(4,128)(2,1)}), bf16[16,4,384]{2,1,0:T(4,128)(2,1)}, u32[]{:S(2)}, u32[]{:S(2)}) async-start(bf16[16,4,384]{2,1,0:T(4,128)(2,1)} %reshape.122), calls=%async_computation | async-start | bytes 98304 | tf_op jit(solution)/shard_map/all_to_all | solution.py:457
  39.9 2.3 %copy.39.refs_4_ = f32[768,256]{1,0:T(8,128)} copy(f32[768,256]{0,1:T(8,128)} %bitcast.91) | data formatting | bytes 1572864 | tf_op jit(solution)/shard_map/tile | solution.py:463
  46.5 2.6 %collective-permute-start.7 = (bf16[192,768]{1,0:T(8,128)(2,1)}, bf16[192,768]{1,0:T(8,128)(2,1)S(1)}, u32[]{:S(2)}, u32[]{:S(2)}) collective-permute-start(bf16[192,768]{1,0:T(8,128)(2,1)} %collective-permute-done.1), channel_id=1, source_target_pairs={{0,8},{1,9},{2,10},{3,11},{4,0},{5,1},{6,2},{7,3},{8,12},{9,13},{1... | collective-permute-start | bytes 884744 | tf_op jit(solution)/shard_map/ppermute | solution.py:87
  57.3 2.8 %collective-permute-start.8 = (bf16[192,768]{1,0:T(8,128)(2,1)S(1)}, bf16[192,768]{1,0:T(8,128)(2,1)S(1)}, u32[]{:S(2)}, u32[]{:S(2)}) collective-permute-start(bf16[192,768]{1,0:T(8,128)(2,1)S(1)} %collective-permute-done.7), channel_id=1, source_target_pairs={{0,8},{1,9},{2,10},{3,11},{4,0},{5,1},{6,2},{7,3},{8,12},{9,13},{1... | collective-permute-start | bytes 884744 | tf_op jit(solution)/shard_map/ppermute | solution.py:87
  60.1 3.0 %collective-permute-done.14 = bf16[192,768]{1,0:T(8,128)(2,1)S(1)} collective-permute-done((bf16[192,768]{1,0:T(8,128)(2,1)}, bf16[192,768]{1,0:T(8,128)(2,1)S(1)}, u32[]{:S(2)}, u32[]{:S(2)}) %collective-permute-start.14) | collective-permute-done | bytes 294944 | tf_op jit(solution)/shard_map/ppermute | solution.py:87
  67.6 2.3 %collective-permute-done.10 = bf16[384,768]{1,0:T(8,128)(2,1)S(1)} collective-permute-done((bf16[384,768]{1,0:T(8,128)(2,1)S(1)}, bf16[384,768]{1,0:T(8,128)(2,1)S(1)}, u32[]{:S(2)}, u32[]{:S(2)}) %collective-permute-start.10) | collective-permute-done | bytes 589856 | tf_op jit(solution)/shard_map/ppermute | solution.py:87
  74.0 5.3 %collective-permute-done.11 = bf16[192,768]{1,0:T(8,128)(2,1)S(1)} collective-permute-done((bf16[192,768]{1,0:T(8,128)(2,1)S(1)}, bf16[192,768]{1,0:T(8,128)(2,1)S(1)}, u32[]{:S(2)}, u32[]{:S(2)}) %collective-permute-start.11) | collective-permute-done | bytes 294944 | tf_op jit(solution)/shard_map/ppermute | solution.py:87
  79.3 2.0 %collective-permute-start.12 = (bf16[192,768]{1,0:T(8,128)(2,1)S(1)}, bf16[192,768]{1,0:T(8,128)(2,1)S(1)}, u32[]{:S(2)}, u32[]{:S(2)}) collective-permute-start(bf16[192,768]{1,0:T(8,128)(2,1)S(1)} %collective-permute-done.8), channel_id=1, source_target_pairs={{0,2},{1,3},{2,0},{3,1},{4,6},{5,7},{6,4},{7,5},{8,10},{9,11},{10,... | collective-permute-start | bytes 884744 | tf_op jit(solution)/shard_map/ppermute | solution.py:87
  82.1 3.5 %collective-permute-done.19 = bf16[192,768]{1,0:T(8,128)(2,1)S(1)} collective-permute-done((bf16[192,768]{1,0:T(8,128)(2,1)S(1)}, bf16[192,768]{1,0:T(8,128)(2,1)S(1)}, u32[]{:S(2)}, u32[]{:S(2)}) %collective-permute-start.19) | collective-permute-done | bytes 294944 | tf_op jit(solution)/shard_map/ppermute | solution.py:87
  85.7 2.0 collective-permute-start.20
  95.8 2.2 %collective-permute-done.20 = bf16[384,768]{1,0:T(8,128)(2,1)S(1)} collective-permute-done((bf16[384,768]{1,0:T(8,128)(2,1)S(1)}, bf16[384,768]{1,0:T(8,128)(2,1)S(1)}, u32[]{:S(2)}, u32[]{:S(2)}) %collective-permute-start.20) | collective-permute-done | bytes 589856 | tf_op jit(solution)/shard_map/ppermute | solution.py:87
  99.3 2.0 collective-permute-done.22
  105.6 5.7 %collective-permute-done.23 = bf16[192,768]{1,0:T(8,128)(2,1)} collective-permute-done((bf16[192,768]{1,0:T(8,128)(2,1)}, bf16[192,768]{1,0:T(8,128)(2,1)}, u32[]{:S(2)}, u32[]{:S(2)}) %collective-permute-start.23) | collective-permute-done | bytes 294944 | tf_op jit(solution)/shard_map/ppermute | solution.py:87
  115.6 10.4 %shard_map.190.refs_7_ = f32[768,256]{1,0:T(8,128)S(1)} custom-call(s32[17]{0:T(128)S(1)} %concatenate.59.refs_0_, f32[2]{0:T(128)S(1)} %pad_maximum_fusion.6.refs_1_, f32[64,256]{1,0:T(8,128)S(1)} %copy-done.21, bf16[768,64]{1,0:T(8,128)(2,1)S(1)} %bitcast.83, f32[768,256]{1,0:T(8,128)S(1)} %copy-done.1, bf16[16,6144]{1,0:T(8,128)(2,1)S(1)} %fusion.3.refs_5_, ...), custom_call_target="tpu_custom_call" | custom-call | flops 1207959552 | bytes 4718592 | tf_op jit(solution)/shard_map/pallas_call | solution.py:355
  126.1 13.0 %shard_map.191 = (f32[64,256]{1,0:T(8,128)S(1)}, bf16[64,256]{1,0:T(8,128)(2,1)S(1)}) custom-call(s32[17]{0:T(128)S(1)} %concatenate.59.refs_0_, f32[2]{0:T(128)S(1)} %pad_maximum_fusion.6.refs_1_, f32[64,256]{1,0:T(8,128)S(1)} %copy-done.21, bf16[768,64]{1,0:T(8,128)(2,1)S(1)} %bitcast.84, f32[768,256]{1,0:T(8,128)S(1)} %copy-done.1, ...), custom_call_target="tpu_custom_call" | custom-call | flops 2415919104 | bytes 9437184 | tf_op jit(solution)/shard_map/pallas_call | solution.py:355
  142.1 2.4 %collective-permute-done.26 = bf16[64,256]{1,0:T(8,128)(2,1)S(1)} collective-permute-done((bf16[64,256]{1,0:T(8,128)(2,1)S(1)}, bf16[64,256]{1,0:T(8,128)(2,1)S(1)}, u32[]{:S(2)}, u32[]{:S(2)}) %collective-permute-start.26) | collective-permute-done | bytes 32800 | tf_op jit(solution)/shard_map/ppermute | solution.py:377
  145.4 3.1 %collective-permute-done.27 = bf16[64,256]{1,0:T(8,128)(2,1)S(1)} collective-permute-done((bf16[64,256]{1,0:T(8,128)(2,1)S(1)}, bf16[64,256]{1,0:T(8,128)(2,1)S(1)}, u32[]{:S(2)}, u32[]{:S(2)}) %collective-permute-start.27) | collective-permute-done | bytes 32800 | tf_op jit(solution)/shard_map/ppermute | solution.py:377
  150.9 3.4 %collective-permute-done.28 = bf16[64,256]{1,0:T(8,128)(2,1)} collective-permute-done((bf16[64,256]{1,0:T(8,128)(2,1)}, bf16[64,256]{1,0:T(8,128)(2,1)}, u32[]{:S(2)}, u32[]{:S(2)}) %collective-permute-start.28) | collective-permute-done | bytes 32800 | tf_op jit(solution)/shard_map/ppermute | solution.py:377
  165.1 21.9 %shard_map.192 = (f32[64,256]{1,0:T(8,128)S(1)}, bf16[64,256]{1,0:T(8,128)(2,1)S(1)}) custom-call(s32[17]{0:T(128)S(1)} %concatenate.59.refs_0_, f32[2]{0:T(128)S(1)} %pad_maximum_fusion.6.refs_1_, f32[64,256]{1,0:T(8,128)S(1)} %fusion.7.refs_2_, bf16[768,64]{1,0:T(8,128)(2,1)S(1)} %bitcast.85, f32[768,256]{1,0:T(8,128)S(1)} %copy-done.2, ...), custom_call_target="tpu_custom_call" | custom-call | flops 3623878656 | bytes 14155776 | tf_op jit(solution)/shard_map/pallas_call | solution.py:355
  189.9 2.4 %collective-permute-done.30 = bf16[64,256]{1,0:T(8,128)(2,1)S(1)} collective-permute-done((bf16[64,256]{1,0:T(8,128)(2,1)S(1)}, bf16[64,256]{1,0:T(8,128)(2,1)S(1)}, u32[]{:S(2)}, u32[]{:S(2)}) %collective-permute-start.30) | collective-permute-done | bytes 32800 | tf_op jit(solution)/shard_map/ppermute | solution.py:377
  193.3 3.0 %collective-permute-done.31 = bf16[64,256]{1,0:T(8,128)(2,1)S(1)} collective-permute-done((bf16[64,256]{1,0:T(8,128)(2,1)S(1)}, bf16[64,256]{1,0:T(8,128)(2,1)S(1)}, u32[]{:S(2)}, u32[]{:S(2)}) %collective-permute-start.31) | collective-permute-done | bytes 32800 | tf_op jit(solution)/shard_map/ppermute | solution.py:377
  198.1 3.1 %collective-permute-done.32 = bf16[64,256]{1,0:T(8,128)(2,1)S(1)} collective-permute-done((bf16[64,256]{1,0:T(8,128)(2,1)S(1)}, bf16[64,256]{1,0:T(8,128)(2,1)S(1)}, u32[]{:S(2)}, u32[]{:S(2)}) %collective-permute-start.32) | collective-permute-done | bytes 32800 | tf_op jit(solution)/shard_map/ppermute | solution.py:377
  (214 shorter events, 87.3 us)
Async XLA Ops:
  1.9 51.9 %collective-permute-start.2 = (bf16[192,768]{1,0:T(8,128)(2,1)}, bf16[192,768]{1,0:T(8,128)(2,1)}, u32[]{:S(2)}, u32[]{:S(2)}) collective-permute-start(bf16[192,768]{1,0:T(8,128)(2,1)} %pad_maximum_fusion.3), channel_id=1, source_target_pairs={{0,2},{1,3},{2,0},{3,1},{4,6},{5,7},{6,4},{7,5},{8,10},{9,11},{10,... | collective-permute-start | bytes 884744 | tf_op jit(solution)/shard_map/ppermute | solution.py:87
  4.8 41.7 %collective-permute-start.1 = (bf16[192,768]{1,0:T(8,128)(2,1)}, bf16[192,768]{1,0:T(8,128)(2,1)}, u32[]{:S(2)}, u32[]{:S(2)}) collective-permute-start(bf16[192,768]{1,0:T(8,128)(2,1)} %pad_maximum_fusion.3), channel_id=1, source_target_pairs={{0,8},{1,9},{2,10},{3,11},{4,0},{5,1},{6,2},{7,3},{8,12},{9,13},{1... | collective-permute-start | bytes 884744 | tf_op jit(solution)/shard_map/ppermute | solution.py:87
  10.5 38.7 %collective-permute-start.9 = (bf16[192,768]{1,0:T(8,128)(2,1)}, bf16[192,768]{1,0:T(8,128)(2,1)}, u32[]{:S(2)}, u32[]{:S(2)}) collective-permute-start(bf16[192,768]{1,0:T(8,128)(2,1)} %maximum_select_fusion), channel_id=1, source_target_pairs={{0,2},{1,3},{2,0},{3,1},{4,6},{5,7},{6,4},{7,5},{8,10},{9,11},{10,... | collective-permute-start | bytes 884744 | tf_op jit(solution)/shard_map/ppermute | solution.py:87
  11.0 38.2 %collective-permute-start.3 = (bf16[192,768]{1,0:T(8,128)(2,1)}, bf16[192,768]{1,0:T(8,128)(2,1)}, u32[]{:S(2)}, u32[]{:S(2)}) collective-permute-start(bf16[192,768]{1,0:T(8,128)(2,1)} %maximum_select_fusion), channel_id=1, source_target_pairs={{0,8},{1,9},{2,10},{3,11},{4,0},{5,1},{6,2},{7,3},{8,12},{9,13},{1... | collective-permute-start | bytes 884744 | tf_op jit(solution)/shard_map/ppermute | solution.py:87
  20.3 23.2 %all-to-all-start = ((bf16[16,4,384]{2,1,0:T(4,128)(2,1)}), bf16[16,4,384]{2,1,0:T(4,128)(2,1)}, u32[]{:S(2)}, u32[]{:S(2)}) async-start(bf16[16,4,384]{2,1,0:T(4,128)(2,1)} %reshape.122), calls=%async_computation | async-start | bytes 98304 | tf_op jit(solution)/shard_map/all_to_all | solution.py:457
  24.7 27.4 %collective-permute-start = (bf16[576,768]{1,0:T(8,128)(2,1)S(1)}, bf16[576,768]{1,0:T(8,128)(2,1)S(1)}, u32[]{:S(2)}, u32[]{:S(2)}) collective-permute-start(bf16[576,768]{1,0:T(8,128)(2,1)S(1)} %constant_dynamic-update-slice_fusion.refs_7_.refs_8_.refs_13_), channel_id=1, source_target_pairs={{0,1},{1,0},{2,3},{3,2},{4,5},{5,4},{6,7},{7,6},{8,9},{9,8},{10,11... | collective-permute-start | bytes 2654216 | tf_op jit(solution)/shard_map/ppermute | solution.py:87
  46.5 10.8 %collective-permute-start.7 = (bf16[192,768]{1,0:T(8,128)(2,1)}, bf16[192,768]{1,0:T(8,128)(2,1)S(1)}, u32[]{:S(2)}, u32[]{:S(2)}) collective-permute-start(bf16[192,768]{1,0:T(8,128)(2,1)} %collective-permute-done.1), channel_id=1, source_target_pairs={{0,8},{1,9},{2,10},{3,11},{4,0},{5,1},{6,2},{7,3},{8,12},{9,13},{1... | collective-permute-start | bytes 884744 | tf_op jit(solution)/shard_map/ppermute | solution.py:87
  49.1 15.6 %collective-permute-start.4 = (bf16[192,768]{1,0:T(8,128)(2,1)}, bf16[192,768]{1,0:T(8,128)(2,1)S(1)}, u32[]{:S(2)}, u32[]{:S(2)}) collective-permute-start(bf16[192,768]{1,0:T(8,128)(2,1)} %collective-permute-done.1), channel_id=1, source_target_pairs={{0,2},{1,3},{2,0},{3,1},{4,6},{5,7},{6,4},{7,5},{8,10},{9,11},{10,... | collective-permute-start | bytes 884744 | tf_op jit(solution)/shard_map/ppermute | solution.py:87
  50.6 12.5 %collective-permute-start.14 = (bf16[192,768]{1,0:T(8,128)(2,1)}, bf16[192,768]{1,0:T(8,128)(2,1)S(1)}, u32[]{:S(2)}, u32[]{:S(2)}) collective-permute-start(bf16[192,768]{1,0:T(8,128)(2,1)} %collective-permute-done.3), channel_id=1, source_target_pairs={{0,8},{1,9},{2,10},{3,11},{4,0},{5,1},{6,2},{7,3},{8,12},{9,13},{1... | collective-permute-start | bytes 884744 | tf_op jit(solution)/shard_map/ppermute | solution.py:87
  52.1 12.5 %collective-permute-start.5 = (bf16[192,768]{1,0:T(8,128)(2,1)}, bf16[192,768]{1,0:T(8,128)(2,1)S(1)}, u32[]{:S(2)}, u32[]{:S(2)}) collective-permute-start(bf16[192,768]{1,0:T(8,128)(2,1)} %collective-permute-done.3), channel_id=1, source_target_pairs={{0,2},{1,3},{2,0},{3,1},{4,6},{5,7},{6,4},{7,5},{8,10},{9,11},{10,... | collective-permute-start | bytes 884744 | tf_op jit(solution)/shard_map/ppermute | solution.py:87
  53.8 16.2 %collective-permute-start.10 = (bf16[384,768]{1,0:T(8,128)(2,1)S(1)}, bf16[384,768]{1,0:T(8,128)(2,1)S(1)}, u32[]{:S(2)}, u32[]{:S(2)}) collective-permute-start(bf16[384,768]{1,0:T(8,128)(2,1)S(1)} %pad_maximum_fusion), channel_id=1, source_target_pairs={{0,16},{1,17},{2,18},{3,19},{4,20},{5,21},{6,22},{7,23},{8,24},{9,... | collective-permute-start | bytes 1769480 | tf_op jit(solution)/shard_map/ppermute | solution.py:87
  57.3 15.3 %collective-permute-start.8 = (bf16[192,768]{1,0:T(8,128)(2,1)S(1)}, bf16[192,768]{1,0:T(8,128)(2,1)S(1)}, u32[]{:S(2)}, u32[]{:S(2)}) collective-permute-start(bf16[192,768]{1,0:T(8,128)(2,1)S(1)} %collective-permute-done.7), channel_id=1, source_target_pairs={{0,8},{1,9},{2,10},{3,11},{4,0},{5,1},{6,2},{7,3},{8,12},{9,13},{1... | collective-permute-start | bytes 884744 | tf_op jit(solution)/shard_map/ppermute | solution.py:87
  64.7 16.6 %collective-permute-start.15 = (bf16[384,768]{1,0:T(8,128)(2,1)S(1)}, bf16[384,768]{1,0:T(8,128)(2,1)S(1)}, u32[]{:S(2)}, u32[]{:S(2)}) collective-permute-start(bf16[384,768]{1,0:T(8,128)(2,1)S(1)} %pad_maximum_fusion.1), channel_id=1, source_target_pairs={{0,16},{1,17},{2,18},{3,19},{4,20},{5,21},{6,22},{7,23},{8,24},{9,... | collective-permute-start | bytes 1769480 | tf_op jit(solution)/shard_map/ppermute | solution.py:87
  66.3 23.9 %collective-permute-start.6 = (bf16[576,768]{1,0:T(8,128)(2,1)S(1)}, bf16[576,768]{1,0:T(8,128)(2,1)S(1)}, u32[]{:S(2)}, u32[]{:S(2)}) collective-permute-start(bf16[576,768]{1,0:T(8,128)(2,1)S(1)} %constant_dynamic-update-slice_fusion.8.refs_9_), channel_id=1, source_target_pairs={{0,1},{1,0},{2,3},{3,2},{4,5},{5,4},{6,7},{7,6},{8,9},{9,8},{10,11... | collective-permute-start | bytes 2654216 | tf_op jit(solution)/shard_map/ppermute | solution.py:87
  72.4 9.7 %collective-permute-start.18 = (bf16[192,768]{1,0:T(8,128)(2,1)S(1)}, bf16[192,768]{1,0:T(8,128)(2,1)S(1)}, u32[]{:S(2)}, u32[]{:S(2)}) collective-permute-start(bf16[192,768]{1,0:T(8,128)(2,1)S(1)} %collective-permute-done.14), channel_id=1, source_target_pairs={{0,8},{1,9},{2,10},{3,11},{4,0},{5,1},{6,2},{7,3},{8,12},{9,13},{1... | collective-permute-start | bytes 884744 | tf_op jit(solution)/shard_map/ppermute | solution.py:87
  72.6 13.0 %collective-permute-start.19 = (bf16[192,768]{1,0:T(8,128)(2,1)S(1)}, bf16[192,768]{1,0:T(8,128)(2,1)S(1)}, u32[]{:S(2)}, u32[]{:S(2)}) collective-permute-start(bf16[192,768]{1,0:T(8,128)(2,1)S(1)} %collective-permute-done.14), channel_id=1, source_target_pairs={{0,2},{1,3},{2,0},{3,1},{4,6},{5,7},{6,4},{7,5},{8,10},{9,11},{10,... | collective-permute-start | bytes 884744 | tf_op jit(solution)/shard_map/ppermute | solution.py:87
  79.3 10.2 %collective-permute-start.12 = (bf16[192,768]{1,0:T(8,128)(2,1)S(1)}, bf16[192,768]{1,0:T(8,128)(2,1)S(1)}, u32[]{:S(2)}, u32[]{:S(2)}) collective-permute-start(bf16[192,768]{1,0:T(8,128)(2,1)S(1)} %collective-permute-done.8), channel_id=1, source_target_pairs={{0,2},{1,3},{2,0},{3,1},{4,6},{5,7},{6,4},{7,5},{8,10},{9,11},{10,... | collective-permute-start | bytes 884744 | tf_op jit(solution)/shard_map/ppermute | solution.py:87
  81.3 20.0 %collective-permute-start.16 = (bf16[768,768]{1,0:T(8,128)(2,1)S(1)}, bf16[768,768]{1,0:T(8,128)(2,1)S(1)}, u32[]{:S(2)}, u32[]{:S(2)}) collective-permute-start(bf16[768,768]{1,0:T(8,128)(2,1)S(1)} %constant_dynamic-update-slice_fusion.15.refs_10_.refs_15_), channel_id=1, source_target_pairs={{0,1},{1,0},{2,3},{3,2},{4,5},{5,4},{6,7},{7,6},{8,9},{9,8},{10,11... | collective-permute-start | bytes 3538952 | tf_op jit(solution)/shard_map/ppermute | solution.py:87
  85.7 12.3 %collective-permute-start.20 = (bf16[384,768]{1,0:T(8,128)(2,1)S(1)}, bf16[384,768]{1,0:T(8,128)(2,1)S(1)}, u32[]{:S(2)}, u32[]{:S(2)}) collective-permute-start(bf16[384,768]{1,0:T(8,128)(2,1)S(1)} %pad_maximum_fusion.2), channel_id=1, source_target_pairs={{0,16},{1,17},{2,18},{3,19},{4,20},{5,21},{6,22},{7,23},{8,24},{9,... | collective-permute-start | bytes 1769480 | tf_op jit(solution)/shard_map/ppermute | solution.py:87
  90.2 22.0 %collective-permute-start.13 = (bf16[768,768]{1,0:T(8,128)(2,1)}, bf16[768,768]{1,0:T(8,128)(2,1)}, u32[]{:S(2)}, u32[]{:S(2)}) collective-permute-start(bf16[768,768]{1,0:T(8,128)(2,1)} %constant_dynamic-update-slice_fusion.11.refs_11_), channel_id=1, source_target_pairs={{0,1},{1,0},{2,3},{3,2},{4,5},{5,4},{6,7},{7,6},{8,9},{9,8},{10,11... | collective-permute-start | bytes 3538952 | tf_op jit(solution)/shard_map/ppermute | solution.py:87
  91.8 9.5 %collective-permute-start.22 = (bf16[192,768]{1,0:T(8,128)(2,1)S(1)}, bf16[192,768]{1,0:T(8,128)(2,1)}, u32[]{:S(2)}, u32[]{:S(2)}) collective-permute-start(bf16[192,768]{1,0:T(8,128)(2,1)S(1)} %collective-permute-done.18), channel_id=1, source_target_pairs={{0,2},{1,3},{2,0},{3,1},{4,6},{5,7},{6,4},{7,5},{8,10},{9,11},{10,... | collective-permute-start | bytes 884744 | tf_op jit(solution)/shard_map/ppermute | solution.py:87
  98.8 27.2 %collective-permute-start.21 = (bf16[768,768]{1,0:T(8,128)(2,1)}, bf16[768,768]{1,0:T(8,128)(2,1)}, u32[]{:S(2)}, u32[]{:S(2)}) collective-permute-start(bf16[768,768]{1,0:T(8,128)(2,1)} %constant_dynamic-update-slice_fusion.21.refs_14_.refs_19_), channel_id=1, source_target_pairs={{0,1},{1,0},{2,3},{3,2},{4,5},{5,4},{6,7},{7,6},{8,9},{9,8},{10,11... | collective-permute-start | bytes 3538952 | tf_op jit(solution)/shard_map/ppermute | solution.py:87
  98.8 27.2 %collective-permute-start.17 = (bf16[768,768]{1,0:T(8,128)(2,1)}, bf16[768,768]{1,0:T(8,128)(2,1)}, u32[]{:S(2)}, u32[]{:S(2)}) collective-permute-start(bf16[768,768]{1,0:T(8,128)(2,1)} %constant_dynamic-update-slice_fusion.18.refs_12_.refs_17_), channel_id=1, source_target_pairs={{0,1},{1,0},{2,3},{3,2},{4,5},{5,4},{6,7},{7,6},{8,9},{9,8},{10,11... | collective-permute-start | bytes 3538952 | tf_op jit(solution)/shard_map/ppermute | solution.py:87
  112.3 13.8 %collective-permute-start.24 = (bf16[384,768]{1,0:T(8,128)(2,1)S(1)}, bf16[384,768]{1,0:T(8,128)(2,1)S(1)}, u32[]{:S(2)}, u32[]{:S(2)}) collective-permute-start(bf16[384,768]{1,0:T(8,128)(2,1)S(1)} %constant_dynamic-update-slice_fusion.24.refs_16_.refs_21_), channel_id=1, source_target_pairs={{0,1},{1,0},{2,3},{3,2},{4,5},{5,4},{6,7},{7,6},{8,9},{9,8},{10,11... | collective-permute-start | bytes 1769480 | tf_op jit(solution)/shard_map/ppermute | solution.py:87
  (44 other events, 280.6 us)

commit v2 on v0

v2 whole, which is shorter than its diff:
```python
import functools
import math

import jax
import jax.numpy as jnp
import numpy as np
from jax import lax
from jax.experimental import pallas as pl
from jax.experimental.pallas import tpu as pltpu
from jax.sharding import PartitionSpec as P

HEADS = 12
ITERS = 2
TRAIN_T = 1000
WINDOW = 5
CORE_COUNTS = False
PAD = 8
VMEM_LIMIT = 53 * 1024 * 1024
BF16 = jnp.bfloat16
F32 = jnp.float32


def noise_levels(train_steps):
    levels = np.arange(train_steps, dtype=np.float32)
    betas = np.float32(0.0001) + np.float32(0.02 - 0.0001) * levels / np.float32(train_steps - 1)
    return np.cumprod((np.float32(1.0) - betas).astype(np.float64)).astype(np.float32)


def position_columns(count, width, samples):
    side = math.isqrt(count)
    quarter = width // 4
    omega = 1.0 / 10000.0 ** (np.arange(quarter, dtype=np.float64) / quarter)
    index = np.arange(count)
    first = omega[:, None] * (index // side)[None, :]
    second = omega[:, None] * (index % side)[None, :]
    table = np.concatenate([np.sin(first), np.cos(first), np.sin(second), np.cos(second)], axis=0)
    return np.tile(table, (1, samples)).astype(np.float32)


def conditioning_kernel(
    steps, samples, times, window, levels, w_in, w_out, classes, blocks, finals, part, scales
):
    half = w_in.shape[0] // 2
    row = lax.broadcasted_iota(jnp.int32, (steps, half), 0)
    lane = lax.broadcasted_iota(jnp.int32, (steps, half), 1).astype(F32)
    place = lax.broadcasted_iota(jnp.int32, (steps, scales.shape[1]), 0)
    current = jnp.zeros((steps, half), F32)
    now = jnp.ones(place.shape, F32)
    then = jnp.ones(place.shape, F32)
    for j in range(steps):
        here, after = times[window[0] + j], times[window[0] + j + 1]
        current = jnp.where(row == j, here.astype(F32), current)
        now = jnp.where(place == j, levels[here], now)
        then = jnp.where(place == j, levels[after], then)
    scale = jnp.sqrt(then / now)
    scales[0:steps, :] = scale
    scales[steps : 2 * steps, :] = jnp.sqrt(1.0 - then) - scale * jnp.sqrt(1.0 - now)
    angles = current * jnp.exp(-math.log(10000.0) * lane / half)
    features = jnp.concatenate([jnp.cos(angles), jnp.sin(angles)], axis=1).astype(BF16)
    hidden = jax.nn.silu(jnp.dot(features, w_in[...], preferred_element_type=F32)).astype(BF16)
    embed = jnp.dot(hidden, w_out[...], preferred_element_type=F32)
    rows = jnp.concatenate(
        [jax.nn.silu(embed + classes[s : s + 1, :]).astype(BF16) for s in range(samples)], axis=0
    )
    to = lax.broadcasted_iota(jnp.int32, (rows.shape[0], rows.shape[0]), 0)
    of = lax.broadcasted_iota(jnp.int32, (rows.shape[0], rows.shape[0]), 1)
    turn = jnp.where(of == (to % samples) * steps + to // samples, 1.0, 0.0).astype(BF16)
    rows = jnp.dot(turn, rows, preferred_element_type=F32).astype(BF16)
    nb = blocks.shape[0]
    contract = (((1,), (1,)), ((), ()))
    part[:, 0:nb] = lax.dot_general(rows, blocks[...], contract, preferred_element_type=F32)
    part[:, nb:] = lax.dot_general(rows, finals[...], contract, preferred_element_type=F32)


def conditioning(
    times, window, labels, time_weight_in, time_weight_out, class_table, blocks, finals, steps
):
    samples = labels.shape[0]
    selector = (
        labels[:, None] == jnp.arange(class_table.shape[0], dtype=jnp.int32)[None, :]
    ).astype(BF16)
    classes = jnp.dot(selector, class_table, preferred_element_type=F32)
    columns = blocks.shape[0] + finals.shape[0]
    smem = pl.BlockSpec(memory_space=pltpu.SMEM)
    vmem = pl.BlockSpec(memory_space=pltpu.VMEM)
    return pl.pallas_call(
        functools.partial(conditioning_kernel, steps, samples),
        out_shape=[
            jax.ShapeDtypeStruct((steps * samples, columns), F32),
            jax.ShapeDtypeStruct((2 * steps, 128), F32),
        ],
        in_specs=[smem] * 3 + [vmem] * 5,
        out_specs=[vmem] * 2,
    )(
        times,
        window,
        jnp.asarray(noise_levels(TRAIN_T)),
        time_weight_in,
        time_weight_out,
        classes,
        blocks,
        finals,
    )


def ring_order(count):
    return list(range(0, count, 2)) + list(range(1, count, 2))[::-1]


ORDER = (
    "zm1", "ym0", "zp1", "yp0", "xm10/m01", "co00/m00", "cp00", "zm2", "ym1", "zp2", "yp1", "b",
    "xm20/m11", "Sm10/m01", "Xm10/m01", "zm3", "ym2", "zp3", "b", "yp2", "xm30/m21",
    "cp10/p01/p11", "Sm20/m11", "Xm20/m11", "ym3", "b", "yp3", "xm31", "Sm30/m21", "Xm30/m21",
    "cp20/p30/p21", "Sm31", "Xm31", "cp31",
)


class Mover:
    def __init__(self, groups, count):
        self.groups, self.count, self.sent, self.pin = groups, count, [], None
        self.to_core = []

    def swap(self, value, distance):
        return self._send(value, lambda i: i ^ distance, lambda g: g, distance > 1 or CORE_COUNTS)

    def across(self, value):
        return self._send(value, lambda i: i, lambda g: g ^ 1)

    def ring(self, value):
        order = ring_order(self.count // 4)
        after = {z: order[(k + 1) % len(order)] for k, z in enumerate(order)}
        return self._send(value, lambda i: after[i // 4] * 4 + i % 4, lambda g: g)

    def _send(self, value, target, side, counts=True):
        if len(self.sent) >= WINDOW:
            value, _ = lax.optimization_barrier((value, self.sent[-WINDOW]))
        if self.pin is not None:
            value, _ = lax.optimization_barrier((value, self.pin))
            self.pin = None
        pairs = [
            (g * self.count + i, side(g) * self.count + target(i))
            for g in range(self.groups)
            for i in range(self.count)
        ]
        value = lax.ppermute(value, ("group", "tm"), pairs)
        (self.sent if counts else self.to_core).append(value)
        return value


def spread_weights(first, halves, groups, count, order):
    mover = Mover(groups, count)
    side = lax.axis_index("group")
    mine = jnp.where(side == 0, halves[0], halves[1])
    other = jnp.where(side == 0, halves[1], halves[0])
    alone = {("p", 0, 0): first, ("m", 0, 0): mine, ("o", 0, 0): other}
    found, stacks = {}, {}

    def note(buffer, keys):
        row = 0
        for key in keys:
            found[key] = (buffer, row)
            row += (first if key[0] == "p" else mine).shape[0]

    def stack(keys):
        rows = [alone[key] for key in keys]
        return jnp.concatenate(rows, axis=0) if len(rows) > 1 else rows[0]

    def pieces():
        lone = [(key + (0,), rows, 0) for key, rows in alone.items()]
        return lone + [(key, *at) for key, at in found.items()]

    for op in order:
        how, kind = op[0], op[1:2]
        keys = [(k[0], int(k[1]), int(k[2])) for k in op[1:].split("/")] if how in "cxSX" else None
        if how == "z":
            r = int(op[2])
            alone[kind, r, 0] = mover.ring(alone[kind, r - 1, 0])
        elif how == "y":
            r = int(op[2])
            alone[kind, r, 1] = mover.swap(alone[kind, r, 0], 2)
        elif how == "x":
            stacks[op[1:]] = (stack(keys), mover.across(stack(keys)))
            note(stacks[op[1:]][1], [("o",) + key[1:] + (0,) for key in keys])
        elif how == "S":
            note(mover.swap(stacks[op[1:]][0], 1), [key + (1,) for key in keys])
        elif how == "X":
            note(mover.swap(stacks[op[1:]][1], 1), [("o",) + key[1:] + (1,) for key in keys])
        elif how == "c":
            note(mover.swap(stack(keys), 1), [key + (1,) for key in keys])
        elif how == "b":
            mover.pin, mover.to_core = mover.to_core, []
    return pieces()


def norm(hidden, shift, scale):
    average = jnp.mean(hidden, axis=0, keepdims=True)
    centered = hidden - average
    variance = jnp.mean(centered * centered, axis=0, keepdims=True)
    return (centered * lax.rsqrt(variance + 1e-06) * (1.0 + scale) + shift).astype(BF16)


def own_terms(packs, flat, samples):
    columns = flat.shape[1]
    position = lax.axis_index("tm")
    for ref, row, rows, shard in packs:
        pack = ref.rows(row, rows)
        where = position * samples
        pick_row = lax.broadcasted_iota(jnp.int32, (PAD, rows), 0)
        pick_of = lax.broadcasted_iota(jnp.int32, (PAD, rows), 1)
        total = jnp.zeros((PAD, columns), F32)
        for k in range(pack.shape[1] // columns):
            hit = (pick_of + k * rows == where + pick_row) & (pick_row < samples)
            pick = jnp.where(hit, 1.0, 0.0).astype(BF16)
            total = total + jnp.dot(
                pick, pack[:, k * columns : (k + 1) * columns], preferred_element_type=F32
            )
        flat[pl.ds(pl.multiple_of(shard * PAD, PAD), PAD), :] = total


def spread_terms(flat_ref, mods, nb, samples):
    columns = flat_ref.shape[1]
    sources = flat_ref.shape[0] // PAD
    tokens = mods.shape[1]
    each = tokens // samples
    block_rows = sources * nb
    flat = flat_ref[...].T.astype(BF16)
    row = lax.broadcasted_iota(jnp.int32, (sources * PAD, tokens), 0)
    sample = lax.broadcasted_iota(jnp.int32, (sources * PAD, tokens), 1) // each
    for j in range(sources):
        spans = [(j * nb, 0, nb), (block_rows + j * (columns - nb), nb, columns)]
        pick = jnp.where(row == j * PAD + sample, 1.0, 0.0).astype(BF16)
        spread = jnp.dot(flat, pick, preferred_element_type=F32)
        for d, u, v in spans:
            mods[pl.ds(d, v - u), :] = spread[u:v]


def product(places, right, limit):
    done = 0
    while done < len(places):
        batch, total = [], 0
        while done < len(places) and (not batch or total + places[done][1] <= limit):
            batch.append(places[done])
            total += places[done][1]
            done += 1
        left = [load() for load, _, _ in batch]
        left = left[0] if len(left) == 1 else jnp.concatenate(left, axis=0)
        result = jnp.dot(left, right, preferred_element_type=F32)
        start = 0
        for _, rows, place in batch:
            yield result[start : start + rows], rows, place
            start += rows


def attention_part(
    state, patch, place, term, queries, mixes, qkv, att, mixed, raised, heads, samples
):
    width, tokens = place.target.shape
    each = tokens // samples
    size = width // heads
    patches = state.ready()[...].astype(BF16)
    hidden = jnp.dot(patch.ready()[...], patches, preferred_element_type=F32)
    hidden = hidden + place.ready()[...]
    normed = norm(hidden, term(0), term(1))
    for result, rows, at in product(queries, normed, width):
        qkv[pl.ds(at, rows), :] = result.astype(BF16)
    sample_of = lax.broadcasted_iota(jnp.int32, (each, tokens), 1) // each
    scale = 1.0 / math.sqrt(size)
    for k in range(heads):
        query = qkv[pl.ds(k * size, size), :]
        key = qkv[pl.ds(width + k * size, size), :]
        scores = lax.dot_general(
            key, query, (((0,), (0,)), ((), ())), preferred_element_type=F32
        )
        mine = scores[0:each]
        for s in range(1, samples):
            mine = jnp.where(sample_of == s, scores[s * each : (s + 1) * each], mine)
        raised[pl.ds(k * each, each), :] = jnp.exp(mine * scale)
    for k in range(heads):
        value = qkv[pl.ds(2 * width + k * size, size), :]
        weights = raised[pl.ds(k * each, each), :]
        weights = weights / jnp.sum(weights, axis=0, keepdims=True)
        spread = jnp.concatenate(
            [jnp.where(sample_of == s, weights, 0.0).astype(BF16) for s in range(samples)], axis=0
        )
        att[pl.ds(k * size, size), :] = jnp.dot(
            value, spread, preferred_element_type=F32
        ).astype(BF16)
    for result, rows, at in product(mixes, att[...], width):
        mixed[pl.ds(at, rows), :] = result
    return hidden + term(2) * mixed[...]


def feed_part(hidden, state, term, out, scales, expands, shrinks, mid, mixed):
    width = hidden.shape[0]
    normed = norm(hidden, term(3), term(4))
    for result, rows, at in product(expands, normed, width):
        mid[pl.ds(at, rows), :] = jax.nn.gelu(result, approximate=True).astype(BF16)
    right = jnp.concatenate([mid[pl.ds(start, width), :] for start, _ in shrinks], axis=0)
    slices = [places for _, places in shrinks]
    joined = [
        (joined_rows([at[k][0] for at in slices]), slices[0][k][1], slices[0][k][2])
        for k in range(len(slices[0]))
    ]
    for result, rows, at in product(joined, right, width):
        mixed[pl.ds(at, rows), :] = result
    hidden = hidden + term(5) * mixed[...]
    normed = norm(hidden, term(6), term(7))
    predicted = jnp.dot(out.ready()[...], normed, preferred_element_type=F32)
    position = lax.axis_index("tm")
    scales = scales.ready()
    scale_state = scales[pl.ds(position, 1), 0:1]
    scale_noise = scales[pl.ds(scales.shape[0] // 2 + position, 1), 0:1]
    return (scale_state - 1.0) * state.ready()[...] + scale_noise * predicted


def owner(r, dy, core):
    position = lax.axis_index("tm")
    depth = lax.axis_size("tm") // 4
    z = position // 4
    spot = jnp.where(z % 2 == 0, z // 2, depth - 1 - z // 2)
    spot = (spot - r + depth) % depth
    z = jnp.where(2 * spot < depth, 2 * spot, 2 * (depth - spot) - 1)
    return z * 4 + ((position % 4) ^ (2 * dy + core))


def joined_rows(loads):
    return lambda: jnp.concatenate([one() for one in loads], axis=1)


class Fetched:
    def __init__(self, source, target, sem):
        self.target, self.copy, self.here = target, pltpu.make_async_copy(source, target, sem), False
        self.copy.start()

    def ready(self):
        if not self.here:
            self.copy.wait()
            self.here = True
        return self.target

    def rows(self, start, rows):
        return self.ready()[pl.ds(start, rows), :]


def load(ref, start, rows):
    return lambda: ref.rows(start, rows)


def placed(keys, refs, sizes):
    nq, nm, ne, ns, width, pack_rows = sizes
    queries, mixes, expands, shrinks, packs = [], [], [], [], []
    if keys[0][0] is None:
        query, mix, expand, shrink = refs
        queries.append((load(query, 0, 3 * width), 3 * width, 0))
        mixes.append((load(mix, 0, width), width, 0))
        expands = [(load(expand, k * width, width), width, k * width) for k in range(ns)]
        shrinks = [(k * width, [(load(shrink, k * width, width), width, 0)]) for k in range(ns)]
        return queries, mixes, expands, shrinks, packs
    side = lax.axis_index("group")
    he, hs = ne // 2, ns // 2
    by_slice = {(kind, k): [] for kind in "mo" for k in range(hs)}
    for (kind, r, dy, core), which, row in keys:
        ref, shard = refs[which], owner(r, dy, core)
        if kind == "p":
            queries.append((load(ref, row, nq), nq, pl.multiple_of(shard * nq, 16)))
            mixes.append((load(ref, row + nq, nm), nm, pl.multiple_of(shard * nm, 16)))
            packs.append((ref, row + nq + nm, pack_rows, shard))
            continue
        half = side if kind == "m" else 1 - side
        expands.append((load(ref, row, he), he, pl.multiple_of(shard * ne + half * he, 16)))
        for k in range(hs):
            by_slice[kind, k].append(
                (load(ref, row + he + k * nm, nm), nm, pl.multiple_of(shard * nm, 16))
            )
    for (kind, k), places in by_slice.items():
        half = side if kind == "m" else 1 - side
        shrinks.append((pl.multiple_of((half * hs + k) * width, width), places))
    return queries, mixes, expands, shrinks, packs


def network_kernel(names, keys, count, sizes, nb, heads, samples, *refs):
    width = sizes[4]
    refs = list(refs)
    take = lambda: refs.pop(0)
    given = [take() for _ in range(len(names) + count)]
    results = [take() for _ in range(2 if "terms" in names else 3)]
    fetched = [Fetched(ref, take(), refs[-1].at[k]) for k, ref in enumerate(given)]
    buffers = fetched[len(names) :]
    by_name = dict(zip(names, fetched))
    state, scales, patch, place, out, terms = (
        by_name.get(name) for name in ("state", "scales", "patch", "place", "out", "terms")
    )
    mods, mixed = take(), take()
    queries, mixes, expands, shrinks, packs = placed(keys, buffers, sizes)
    if terms is None:
        flat = results[2]
        own_terms(packs, flat, samples)
    else:
        flat = terms.ready()
    spread_terms(flat, mods, nb, samples)
    term = lambda k: mods[pl.ds(k * width, width), :]
    qkv, att, mid, raised = take(), take(), take(), take()
    hidden = attention_part(
        state, patch, place, term, queries, mixes, qkv, att, mixed, raised, heads, samples
    )
    drift = feed_part(
        hidden, state, term, out, scales, expands, shrinks, mid, mixed
    )
    results[0][...] = drift
    results[1][...] = drift.astype(BF16)
    for one in fetched:
        one.ready()


def run_network(fixed, pieces, sizes, nb, columns, heads, samples):
    width, tokens = fixed["place"].shape
    patch = fixed["state"].shape[0]
    ff = sizes[3] * width
    needs = ["terms", "state", "patch", "place", "out", "scales"]
    names = [name for name in needs if name in fixed]
    buffers, keys = [], []
    if pieces[0][0] is not None:
        pieces = sorted(pieces, key=lambda piece: (piece[0][0] != "p", piece[0][1:]))
    for key, rows, row in pieces:
        which = [k for k, known in enumerate(buffers) if known is rows]
        keys.append((key, which[0] if which else len(buffers), row))
        if not which:
            buffers.append(rows)
    operands = [fixed[name] for name in names] + buffers
    scratch = [pltpu.VMEM(rows.shape, rows.dtype) for rows in operands]
    scratch += [pltpu.VMEM((8 * width, tokens), F32), pltpu.VMEM((width, tokens), F32)]
    scratch += [
        pltpu.VMEM((3 * width, tokens), BF16),
        pltpu.VMEM((width, tokens), BF16),
        pltpu.VMEM((ff, tokens), BF16),
        pltpu.VMEM((heads * tokens // samples, tokens), F32),
    ]
    out_shape = [
        jax.ShapeDtypeStruct((patch, tokens), F32),
        jax.ShapeDtypeStruct((patch, tokens), BF16),
    ]
    if "terms" not in names:
        sources = 8 * width // columns
        out_shape.append(jax.ShapeDtypeStruct((sources * PAD, columns), F32))
    scratch.append(pltpu.SemaphoreType.DMA((len(operands),)))
    rows = 4 * width + 2 * ff
    return pl.pallas_call(
        functools.partial(
            network_kernel, names, keys, len(buffers), sizes, nb, heads, samples
        ),
        out_shape=out_shape,
        in_specs=[pl.BlockSpec(memory_space=pl.ANY)] * len(operands),
        out_specs=[pl.BlockSpec(memory_space=pltpu.VMEM)] * len(out_shape),
        scratch_shapes=scratch,
        compiler_params=pltpu.CompilerParams(vmem_limit_bytes=VMEM_LIMIT),
        cost_estimate=pl.CostEstimate(
            flops=2 * rows * width * tokens, bytes_accessed=2 * rows * width, transcendentals=0
        ),
    )(*operands)


def earlier_sum(value, narrow, count):
    position = lax.axis_index("tm")
    total = value
    before = jnp.zeros_like(value)
    distance = 1
    while distance < count:
        pairs = [(i, i ^ distance) for i in range(count)]
        other = lax.ppermute(narrow, "tm", pairs).astype(value.dtype)
        before = jnp.where((position & distance) != 0, before + other, before)
        total = total + other
        narrow = total.astype(BF16)
        distance *= 2
    return before


def body(
    noise,
    labels,
    timesteps,
    window_start,
    time_weight_in,
    time_weight_out,
    class_table,
    patch_weight,
    query_key_value,
    mix_weight,
    expand_weight,
    shrink_weight,
    block_modulation,
    final_modulation,
    output_weight,
):
    groups, count = lax.axis_size("group"), lax.axis_size("tm")
    samples, latent = noise.shape
    patch, width = patch_weight.shape
    each = latent // patch
    tokens = samples * each

    nq, nm, ne = query_key_value.shape[2], mix_weight.shape[2], expand_weight.shape[2]
    ns = shrink_weight.shape[1] // width
    columns = block_modulation.shape[2] + final_modulation.shape[1]
    packed = width // columns
    pack_rows = count * samples // max(packed, 1)
    sizes = (nq, nm, ne, ns, width, pack_rows)
    q_rows, m_rows, e_rows = query_key_value[0].T, mix_weight[0].T, expand_weight[0].T
    s_rows = shrink_weight[0].reshape(ns, width, nm).transpose(0, 2, 1)
    nb = block_modulation.shape[2]

    def prelude(times):
        return conditioning(
            times,
            window_start,
            labels,
            time_weight_in,
            time_weight_out,
            class_table,
            block_modulation[0].T,
            final_modulation.T,
            count,
        )

    place = jnp.asarray(position_columns(each, width, samples))
    part, scales = prelude(timesteps)
    start = noise.reshape(samples, each, patch).transpose(2, 0, 1).reshape(patch, tokens)
    fixed = dict(
        scales=scales, patch=patch_weight.T, place=place, out=output_weight.T, state=start
    )

    def network(pieces, **more):
        return run_network({**fixed, **more}, pieces, sizes, nb, columns, HEADS, samples)

    short = (
        groups == 2
        and count == 16
        and ns % 2 == 0
        and packed * columns == width
        and packed * pack_rows == count * samples
        and samples <= PAD
        and all(v % 16 == 0 for v in (nq, nm, ne // 2, pack_rows))
    )
    if short:
        half_e, half_s = ne // 2, ns // 2
        packs = [part[k * pack_rows : (k + 1) * pack_rows] for k in range(packed)]
        packs = jnp.concatenate(packs, axis=1).astype(BF16)
        first = jnp.concatenate([q_rows, m_rows, packs], axis=0)
        halves = [
            jnp.concatenate(
                [e_rows[k * half_e : (k + 1) * half_e]]
                + [s_rows[k * half_s + j] for j in range(half_s)],
                axis=0,
            )
            for k in range(2)
        ]
        pieces = spread_weights(first, halves, groups, count, ORDER)
        drift, narrow, terms = network(pieces)
    else:
        whole = lambda rows, axis: lax.all_gather(rows, "tm", axis=axis, tiled=True)
        terms = part.astype(BF16).reshape(count, samples, columns)
        terms = lax.all_to_all(terms, "tm", split_axis=0, concat_axis=0, tiled=True)
        terms = jnp.pad(terms.astype(F32), ((0, 0), (0, -samples % PAD), (0, 0)))
        terms = terms.reshape(count * PAD, columns)
        pieces = [
            (None, whole(q_rows, 0), 0),
            (None, whole(m_rows, 0), 0),
            (None, whole(e_rows, 0), 0),
            (None, whole(s_rows, 1).reshape(ns * width, width), 0),
        ]
        drift, narrow = network(pieces, terms=terms)

    states = start
    for sweep in range(ITERS):
        if sweep > 0:
            drift, narrow = network(pieces, terms=terms, state=states)
        before = earlier_sum(drift, narrow, count)
        running = before + drift
        states = start + before
    result = (start + running).reshape(patch, samples, each).transpose(1, 2, 0)
    return result.reshape(1, samples, latent)


def solution(mesh):
    return jax.shard_map(
        body,
        mesh=mesh,
        in_specs=(
            P("group", None),
            P("group"),
            P(),
            P(),
            P(),
            P(),
            P(),
            P(),
            P(None, None, "tm"),
            P(None, None, "tm"),
            P(None, None, "tm"),
            P(None, None, "tm"),
            P(None, None, "tm"),
            P(None, "tm"),
            P(),
        ),
        out_specs=P("tm", "group", None),
        check_vma=False,
    )
```

time: 297 us -> 143 us (0.48)
  blocking collectives: 63 us -> 0 us
  waiting for transfers between devices: 119 us -> 61.1 us
  matrix products: 46.3 us -> 0.95 us
  Pallas kernels: 0 us -> 33.8 us
  starting transfers between devices: 9.61 us -> 38.3 us
  local copies, waits for them, and re-layouts: 31.9 us -> 5.3 us
  between operations: 17.4 us -> 1.19 us
  other arithmetic: 8.2 us -> 2.39 us
    all_gather x4 -> x0, waiting for transfers between devices: 110 us -> none  [the longest x1 51.8 us: body(): lax.all_gather(expand_weight, 'tm', axis=2, tiled=True)]
    all_gather x3 -> x0, blocking collectives: 63 us -> none  [the longest x2 39.5 us: carried_in(): everything = lax.all_gather(x.astype(jnp.bfloat16), axis)]
    ppermute x0 -> x39, waiting for transfers between devices: none -> 61.1 us  [the longest x31 43.4 us: _send(): value = lax.ppermute(value, ('group', 'tm'), pairs)]
    dot_general x21 -> x1, matrix products: 46.3 us -> 0.95 us  [conditioning(): classes = jnp.dot(selector, class_table, preferred_element_type=F32)]
    ppermute x0 -> x39, starting transfers between devices: none -> 38.3 us  [the longest x31 26.1 us: _send(): value = lax.ppermute(value, ('group', 'tm'), pairs)]
    pallas_call x0 -> x3, Pallas kernels: none -> 33.8 us  [the longest x2 30.7 us: run_network(): pl.pallas_call(functools.partial(network_kernel, names, keys, len(buffers...]
    unnamed x78 -> x72, local copies, waits for them, and re-layouts: 12.4 us -> 1.8 us
    all_to_all x2 -> x0, starting transfers between devices: 9.46 us -> none  [the longest x1 5.98 us: body(): lax.all_to_all(block_part.astype(jnp.bfloat16), 'tm', split_axis=1, conca...]
  transfers between devices with their start and end apart: 6 -> 39, of which waited for: 4 -> 22; matrix products, arithmetic and copies ran while one was open for 15% -> 4% of each run, Pallas kernels for 0% -> 2%
where the time goes in v2:
time: 143 us
  waiting for transfers between devices  61.1 us (43%)
  starting transfers between devices  38.3 us (27%)
  Pallas kernels  33.8 us (24%)
  local copies, waits for them, and re-layouts  5.3 us (4%)
  other arithmetic  2.39 us (2%)
    ppermute x31, waiting for transfers between devices, _send(): value = lax.ppermute(value, ('group', 'tm'), pairs)  43.4 us
    pallas_call x2, Pallas kernels, run_network(): pl.pallas_call(functools.partial(network_kernel, names, keys, len(buffers...  30.7 us
    ppermute x31, starting transfers between devices, _send(): value = lax.ppermute(value, ('group', 'tm'), pairs)  26.1 us
    ppermute x8, waiting for transfers between devices, earlier_sum(): other = lax.ppermute(narrow, 'tm', pairs).astype(value.dtype)  17.6 us
    ppermute x8, starting transfers between devices, earlier_sum(): other = lax.ppermute(narrow, 'tm', pairs).astype(value.dtype)  12.2 us
    pallas_call x1, Pallas kernels, conditioning(): pl.pallas_call(functools.partial(conditioning_kernel, steps, samples), ou...  3.12 us
  transfers between devices with their start and end apart: 39, of which 22 were waited for; matrix products, arithmetic and copies ran while one was open for 4% of the time, Pallas kernels for 2%

profile of v2, /device:TPU:0, one launch (start us, length us, event | category | flops | bytes accessed | tf_op | source)
XLA Modules:
  0.0 143.0 jit_solution(1242319478979857011)
XLA Ops:
  1.6 4.1 %collective-permute-start = (bf16[192,768]{1,0:T(8,128)(2,1)S(1)}, bf16[192,768]{1,0:T(8,128)(2,1)S(1)}, u32[]{:S(2)}, u32[]{:S(2)}) collective-permute-start(bf16[192,768]{1,0:T(8,128)(2,1)S(1)} %get-tuple-element.78.refs_17_.refs_18_), channel_id=1, source_target_pairs={{0,8},{1,9},{2,10},{3,11},{4,0},{5,1},{6,2},{7,3},{8,12},{9,13},{1... | collective-permute-start | bytes 884744 | tf_op jit(solution)/shard_map/ppermute | solution.py:145
  8.8 3.1 %shard_map.163 = (f32[64,384]{1,0:T(8,128)}, f32[32,128]{1,0:T(8,128)}) custom-call(s32[25]{0:T(128)} %times.1, s32[1]{0:T(128)S(6)} %copy.30.window, f32[1000]{0:T(1024)} %constant.26.clone.levels, bf16[256,768]{1,0:T(8,128)(2,1)} %w_in.1, bf16[768,768]{1,0:T(8,128)(2,1)} %w_out.1, f32[4,768]{1,0:T(4,128)} %fusion.9.classes, bf16[288,768]{1,0:T(8,128)(2,1)} %bitcast.38, ...), custom_call_target="tpu_custom_call" | custom-call | tf_op jit(solution)/shard_map/pallas_call | solution.py:86
  17.1 5.1 %collective-permute-done.2.refs_7_.refs_8_ = bf16[224,768]{1,0:T(8,128)(2,1)S(1)} collective-permute-done((bf16[224,768]{1,0:T(8,128)(2,1)S(1)}, bf16[224,768]{1,0:T(8,128)(2,1)S(1)}, u32[]{:S(2)}, u32[]{:S(2)}) %collective-permute-start.2) | collective-permute-done | bytes 344096 | tf_op jit(solution)/shard_map/ppermute | solution.py:145
  24.5 4.3 %collective-permute-done.5.refs_29_.refs_30_ = bf16[192,768]{1,0:T(8,128)(2,1)S(1)} collective-permute-done((bf16[192,768]{1,0:T(8,128)(2,1)S(1)}, bf16[192,768]{1,0:T(8,128)(2,1)S(1)}, u32[]{:S(2)}, u32[]{:S(2)}) %collective-permute-start.5) | collective-permute-done | bytes 294944 | tf_op jit(solution)/shard_map/ppermute | solution.py:145
  30.3 2.5 %collective-permute-start.6 = (bf16[192,768]{1,0:T(8,128)(2,1)S(1)}, bf16[192,768]{1,0:T(8,128)(2,1)S(1)}, u32[]{:S(2)}, u32[]{:S(2)}) collective-permute-start(bf16[192,768]{1,0:T(8,128)(2,1)S(1)} %collective-permute-done.5.refs_29_.refs_30_), channel_id=1, source_target_pairs={{0,8},{1,9},{2,10},{3,11},{4,0},{5,1},{6,2},{7,3},{8,12},{9,13},{1... | collective-permute-start | bytes 884744 | tf_op jit(solution)/shard_map/ppermute | solution.py:145
  34.5 2.3 %collective-permute-done.4.refs_10_.refs_11_ = bf16[224,768]{1,0:T(8,128)(2,1)S(1)} collective-permute-done((bf16[224,768]{1,0:T(8,128)(2,1)S(1)}, bf16[224,768]{1,0:T(8,128)(2,1)S(1)}, u32[]{:S(2)}, u32[]{:S(2)}) %collective-permute-start.4) | collective-permute-done | bytes 344096 | tf_op jit(solution)/shard_map/ppermute | solution.py:145
  37.0 3.2 %collective-permute-done.6.refs_34_.refs_35_ = bf16[192,768]{1,0:T(8,128)(2,1)S(1)} collective-permute-done((bf16[192,768]{1,0:T(8,128)(2,1)S(1)}, bf16[192,768]{1,0:T(8,128)(2,1)S(1)}, u32[]{:S(2)}, u32[]{:S(2)}) %collective-permute-start.6) | collective-permute-done | bytes 294944 | tf_op jit(solution)/shard_map/ppermute | solution.py:145
  40.2 4.1 %collective-permute-done.8.refs_11_.refs_12_ = bf16[224,768]{1,0:T(8,128)(2,1)S(1)} collective-permute-done((bf16[224,768]{1,0:T(8,128)(2,1)S(1)}, bf16[224,768]{1,0:T(8,128)(2,1)S(1)}, u32[]{:S(2)}, u32[]{:S(2)}) %collective-permute-start.8) | collective-permute-done | bytes 344096 | tf_op jit(solution)/shard_map/ppermute | solution.py:145
  45.8 2.7 %collective-permute-start.9 = (bf16[224,768]{1,0:T(8,128)(2,1)S(1)}, bf16[224,768]{1,0:T(8,128)(2,1)S(1)}, u32[]{:S(2)}, u32[]{:S(2)}) collective-permute-start(bf16[224,768]{1,0:T(8,128)(2,1)S(1)} %collective-permute-done.8.refs_11_.refs_12_), channel_id=1, source_target_pairs={{0,8},{1,9},{2,10},{3,11},{4,0},{5,1},{6,2},{7,3},{8,12},{9,13},{1... | collective-permute-start | bytes 1032200 | tf_op jit(solution)/shard_map/ppermute | solution.py:145
  48.5 2.6 %collective-permute-done.17.refs_30_.refs_31_ = bf16[192,768]{1,0:T(8,128)(2,1)S(1)} collective-permute-done((bf16[192,768]{1,0:T(8,128)(2,1)S(1)}, bf16[192,768]{1,0:T(8,128)(2,1)S(1)}, u32[]{:S(2)}, u32[]{:S(2)}) %collective-permute-start.17) | collective-permute-done | bytes 294944 | tf_op jit(solution)/shard_map/ppermute | solution.py:145
  53.1 3.2 %collective-permute-done.9.refs_14_.refs_15_ = bf16[224,768]{1,0:T(8,128)(2,1)S(1)} collective-permute-done((bf16[224,768]{1,0:T(8,128)(2,1)S(1)}, bf16[224,768]{1,0:T(8,128)(2,1)S(1)}, u32[]{:S(2)}, u32[]{:S(2)}) %collective-permute-start.9) | collective-permute-done | bytes 344096 | tf_op jit(solution)/shard_map/ppermute | solution.py:145
  62.3 7.7 %collective-permute-done.27.refs_35_.refs_36_ = bf16[192,768]{1,0:T(8,128)(2,1)S(1)} collective-permute-done((bf16[192,768]{1,0:T(8,128)(2,1)S(1)}, bf16[192,768]{1,0:T(8,128)(2,1)S(1)}, u32[]{:S(2)}, u32[]{:S(2)}) %collective-permute-start.27) | collective-permute-done | bytes 294944 | tf_op jit(solution)/shard_map/ppermute | solution.py:145
  72.0 5.1 %collective-permute-done.22.refs_15_.refs_16_ = bf16[224,768]{1,0:T(8,128)(2,1)} collective-permute-done((bf16[224,768]{1,0:T(8,128)(2,1)S(1)}, bf16[224,768]{1,0:T(8,128)(2,1)}, u32[]{:S(2)}, u32[]{:S(2)}) %collective-permute-start.22) | collective-permute-done | bytes 344096 | tf_op jit(solution)/shard_map/ppermute | solution.py:145
  81.3 15.7 %shard_map.164 = (f32[64,256]{1,0:T(8,128)S(1)}, bf16[64,256]{1,0:T(8,128)(2,1)S(1)}, f32[128,384]{1,0:T(8,128)S(1)}) custom-call(f32[64,256]{1,0:T(8,128)S(1)} %reshape.14.refs_0_, bf16[768,64]{1,0:T(8,128)(2,1)S(1)} %bitcast.31, f32[768,256]{1,0:T(8,128)} %constant.25.clone.refs_2_.refs_3_, bf16[64,768]{1,0:T(8,128)(2,1)S(1)} %bitcast.33, ...), custom_call_target="tpu_custom_call" | custom-call | flops 3623878656 | bytes 14155776 | tf_op jit(solution)/shard_map/pallas_call | solution.py:447
  99.9 2.4 %collective-permute-done.32 = bf16[64,256]{1,0:T(8,128)(2,1)S(1)} collective-permute-done((bf16[64,256]{1,0:T(8,128)(2,1)S(1)}, bf16[64,256]{1,0:T(8,128)(2,1)S(1)}, u32[]{:S(2)}, u32[]{:S(2)}) %collective-permute-start.32) | collective-permute-done | bytes 32800 | tf_op jit(solution)/shard_map/ppermute | solution.py:469
  102.3 1.8 %collective-permute-start.33 = (bf16[64,256]{1,0:T(8,128)(2,1)S(1)}, bf16[64,256]{1,0:T(8,128)(2,1)S(1)}, u32[]{:S(2)}, u32[]{:S(2)}) collective-permute-start(bf16[64,256]{1,0:T(8,128)(2,1)S(1)} %fusion.7), channel_id=1, source_target_pairs={{0,4},{1,5},{2,6},{3,7},{4,0},{5,1},{6,2},{7,3},{8,12},{9,13},{10,... | collective-permute-start | bytes 98312 | tf_op jit(solution)/shard_map/ppermute | solution.py:469
  104.2 2.1 %collective-permute-done.33 = bf16[64,256]{1,0:T(8,128)(2,1)S(1)} collective-permute-done((bf16[64,256]{1,0:T(8,128)(2,1)S(1)}, bf16[64,256]{1,0:T(8,128)(2,1)S(1)}, u32[]{:S(2)}, u32[]{:S(2)}) %collective-permute-start.33) | collective-permute-done | bytes 32800 | tf_op jit(solution)/shard_map/ppermute | solution.py:469
  106.3 4.4 %collective-permute-start.34 = (bf16[64,256]{1,0:T(8,128)(2,1)S(1)}, bf16[64,256]{1,0:T(8,128)(2,1)S(1)}, u32[]{:S(2)}, u32[]{:S(2)}) collective-permute-start(bf16[64,256]{1,0:T(8,128)(2,1)S(1)} %fusion), channel_id=1, source_target_pairs={{0,8},{1,9},{2,10},{3,11},{4,12},{5,13},{6,14},{7,15},{8,0},{9,1},... | collective-permute-start | bytes 98312 | tf_op jit(solution)/shard_map/ppermute | solution.py:469
  110.7 2.1 %collective-permute-done.34 = bf16[64,256]{1,0:T(8,128)(2,1)S(1)} collective-permute-done((bf16[64,256]{1,0:T(8,128)(2,1)S(1)}, bf16[64,256]{1,0:T(8,128)(2,1)S(1)}, u32[]{:S(2)}, u32[]{:S(2)}) %collective-permute-start.34) | collective-permute-done | bytes 32800 | tf_op jit(solution)/shard_map/ppermute | solution.py:469
  112.8 15.0 %shard_map.165 = (f32[64,256]{1,0:T(8,128)S(1)}, bf16[64,256]{1,0:T(8,128)(2,1)S(1)}) custom-call(f32[128,384]{1,0:T(8,128)S(1)} %get-tuple-element.72.refs_0_, f32[64,256]{1,0:T(8,128)S(1)} %fusion.2.refs_1_, bf16[768,64]{1,0:T(8,128)(2,1)S(1)} %bitcast.32, f32[768,256]{1,0:T(8,128)} %constant.25.clone.refs_2_.refs_3_, bf16[64,768]{1,0:T(8,128)(2,1)S(1)} %bitcast.34, ...), custom_call_target="tpu_custom_call" | custom-call | flops 3623878656 | bytes 14155776 | tf_op jit(solution)/shard_map/pallas_call | solution.py:447
  129.8 3.3 %collective-permute-done.36 = bf16[64,256]{1,0:T(8,128)(2,1)S(1)} collective-permute-done((bf16[64,256]{1,0:T(8,128)(2,1)S(1)}, bf16[64,256]{1,0:T(8,128)(2,1)S(1)}, u32[]{:S(2)}, u32[]{:S(2)}) %collective-permute-start.36) | collective-permute-done | bytes 32800 | tf_op jit(solution)/shard_map/ppermute | solution.py:469
  133.4 3.7 %collective-permute-done.37 = bf16[64,256]{1,0:T(8,128)(2,1)S(1)} collective-permute-done((bf16[64,256]{1,0:T(8,128)(2,1)S(1)}, bf16[64,256]{1,0:T(8,128)(2,1)S(1)}, u32[]{:S(2)}, u32[]{:S(2)}) %collective-permute-start.37) | collective-permute-done | bytes 32800 | tf_op jit(solution)/shard_map/ppermute | solution.py:469
  137.1 2.8 %collective-permute-start.38 = (bf16[64,256]{1,0:T(8,128)(2,1)S(1)}, bf16[64,256]{1,0:T(8,128)(2,1)S(1)}, u32[]{:S(2)}, u32[]{:S(2)}) collective-permute-start(bf16[64,256]{1,0:T(8,128)(2,1)S(1)} %fusion.1), channel_id=1, source_target_pairs={{0,8},{1,9},{2,10},{3,11},{4,12},{5,13},{6,14},{7,15},{8,0},{9,1},... | collective-permute-start | bytes 98312 | tf_op jit(solution)/shard_map/ppermute | solution.py:469
  139.9 2.1 %collective-permute-done.38 = bf16[64,256]{1,0:T(8,128)(2,1)S(1)} collective-permute-done((bf16[64,256]{1,0:T(8,128)(2,1)S(1)}, bf16[64,256]{1,0:T(8,128)(2,1)S(1)}, u32[]{:S(2)}, u32[]{:S(2)}) %collective-permute-start.38) | collective-permute-done | bytes 32800 | tf_op jit(solution)/shard_map/ppermute | solution.py:469
  (158 shorter events, 36.6 us)
Async XLA Ops:
  1.6 13.5 %collective-permute-start = (bf16[192,768]{1,0:T(8,128)(2,1)S(1)}, bf16[192,768]{1,0:T(8,128)(2,1)S(1)}, u32[]{:S(2)}, u32[]{:S(2)}) collective-permute-start(bf16[192,768]{1,0:T(8,128)(2,1)S(1)} %get-tuple-element.78.refs_17_.refs_18_), channel_id=1, source_target_pairs={{0,8},{1,9},{2,10},{3,11},{4,0},{5,1},{6,2},{7,3},{8,12},{9,13},{1... | collective-permute-start | bytes 884744 | tf_op jit(solution)/shard_map/ppermute | solution.py:145
  5.7 9.8 %collective-permute-start.10 = (bf16[192,768]{1,0:T(8,128)(2,1)S(1)}, bf16[192,768]{1,0:T(8,128)(2,1)S(1)}, u32[]{:S(2)}, u32[]{:S(2)}) collective-permute-start(bf16[192,768]{1,0:T(8,128)(2,1)S(1)} %get-tuple-element.78.refs_17_.refs_18_), channel_id=1, source_target_pairs={{0,2},{1,3},{2,0},{3,1},{4,6},{5,7},{6,4},{7,5},{8,10},{9,11},{10,... | collective-permute-start | bytes 884744 | tf_op jit(solution)/shard_map/ppermute | solution.py:145
  12.9 9.3 %collective-permute-start.2 = (bf16[224,768]{1,0:T(8,128)(2,1)S(1)}, bf16[224,768]{1,0:T(8,128)(2,1)S(1)}, u32[]{:S(2)}, u32[]{:S(2)}) collective-permute-start(bf16[224,768]{1,0:T(8,128)(2,1)S(1)} %maximum_maximum_fusion.refs_5_.refs_6_), channel_id=1, source_target_pairs={{0,2},{1,3},{2,0},{3,1},{4,6},{5,7},{6,4},{7,5},{8,10},{9,11},{10,... | collective-permute-start | bytes 1032200 | tf_op jit(solution)/shard_map/ppermute | solution.py:145
  13.5 11.0 %collective-permute-start.3 = (bf16[224,768]{1,0:T(8,128)(2,1)S(1)}, bf16[224,768]{1,0:T(8,128)(2,1)S(1)}, u32[]{:S(2)}, u32[]{:S(2)}) collective-permute-start(bf16[224,768]{1,0:T(8,128)(2,1)S(1)} %maximum_maximum_fusion.refs_5_.refs_6_), channel_id=1, source_target_pairs={{0,8},{1,9},{2,10},{3,11},{4,0},{5,1},{6,2},{7,3},{8,12},{9,13},{1... | collective-permute-start | bytes 1032200 | tf_op jit(solution)/shard_map/ppermute | solution.py:145
  15.0 13.7 %collective-permute-start.5 = (bf16[192,768]{1,0:T(8,128)(2,1)S(1)}, bf16[192,768]{1,0:T(8,128)(2,1)S(1)}, u32[]{:S(2)}, u32[]{:S(2)}) collective-permute-start(bf16[192,768]{1,0:T(8,128)(2,1)S(1)} %collective-permute-done.refs_24_.refs_25_), channel_id=1, source_target_pairs={{0,8},{1,9},{2,10},{3,11},{4,0},{5,1},{6,2},{7,3},{8,12},{9,13},{1... | collective-permute-start | bytes 884744 | tf_op jit(solution)/shard_map/ppermute | solution.py:145
  15.5 17.3 %collective-permute-start.12 = (bf16[384,768]{1,0:T(8,128)(2,1)S(1)}, bf16[384,768]{1,0:T(8,128)(2,1)S(1)}, u32[]{:S(2)}, u32[]{:S(2)}) collective-permute-start(bf16[384,768]{1,0:T(8,128)(2,1)S(1)} %constant_dynamic-update-slice_fusion), channel_id=1, source_target_pairs={{0,16},{1,17},{2,18},{3,19},{4,20},{5,21},{6,22},{7,23},{8,24},{9,... | collective-permute-start | bytes 1769480 | tf_op jit(solution)/shard_map/ppermute | solution.py:145
  17.1 15.9 %collective-permute-start.19 = (bf16[384,768]{1,0:T(8,128)(2,1)S(1)}, bf16[384,768]{1,0:T(8,128)(2,1)S(1)}, u32[]{:S(2)}, u32[]{:S(2)}) collective-permute-start(bf16[384,768]{1,0:T(8,128)(2,1)S(1)} %pad_maximum_fusion.2), channel_id=1, source_target_pairs={{0,1},{1,0},{2,3},{3,2},{4,5},{5,4},{6,7},{7,6},{8,9},{9,8},{10,11... | collective-permute-start | bytes 1769480 | tf_op jit(solution)/shard_map/ppermute | solution.py:145
  24.5 8.4 %collective-permute-start.1 = (bf16[224,768]{1,0:T(8,128)(2,1)S(1)}, bf16[224,768]{1,0:T(8,128)(2,1)S(1)}, u32[]{:S(2)}, u32[]{:S(2)}) collective-permute-start(bf16[224,768]{1,0:T(8,128)(2,1)S(1)} %maximum_maximum_fusion.refs_5_.refs_6_), channel_id=1, source_target_pairs={{0,1},{1,0},{2,3},{3,2},{4,5},{5,4},{6,7},{7,6},{8,9},{9,8},{10,11... | collective-permute-start | bytes 1032200 | tf_op jit(solution)/shard_map/ppermute | solution.py:145
  28.7 8.1 %collective-permute-start.4 = (bf16[224,768]{1,0:T(8,128)(2,1)S(1)}, bf16[224,768]{1,0:T(8,128)(2,1)S(1)}, u32[]{:S(2)}, u32[]{:S(2)}) collective-permute-start(bf16[224,768]{1,0:T(8,128)(2,1)S(1)} %collective-permute-done.3.refs_9_.refs_10_), channel_id=1, source_target_pairs={{0,2},{1,3},{2,0},{3,1},{4,6},{5,7},{6,4},{7,5},{8,10},{9,11},{10,... | collective-permute-start | bytes 1032200 | tf_op jit(solution)/shard_map/ppermute | solution.py:145
  30.3 9.9 %collective-permute-start.6 = (bf16[192,768]{1,0:T(8,128)(2,1)S(1)}, bf16[192,768]{1,0:T(8,128)(2,1)S(1)}, u32[]{:S(2)}, u32[]{:S(2)}) collective-permute-start(bf16[192,768]{1,0:T(8,128)(2,1)S(1)} %collective-permute-done.5.refs_29_.refs_30_), channel_id=1, source_target_pairs={{0,8},{1,9},{2,10},{3,11},{4,0},{5,1},{6,2},{7,3},{8,12},{9,13},{1... | collective-permute-start | bytes 884744 | tf_op jit(solution)/shard_map/ppermute | solution.py:145
  32.8 11.6 %collective-permute-start.8 = (bf16[224,768]{1,0:T(8,128)(2,1)S(1)}, bf16[224,768]{1,0:T(8,128)(2,1)S(1)}, u32[]{:S(2)}, u32[]{:S(2)}) collective-permute-start(bf16[224,768]{1,0:T(8,128)(2,1)S(1)} %collective-permute-done.3.refs_9_.refs_10_), channel_id=1, source_target_pairs={{0,8},{1,9},{2,10},{3,11},{4,0},{5,1},{6,2},{7,3},{8,12},{9,13},{1... | collective-permute-start | bytes 1032200 | tf_op jit(solution)/shard_map/ppermute | solution.py:145
  32.9 12.8 %collective-permute-start.20 = (bf16[384,768]{1,0:T(8,128)(2,1)S(1)}, bf16[384,768]{1,0:T(8,128)(2,1)S(1)}, u32[]{:S(2)}, u32[]{:S(2)}) collective-permute-start(bf16[384,768]{1,0:T(8,128)(2,1)S(1)} %constant_dynamic-update-slice_fusion.2), channel_id=1, source_target_pairs={{0,16},{1,17},{2,18},{3,19},{4,20},{5,21},{6,22},{7,23},{8,24},{9,... | collective-permute-start | bytes 1769480 | tf_op jit(solution)/shard_map/ppermute | solution.py:145
  34.5 11.3 %collective-permute-start.11 = (bf16[384,768]{1,0:T(8,128)(2,1)S(1)}, bf16[384,768]{1,0:T(8,128)(2,1)S(1)}, u32[]{:S(2)}, u32[]{:S(2)}) collective-permute-start(bf16[384,768]{1,0:T(8,128)(2,1)S(1)} %constant_dynamic-update-slice_fusion), channel_id=1, source_target_pairs={{0,1},{1,0},{2,3},{3,2},{4,5},{5,4},{6,7},{7,6},{8,9},{9,8},{10,11... | collective-permute-start | bytes 1769480 | tf_op jit(solution)/shard_map/ppermute | solution.py:145
  36.8 11.7 %collective-permute-start.13 = (bf16[384,768]{1,0:T(8,128)(2,1)S(1)}, bf16[384,768]{1,0:T(8,128)(2,1)S(1)}, u32[]{:S(2)}, u32[]{:S(2)}) collective-permute-start(bf16[384,768]{1,0:T(8,128)(2,1)S(1)} %collective-permute-done.12.refs_21_.refs_22_), channel_id=1, source_target_pairs={{0,1},{1,0},{2,3},{3,2},{4,5},{5,4},{6,7},{7,6},{8,9},{9,8},{10,11... | collective-permute-start | bytes 1769480 | tf_op jit(solution)/shard_map/ppermute | solution.py:145
  40.2 21.5 %collective-permute-start.7 = (bf16[672,768]{1,0:T(8,128)(2,1)S(1)}, bf16[672,768]{1,0:T(8,128)(2,1)S(1)}, u32[]{:S(2)}, u32[]{:S(2)}) collective-permute-start(bf16[672,768]{1,0:T(8,128)(2,1)S(1)} %pad_maximum_fusion), channel_id=1, source_target_pairs={{0,1},{1,0},{2,3},{3,2},{4,5},{5,4},{6,7},{7,6},{8,9},{9,8},{10,11... | collective-permute-start | bytes 3096584 | tf_op jit(solution)/shard_map/ppermute | solution.py:145
  45.8 14.3 %collective-permute-start.18 = (bf16[384,768]{1,0:T(8,128)(2,1)S(1)}, bf16[384,768]{1,0:T(8,128)(2,1)S(1)}, u32[]{:S(2)}, u32[]{:S(2)}) collective-permute-start(bf16[384,768]{1,0:T(8,128)(2,1)S(1)} %constant_dynamic-update-slice_fusion.2), channel_id=1, source_target_pairs={{0,1},{1,0},{2,3},{3,2},{4,5},{5,4},{6,7},{7,6},{8,9},{9,8},{10,11... | collective-permute-start | bytes 1769480 | tf_op jit(solution)/shard_map/ppermute | solution.py:145
  45.8 10.5 %collective-permute-start.9 = (bf16[224,768]{1,0:T(8,128)(2,1)S(1)}, bf16[224,768]{1,0:T(8,128)(2,1)S(1)}, u32[]{:S(2)}, u32[]{:S(2)}) collective-permute-start(bf16[224,768]{1,0:T(8,128)(2,1)S(1)} %collective-permute-done.8.refs_11_.refs_12_), channel_id=1, source_target_pairs={{0,8},{1,9},{2,10},{3,11},{4,0},{5,1},{6,2},{7,3},{8,12},{9,13},{1... | collective-permute-start | bytes 1032200 | tf_op jit(solution)/shard_map/ppermute | solution.py:145
  48.5 13.2 %collective-permute-start.21 = (bf16[384,768]{1,0:T(8,128)(2,1)S(1)}, bf16[384,768]{1,0:T(8,128)(2,1)S(1)}, u32[]{:S(2)}, u32[]{:S(2)}) collective-permute-start(bf16[384,768]{1,0:T(8,128)(2,1)S(1)} %collective-permute-done.20.refs_26_.refs_27_), channel_id=1, source_target_pairs={{0,1},{1,0},{2,3},{3,2},{4,5},{5,4},{6,7},{7,6},{8,9},{9,8},{10,11... | collective-permute-start | bytes 1769480 | tf_op jit(solution)/shard_map/ppermute | solution.py:145
  56.3 15.2 %collective-permute-start.24 = (bf16[384,768]{1,0:T(8,128)(2,1)}, bf16[384,768]{1,0:T(8,128)(2,1)}, u32[]{:S(2)}, u32[]{:S(2)}) collective-permute-start(bf16[384,768]{1,0:T(8,128)(2,1)} %constant_dynamic-update-slice_fusion.4), channel_id=1, source_target_pairs={{0,16},{1,17},{2,18},{3,19},{4,20},{5,21},{6,22},{7,23},{8,24},{9,... | collective-permute-start | bytes 1769480 | tf_op jit(solution)/shard_map/ppermute | solution.py:145
  60.1 21.2 %collective-permute-start.15 = (bf16[672,768]{1,0:T(8,128)(2,1)}, bf16[672,768]{1,0:T(8,128)(2,1)}, u32[]{:S(2)}, u32[]{:S(2)}) collective-permute-start(bf16[672,768]{1,0:T(8,128)(2,1)} %pad_maximum_fusion.1), channel_id=1, source_target_pairs={{0,1},{1,0},{2,3},{3,2},{4,5},{5,4},{6,7},{7,6},{8,9},{9,8},{10,11... | collective-permute-start | bytes 3096584 | tf_op jit(solution)/shard_map/ppermute | solution.py:145
  60.1 9.9 %collective-permute-start.27 = (bf16[192,768]{1,0:T(8,128)(2,1)S(1)}, bf16[192,768]{1,0:T(8,128)(2,1)S(1)}, u32[]{:S(2)}, u32[]{:S(2)}) collective-permute-start(bf16[192,768]{1,0:T(8,128)(2,1)S(1)} %collective-permute-done.6.refs_34_.refs_35_), channel_id=1, source_target_pairs={{0,2},{1,3},{2,0},{3,1},{4,6},{5,7},{6,4},{7,5},{8,10},{9,11},{10,... | collective-permute-start | bytes 884744 | tf_op jit(solution)/shard_map/ppermute | solution.py:145
  61.7 15.3 %collective-permute-start.22 = (bf16[224,768]{1,0:T(8,128)(2,1)S(1)}, bf16[224,768]{1,0:T(8,128)(2,1)}, u32[]{:S(2)}, u32[]{:S(2)}) collective-permute-start(bf16[224,768]{1,0:T(8,128)(2,1)S(1)} %collective-permute-done.9.refs_14_.refs_15_), channel_id=1, source_target_pairs={{0,2},{1,3},{2,0},{3,1},{4,6},{5,7},{6,4},{7,5},{8,10},{9,11},{10,... | collective-permute-start | bytes 1032200 | tf_op jit(solution)/shard_map/ppermute | solution.py:145
  70.0 8.4 %collective-permute-start.28 = (bf16[192,768]{1,0:T(8,128)(2,1)S(1)}, bf16[192,768]{1,0:T(8,128)(2,1)}, u32[]{:S(2)}, u32[]{:S(2)}) collective-permute-start(bf16[192,768]{1,0:T(8,128)(2,1)S(1)} %collective-permute-done.27.refs_35_.refs_36_), channel_id=1, source_target_pairs={{0,16},{1,17},{2,18},{3,19},{4,20},{5,21},{6,22},{7,23},{8,24},{9,... | collective-permute-start | bytes 884744 | tf_op jit(solution)/shard_map/ppermute | solution.py:145
  71.5 9.8 %collective-permute-start.25 = (bf16[384,768]{1,0:T(8,128)(2,1)}, bf16[384,768]{1,0:T(8,128)(2,1)}, u32[]{:S(2)}, u32[]{:S(2)}) collective-permute-start(bf16[384,768]{1,0:T(8,128)(2,1)} %constant_dynamic-update-slice_fusion.4), channel_id=1, source_target_pairs={{0,1},{1,0},{2,3},{3,2},{4,5},{5,4},{6,7},{7,6},{8,9},{9,8},{10,11... | collective-permute-start | bytes 1769480 | tf_op jit(solution)/shard_map/ppermute | solution.py:145
  (49 other events, 605.5 us)

commit v3 on v2

--- a/solution.py
+++ b/solution.py
@@ -252,7 +252,7 @@
 
 
 def attention_part(
-    state, patch, place, term, queries, mixes, qkv, att, mixed, raised, heads, samples
+    state, patch, place, term, queries, mixes, qkv, att, mixed, raised, heads, samples, landed
 ):
     width, tokens = place.target.shape
     each = tokens // samples
@@ -261,6 +261,7 @@
     hidden = jnp.dot(patch.ready()[...], patches, preferred_element_type=F32)
     hidden = hidden + place.ready()[...]
     normed = norm(hidden, term(0), term(1))
+    landed()
     for result, rows, at in product(queries, normed, width):
         qkv[pl.ds(at, rows), :] = result.astype(BF16)
     sample_of = lax.broadcasted_iota(jnp.int32, (each, tokens), 1) // each
@@ -330,6 +331,8 @@
 class Fetched:
     def __init__(self, source, target, sem):
         self.target, self.copy, self.here = target, pltpu.make_async_copy(source, target, sem), False
+
+    def begin(self):
         self.copy.start()
 
     def ready(self):
@@ -386,6 +389,18 @@
     results = [take() for _ in range(2 if "terms" in names else 3)]
     fetched = [Fetched(ref, take(), refs[-1].at[k]) for k, ref in enumerate(given)]
     buffers = fetched[len(names) :]
+    early = {0, 1} if keys[0][0] is None else {which for key, which, _ in keys if key[0] == "p"}
+    soon = [one for k, one in enumerate(buffers) if k in early]
+    later = [one for k, one in enumerate(buffers) if k not in early]
+    for one in fetched[: len(names)] + soon:
+        one.begin()
+
+    def landed():
+        for one in soon:
+            one.ready()
+        for one in later:
+            one.begin()
+
     by_name = dict(zip(names, fetched))
     state, scales, patch, place, out, terms = (
         by_name.get(name) for name in ("state", "scales", "patch", "place", "out", "terms")
@@ -401,7 +416,7 @@
     term = lambda k: mods[pl.ds(k * width, width), :]
     qkv, att, mid, raised = take(), take(), take(), take()
     hidden = attention_part(
-        state, patch, place, term, queries, mixes, qkv, att, mixed, raised, heads, samples
+        state, patch, place, term, queries, mixes, qkv, att, mixed, raised, heads, samples, landed
     )
     drift = feed_part(
         hidden, state, term, out, scales, expands, shrinks, mid, mixed
@@ -463,14 +478,20 @@
     position = lax.axis_index("tm")
     total = value
     before = jnp.zeros_like(value)
-    distance = 1
-    while distance < count:
-        pairs = [(i, i ^ distance) for i in range(count)]
-        other = lax.ppermute(narrow, "tm", pairs).astype(value.dtype)
-        before = jnp.where((position & distance) != 0, before + other, before)
-        total = total + other
+    low = 1
+    while low < count:
+        wide = low in (1, 4) and low * 2 < count
+        distances = (low, 2 * low, 3 * low) if wide else (low,)
+        others = [
+            lax.ppermute(narrow, "tm", [(i, i ^ far) for i in range(count)]) for far in distances
+        ]
+        for far, other in zip(distances, others):
+            other = other.astype(value.dtype)
+            top = 2 * low if far > low else low
+            before = jnp.where((position & top) != 0, before + other, before)
+            total = total + other
         narrow = total.astype(BF16)
-        distance *= 2
+        low *= 4 if wide else 2
     return before
 
 

time: 143 us -> 138 us (0.965)
  waiting for transfers between devices: 61.1 us -> 55.3 us
    ppermute x8 -> x12, waiting for transfers between devices: 17.6 us -> 12 us  [earlier_sum(): lax.ppermute(narrow, 'tm', [(i, i ^ far) for i in range(count)])]
    ppermute x8 -> x12, starting transfers between devices: 12.2 us -> 12.9 us  [earlier_sum(): lax.ppermute(narrow, 'tm', [(i, i ^ far) for i in range(count)])]
  transfers between devices with their start and end apart: 39 -> 43, of which waited for: 22 -> 24; matrix products, arithmetic and copies ran while one was open for 4% -> 4% of each run, Pallas kernels for 2% -> 2%
where the time goes in v3:
time: 138 us
  waiting for transfers between devices  55.3 us (40%)
  starting transfers between devices  38.9 us (28%)
  Pallas kernels  33.6 us (24%)
  local copies, waits for them, and re-layouts  5.31 us (4%)
  other arithmetic  2.38 us (2%)
    ppermute x31, waiting for transfers between devices, _send(): value = lax.ppermute(value, ('group', 'tm'), pairs)  43.3 us
    pallas_call x2, Pallas kernels, run_network(): pl.pallas_call(functools.partial(network_kernel, names, keys, len(buffers...  30.5 us
    ppermute x31, starting transfers between devices, _send(): value = lax.ppermute(value, ('group', 'tm'), pairs)  26 us
    ppermute x12, starting transfers between devices, earlier_sum(): lax.ppermute(narrow, 'tm', [(i, i ^ far) for i in range(count)])  12.9 us
    ppermute x12, waiting for transfers between devices, earlier_sum(): lax.ppermute(narrow, 'tm', [(i, i ^ far) for i in range(count)])  12 us
    pallas_call x1, Pallas kernels, conditioning(): pl.pallas_call(functools.partial(conditioning_kernel, steps, samples), ou...  3.13 us
  transfers between devices with their start and end apart: 43, of which 24 were waited for; matrix products, arithmetic and copies ran while one was open for 4% of the time, Pallas kernels for 2%

profile of v3, /device:TPU:0, one launch (start us, length us, event | category | flops | bytes accessed | tf_op | source)
XLA Modules:
  0.0 137.6 jit_solution(1870073154487950887)
XLA Ops:
  1.6 4.1 %collective-permute-start = (bf16[192,768]{1,0:T(8,128)(2,1)S(1)}, bf16[192,768]{1,0:T(8,128)(2,1)S(1)}, u32[]{:S(2)}, u32[]{:S(2)}) collective-permute-start(bf16[192,768]{1,0:T(8,128)(2,1)S(1)} %get-tuple-element.78.refs_17_.refs_18_), channel_id=1, source_target_pairs={{0,8},{1,9},{2,10},{3,11},{4,0},{5,1},{6,2},{7,3},{8,12},{9,13},{1... | collective-permute-start | bytes 884744 | tf_op jit(solution)/shard_map/ppermute | solution.py:145
  8.8 3.1 %shard_map.163 = (f32[64,384]{1,0:T(8,128)}, f32[32,128]{1,0:T(8,128)}) custom-call(s32[25]{0:T(128)} %times.1, s32[1]{0:T(128)S(6)} %copy.30.window, f32[1000]{0:T(1024)} %constant.26.clone.levels, bf16[256,768]{1,0:T(8,128)(2,1)} %w_in.1, bf16[768,768]{1,0:T(8,128)(2,1)} %w_out.1, f32[4,768]{1,0:T(4,128)} %fusion.5.classes, bf16[288,768]{1,0:T(8,128)(2,1)} %bitcast.38, ...), custom_call_target="tpu_custom_call" | custom-call | tf_op jit(solution)/shard_map/pallas_call | solution.py:86
  13.5 1.6 %collective-permute-start.3 = (bf16[224,768]{1,0:T(8,128)(2,1)S(1)}, bf16[224,768]{1,0:T(8,128)(2,1)S(1)}, u32[]{:S(2)}, u32[]{:S(2)}) collective-permute-start(bf16[224,768]{1,0:T(8,128)(2,1)S(1)} %maximum_maximum_fusion.refs_5_.refs_6_), channel_id=1, source_target_pairs={{0,8},{1,9},{2,10},{3,11},{4,0},{5,1},{6,2},{7,3},{8,12},{9,13},{1... | collective-permute-start | bytes 1032200 | tf_op jit(solution)/shard_map/ppermute | solution.py:145
  17.1 5.1 %collective-permute-done.2.refs_7_.refs_8_ = bf16[224,768]{1,0:T(8,128)(2,1)S(1)} collective-permute-done((bf16[224,768]{1,0:T(8,128)(2,1)S(1)}, bf16[224,768]{1,0:T(8,128)(2,1)S(1)}, u32[]{:S(2)}, u32[]{:S(2)}) %collective-permute-start.2) | collective-permute-done | bytes 344096 | tf_op jit(solution)/shard_map/ppermute | solution.py:145
  24.5 4.3 %collective-permute-done.5.refs_29_.refs_30_ = bf16[192,768]{1,0:T(8,128)(2,1)S(1)} collective-permute-done((bf16[192,768]{1,0:T(8,128)(2,1)S(1)}, bf16[192,768]{1,0:T(8,128)(2,1)S(1)}, u32[]{:S(2)}, u32[]{:S(2)}) %collective-permute-start.5) | collective-permute-done | bytes 294944 | tf_op jit(solution)/shard_map/ppermute | solution.py:145
  30.3 2.5 %collective-permute-start.6 = (bf16[192,768]{1,0:T(8,128)(2,1)S(1)}, bf16[192,768]{1,0:T(8,128)(2,1)S(1)}, u32[]{:S(2)}, u32[]{:S(2)}) collective-permute-start(bf16[192,768]{1,0:T(8,128)(2,1)S(1)} %collective-permute-done.5.refs_29_.refs_30_), channel_id=1, source_target_pairs={{0,8},{1,9},{2,10},{3,11},{4,0},{5,1},{6,2},{7,3},{8,12},{9,13},{1... | collective-permute-start | bytes 884744 | tf_op jit(solution)/shard_map/ppermute | solution.py:145
  34.5 2.3 %collective-permute-done.4.refs_10_.refs_11_ = bf16[224,768]{1,0:T(8,128)(2,1)S(1)} collective-permute-done((bf16[224,768]{1,0:T(8,128)(2,1)S(1)}, bf16[224,768]{1,0:T(8,128)(2,1)S(1)}, u32[]{:S(2)}, u32[]{:S(2)}) %collective-permute-start.4) | collective-permute-done | bytes 344096 | tf_op jit(solution)/shard_map/ppermute | solution.py:145
  37.1 3.2 %collective-permute-done.6.refs_34_.refs_35_ = bf16[192,768]{1,0:T(8,128)(2,1)S(1)} collective-permute-done((bf16[192,768]{1,0:T(8,128)(2,1)S(1)}, bf16[192,768]{1,0:T(8,128)(2,1)S(1)}, u32[]{:S(2)}, u32[]{:S(2)}) %collective-permute-start.6) | collective-permute-done | bytes 294944 | tf_op jit(solution)/shard_map/ppermute | solution.py:145
  40.2 4.1 %collective-permute-done.8.refs_11_.refs_12_ = bf16[224,768]{1,0:T(8,128)(2,1)S(1)} collective-permute-done((bf16[224,768]{1,0:T(8,128)(2,1)S(1)}, bf16[224,768]{1,0:T(8,128)(2,1)S(1)}, u32[]{:S(2)}, u32[]{:S(2)}) %collective-permute-start.8) | collective-permute-done | bytes 344096 | tf_op jit(solution)/shard_map/ppermute | solution.py:145
  45.8 2.5 %collective-permute-start.9 = (bf16[224,768]{1,0:T(8,128)(2,1)S(1)}, bf16[224,768]{1,0:T(8,128)(2,1)S(1)}, u32[]{:S(2)}, u32[]{:S(2)}) collective-permute-start(bf16[224,768]{1,0:T(8,128)(2,1)S(1)} %collective-permute-done.8.refs_11_.refs_12_), channel_id=1, source_target_pairs={{0,8},{1,9},{2,10},{3,11},{4,0},{5,1},{6,2},{7,3},{8,12},{9,13},{1... | collective-permute-start | bytes 1032200 | tf_op jit(solution)/shard_map/ppermute | solution.py:145
  48.5 2.6 %collective-permute-done.17.refs_30_.refs_31_ = bf16[192,768]{1,0:T(8,128)(2,1)S(1)} collective-permute-done((bf16[192,768]{1,0:T(8,128)(2,1)S(1)}, bf16[192,768]{1,0:T(8,128)(2,1)S(1)}, u32[]{:S(2)}, u32[]{:S(2)}) %collective-permute-start.17) | collective-permute-done | bytes 294944 | tf_op jit(solution)/shard_map/ppermute | solution.py:145
  53.1 3.1 %collective-permute-done.9.refs_14_.refs_15_ = bf16[224,768]{1,0:T(8,128)(2,1)S(1)} collective-permute-done((bf16[224,768]{1,0:T(8,128)(2,1)S(1)}, bf16[224,768]{1,0:T(8,128)(2,1)S(1)}, u32[]{:S(2)}, u32[]{:S(2)}) %collective-permute-start.9) | collective-permute-done | bytes 344096 | tf_op jit(solution)/shard_map/ppermute | solution.py:145
  60.0 1.6 %collective-permute-start.27 = (bf16[192,768]{1,0:T(8,128)(2,1)S(1)}, bf16[192,768]{1,0:T(8,128)(2,1)S(1)}, u32[]{:S(2)}, u32[]{:S(2)}) collective-permute-start(bf16[192,768]{1,0:T(8,128)(2,1)S(1)} %collective-permute-done.6.refs_34_.refs_35_), channel_id=1, source_target_pairs={{0,2},{1,3},{2,0},{3,1},{4,6},{5,7},{6,4},{7,5},{8,10},{9,11},{10,... | collective-permute-start | bytes 884744 | tf_op jit(solution)/shard_map/ppermute | solution.py:145
  62.2 7.7 %collective-permute-done.27.refs_35_.refs_36_ = bf16[192,768]{1,0:T(8,128)(2,1)S(1)} collective-permute-done((bf16[192,768]{1,0:T(8,128)(2,1)S(1)}, bf16[192,768]{1,0:T(8,128)(2,1)S(1)}, u32[]{:S(2)}, u32[]{:S(2)}) %collective-permute-start.27) | collective-permute-done | bytes 294944 | tf_op jit(solution)/shard_map/ppermute | solution.py:145
  71.8 5.1 %collective-permute-done.22.refs_15_.refs_16_ = bf16[224,768]{1,0:T(8,128)(2,1)} collective-permute-done((bf16[224,768]{1,0:T(8,128)(2,1)S(1)}, bf16[224,768]{1,0:T(8,128)(2,1)}, u32[]{:S(2)}, u32[]{:S(2)}) %collective-permute-start.22) | collective-permute-done | bytes 344096 | tf_op jit(solution)/shard_map/ppermute | solution.py:145
  81.1 16.1 %shard_map.164 = (f32[64,256]{1,0:T(8,128)S(1)}, bf16[64,256]{1,0:T(8,128)(2,1)S(1)}, f32[128,384]{1,0:T(8,128)S(1)}) custom-call(f32[64,256]{1,0:T(8,128)S(1)} %reshape.14.refs_0_, bf16[768,64]{1,0:T(8,128)(2,1)S(1)} %bitcast.31, f32[768,256]{1,0:T(8,128)} %constant.25.clone.refs_2_.refs_3_, bf16[64,768]{1,0:T(8,128)(2,1)S(1)} %bitcast.33, ...), custom_call_target="tpu_custom_call" | custom-call | flops 3623878656 | bytes 14155776 | tf_op jit(solution)/shard_map/pallas_call | solution.py:462
  100.7 2.1 %collective-permute-done.32 = bf16[64,256]{1,0:T(8,128)(2,1)S(1)} collective-permute-done((bf16[64,256]{1,0:T(8,128)(2,1)S(1)}, bf16[64,256]{1,0:T(8,128)(2,1)S(1)}, u32[]{:S(2)}, u32[]{:S(2)}) %collective-permute-start.32) | collective-permute-done | bytes 32800 | tf_op jit(solution)/shard_map/ppermute | solution.py:486
  102.8 2.0 %collective-permute-start.36 = (bf16[64,256]{1,0:T(8,128)(2,1)S(1)}, bf16[64,256]{1,0:T(8,128)(2,1)S(1)}, u32[]{:S(2)}, u32[]{:S(2)}) collective-permute-start(bf16[64,256]{1,0:T(8,128)(2,1)S(1)} %fusion), channel_id=1, source_target_pairs={{0,12},{1,13},{2,14},{3,15},{4,8},{5,9},{6,10},{7,11},{8,4},{9,5},... | collective-permute-start | bytes 98312 | tf_op jit(solution)/shard_map/ppermute | solution.py:486
  104.8 1.7 %collective-permute-start.35 = (bf16[64,256]{1,0:T(8,128)(2,1)S(1)}, bf16[64,256]{1,0:T(8,128)(2,1)S(1)}, u32[]{:S(2)}, u32[]{:S(2)}) collective-permute-start(bf16[64,256]{1,0:T(8,128)(2,1)S(1)} %fusion), channel_id=1, source_target_pairs={{0,8},{1,9},{2,10},{3,11},{4,12},{5,13},{6,14},{7,15},{8,0},{9,1},... | collective-permute-start | bytes 98312 | tf_op jit(solution)/shard_map/ppermute | solution.py:486
  110.4 14.3 %shard_map.165 = (f32[64,256]{1,0:T(8,128)S(1)}, bf16[64,256]{1,0:T(8,128)(2,1)S(1)}) custom-call(f32[128,384]{1,0:T(8,128)S(1)} %get-tuple-element.72.refs_0_, f32[64,256]{1,0:T(8,128)S(1)} %fusion.2.refs_1_, bf16[768,64]{1,0:T(8,128)(2,1)S(1)} %bitcast.32, f32[768,256]{1,0:T(8,128)} %constant.25.clone.refs_2_.refs_3_, bf16[64,768]{1,0:T(8,128)(2,1)S(1)} %bitcast.34, ...), custom_call_target="tpu_custom_call" | custom-call | flops 3623878656 | bytes 14155776 | tf_op jit(solution)/shard_map/pallas_call | solution.py:462
  124.8 1.6 %collective-permute-start.38 = (bf16[64,256]{1,0:T(8,128)(2,1)S(1)}, bf16[64,256]{1,0:T(8,128)(2,1)S(1)}, u32[]{:S(2)}, u32[]{:S(2)}) collective-permute-start(bf16[64,256]{1,0:T(8,128)(2,1)S(1)} %get-tuple-element.75), channel_id=1, source_target_pairs={{0,2},{1,3},{2,0},{3,1},{4,6},{5,7},{6,4},{7,5},{8,10},{9,11},{10,... | collective-permute-start | bytes 98312 | tf_op jit(solution)/shard_map/ppermute | solution.py:486
  126.6 1.8 %collective-permute-done.39 = bf16[64,256]{1,0:T(8,128)(2,1)S(1)} collective-permute-done((bf16[64,256]{1,0:T(8,128)(2,1)S(1)}, bf16[64,256]{1,0:T(8,128)(2,1)S(1)}, u32[]{:S(2)}, u32[]{:S(2)}) %collective-permute-start.39) | collective-permute-done | bytes 32800 | tf_op jit(solution)/shard_map/ppermute | solution.py:486
  128.8 2.9 %collective-permute-start.42 = (bf16[64,256]{1,0:T(8,128)(2,1)S(1)}, bf16[64,256]{1,0:T(8,128)(2,1)S(1)}, u32[]{:S(2)}, u32[]{:S(2)}) collective-permute-start(bf16[64,256]{1,0:T(8,128)(2,1)S(1)} %fusion.1), channel_id=1, source_target_pairs={{0,12},{1,13},{2,14},{3,15},{4,8},{5,9},{6,10},{7,11},{8,4},{9,5},... | collective-permute-start | bytes 98312 | tf_op jit(solution)/shard_map/ppermute | solution.py:486
  133.3 1.7 %collective-permute-done.42 = bf16[64,256]{1,0:T(8,128)(2,1)S(1)} collective-permute-done((bf16[64,256]{1,0:T(8,128)(2,1)S(1)}, bf16[64,256]{1,0:T(8,128)(2,1)S(1)}, u32[]{:S(2)}, u32[]{:S(2)}) %collective-permute-start.42) | collective-permute-done | bytes 32800 | tf_op jit(solution)/shard_map/ppermute | solution.py:486
  (162 shorter events, 39.5 us)
Async XLA Ops:
  1.6 13.5 %collective-permute-start = (bf16[192,768]{1,0:T(8,128)(2,1)S(1)}, bf16[192,768]{1,0:T(8,128)(2,1)S(1)}, u32[]{:S(2)}, u32[]{:S(2)}) collective-permute-start(bf16[192,768]{1,0:T(8,128)(2,1)S(1)} %get-tuple-element.78.refs_17_.refs_18_), channel_id=1, source_target_pairs={{0,8},{1,9},{2,10},{3,11},{4,0},{5,1},{6,2},{7,3},{8,12},{9,13},{1... | collective-permute-start | bytes 884744 | tf_op jit(solution)/shard_map/ppermute | solution.py:145
  5.7 9.8 %collective-permute-start.10 = (bf16[192,768]{1,0:T(8,128)(2,1)S(1)}, bf16[192,768]{1,0:T(8,128)(2,1)S(1)}, u32[]{:S(2)}, u32[]{:S(2)}) collective-permute-start(bf16[192,768]{1,0:T(8,128)(2,1)S(1)} %get-tuple-element.78.refs_17_.refs_18_), channel_id=1, source_target_pairs={{0,2},{1,3},{2,0},{3,1},{4,6},{5,7},{6,4},{7,5},{8,10},{9,11},{10,... | collective-permute-start | bytes 884744 | tf_op jit(solution)/shard_map/ppermute | solution.py:145
  12.9 9.3 %collective-permute-start.2 = (bf16[224,768]{1,0:T(8,128)(2,1)S(1)}, bf16[224,768]{1,0:T(8,128)(2,1)S(1)}, u32[]{:S(2)}, u32[]{:S(2)}) collective-permute-start(bf16[224,768]{1,0:T(8,128)(2,1)S(1)} %maximum_maximum_fusion.refs_5_.refs_6_), channel_id=1, source_target_pairs={{0,2},{1,3},{2,0},{3,1},{4,6},{5,7},{6,4},{7,5},{8,10},{9,11},{10,... | collective-permute-start | bytes 1032200 | tf_op jit(solution)/shard_map/ppermute | solution.py:145
  13.5 11.0 %collective-permute-start.3 = (bf16[224,768]{1,0:T(8,128)(2,1)S(1)}, bf16[224,768]{1,0:T(8,128)(2,1)S(1)}, u32[]{:S(2)}, u32[]{:S(2)}) collective-permute-start(bf16[224,768]{1,0:T(8,128)(2,1)S(1)} %maximum_maximum_fusion.refs_5_.refs_6_), channel_id=1, source_target_pairs={{0,8},{1,9},{2,10},{3,11},{4,0},{5,1},{6,2},{7,3},{8,12},{9,13},{1... | collective-permute-start | bytes 1032200 | tf_op jit(solution)/shard_map/ppermute | solution.py:145
  15.1 13.7 %collective-permute-start.5 = (bf16[192,768]{1,0:T(8,128)(2,1)S(1)}, bf16[192,768]{1,0:T(8,128)(2,1)S(1)}, u32[]{:S(2)}, u32[]{:S(2)}) collective-permute-start(bf16[192,768]{1,0:T(8,128)(2,1)S(1)} %collective-permute-done.refs_24_.refs_25_), channel_id=1, source_target_pairs={{0,8},{1,9},{2,10},{3,11},{4,0},{5,1},{6,2},{7,3},{8,12},{9,13},{1... | collective-permute-start | bytes 884744 | tf_op jit(solution)/shard_map/ppermute | solution.py:145
  15.5 17.3 %collective-permute-start.12 = (bf16[384,768]{1,0:T(8,128)(2,1)S(1)}, bf16[384,768]{1,0:T(8,128)(2,1)S(1)}, u32[]{:S(2)}, u32[]{:S(2)}) collective-permute-start(bf16[384,768]{1,0:T(8,128)(2,1)S(1)} %constant_dynamic-update-slice_fusion), channel_id=1, source_target_pairs={{0,16},{1,17},{2,18},{3,19},{4,20},{5,21},{6,22},{7,23},{8,24},{9,... | collective-permute-start | bytes 1769480 | tf_op jit(solution)/shard_map/ppermute | solution.py:145
  17.1 15.9 %collective-permute-start.19 = (bf16[384,768]{1,0:T(8,128)(2,1)S(1)}, bf16[384,768]{1,0:T(8,128)(2,1)S(1)}, u32[]{:S(2)}, u32[]{:S(2)}) collective-permute-start(bf16[384,768]{1,0:T(8,128)(2,1)S(1)} %pad_maximum_fusion.2), channel_id=1, source_target_pairs={{0,1},{1,0},{2,3},{3,2},{4,5},{5,4},{6,7},{7,6},{8,9},{9,8},{10,11... | collective-permute-start | bytes 1769480 | tf_op jit(solution)/shard_map/ppermute | solution.py:145
  24.5 8.4 %collective-permute-start.1 = (bf16[224,768]{1,0:T(8,128)(2,1)S(1)}, bf16[224,768]{1,0:T(8,128)(2,1)S(1)}, u32[]{:S(2)}, u32[]{:S(2)}) collective-permute-start(bf16[224,768]{1,0:T(8,128)(2,1)S(1)} %maximum_maximum_fusion.refs_5_.refs_6_), channel_id=1, source_target_pairs={{0,1},{1,0},{2,3},{3,2},{4,5},{5,4},{6,7},{7,6},{8,9},{9,8},{10,11... | collective-permute-start | bytes 1032200 | tf_op jit(solution)/shard_map/ppermute | solution.py:145
  28.8 8.1 %collective-permute-start.4 = (bf16[224,768]{1,0:T(8,128)(2,1)S(1)}, bf16[224,768]{1,0:T(8,128)(2,1)S(1)}, u32[]{:S(2)}, u32[]{:S(2)}) collective-permute-start(bf16[224,768]{1,0:T(8,128)(2,1)S(1)} %collective-permute-done.3.refs_9_.refs_10_), channel_id=1, source_target_pairs={{0,2},{1,3},{2,0},{3,1},{4,6},{5,7},{6,4},{7,5},{8,10},{9,11},{10,... | collective-permute-start | bytes 1032200 | tf_op jit(solution)/shard_map/ppermute | solution.py:145
  30.3 9.9 %collective-permute-start.6 = (bf16[192,768]{1,0:T(8,128)(2,1)S(1)}, bf16[192,768]{1,0:T(8,128)(2,1)S(1)}, u32[]{:S(2)}, u32[]{:S(2)}) collective-permute-start(bf16[192,768]{1,0:T(8,128)(2,1)S(1)} %collective-permute-done.5.refs_29_.refs_30_), channel_id=1, source_target_pairs={{0,8},{1,9},{2,10},{3,11},{4,0},{5,1},{6,2},{7,3},{8,12},{9,13},{1... | collective-permute-start | bytes 884744 | tf_op jit(solution)/shard_map/ppermute | solution.py:145
  32.8 11.6 %collective-permute-start.8 = (bf16[224,768]{1,0:T(8,128)(2,1)S(1)}, bf16[224,768]{1,0:T(8,128)(2,1)S(1)}, u32[]{:S(2)}, u32[]{:S(2)}) collective-permute-start(bf16[224,768]{1,0:T(8,128)(2,1)S(1)} %collective-permute-done.3.refs_9_.refs_10_), channel_id=1, source_target_pairs={{0,8},{1,9},{2,10},{3,11},{4,0},{5,1},{6,2},{7,3},{8,12},{9,13},{1... | collective-permute-start | bytes 1032200 | tf_op jit(solution)/shard_map/ppermute | solution.py:145
  33.0 12.8 %collective-permute-start.20 = (bf16[384,768]{1,0:T(8,128)(2,1)S(1)}, bf16[384,768]{1,0:T(8,128)(2,1)S(1)}, u32[]{:S(2)}, u32[]{:S(2)}) collective-permute-start(bf16[384,768]{1,0:T(8,128)(2,1)S(1)} %constant_dynamic-update-slice_fusion.2), channel_id=1, source_target_pairs={{0,16},{1,17},{2,18},{3,19},{4,20},{5,21},{6,22},{7,23},{8,24},{9,... | collective-permute-start | bytes 1769480 | tf_op jit(solution)/shard_map/ppermute | solution.py:145
  34.5 11.3 %collective-permute-start.11 = (bf16[384,768]{1,0:T(8,128)(2,1)S(1)}, bf16[384,768]{1,0:T(8,128)(2,1)S(1)}, u32[]{:S(2)}, u32[]{:S(2)}) collective-permute-start(bf16[384,768]{1,0:T(8,128)(2,1)S(1)} %constant_dynamic-update-slice_fusion), channel_id=1, source_target_pairs={{0,1},{1,0},{2,3},{3,2},{4,5},{5,4},{6,7},{7,6},{8,9},{9,8},{10,11... | collective-permute-start | bytes 1769480 | tf_op jit(solution)/shard_map/ppermute | solution.py:145
  36.8 11.5 %collective-permute-start.13 = (bf16[384,768]{1,0:T(8,128)(2,1)S(1)}, bf16[384,768]{1,0:T(8,128)(2,1)S(1)}, u32[]{:S(2)}, u32[]{:S(2)}) collective-permute-start(bf16[384,768]{1,0:T(8,128)(2,1)S(1)} %collective-permute-done.12.refs_21_.refs_22_), channel_id=1, source_target_pairs={{0,1},{1,0},{2,3},{3,2},{4,5},{5,4},{6,7},{7,6},{8,9},{9,8},{10,11... | collective-permute-start | bytes 1769480 | tf_op jit(solution)/shard_map/ppermute | solution.py:145
  40.2 21.3 %collective-permute-start.7 = (bf16[672,768]{1,0:T(8,128)(2,1)S(1)}, bf16[672,768]{1,0:T(8,128)(2,1)S(1)}, u32[]{:S(2)}, u32[]{:S(2)}) collective-permute-start(bf16[672,768]{1,0:T(8,128)(2,1)S(1)} %pad_maximum_fusion), channel_id=1, source_target_pairs={{0,1},{1,0},{2,3},{3,2},{4,5},{5,4},{6,7},{7,6},{8,9},{9,8},{10,11... | collective-permute-start | bytes 3096584 | tf_op jit(solution)/shard_map/ppermute | solution.py:145
  45.8 14.2 %collective-permute-start.18 = (bf16[384,768]{1,0:T(8,128)(2,1)S(1)}, bf16[384,768]{1,0:T(8,128)(2,1)S(1)}, u32[]{:S(2)}, u32[]{:S(2)}) collective-permute-start(bf16[384,768]{1,0:T(8,128)(2,1)S(1)} %constant_dynamic-update-slice_fusion.2), channel_id=1, source_target_pairs={{0,1},{1,0},{2,3},{3,2},{4,5},{5,4},{6,7},{7,6},{8,9},{9,8},{10,11... | collective-permute-start | bytes 1769480 | tf_op jit(solution)/shard_map/ppermute | solution.py:145
  45.8 10.5 %collective-permute-start.9 = (bf16[224,768]{1,0:T(8,128)(2,1)S(1)}, bf16[224,768]{1,0:T(8,128)(2,1)S(1)}, u32[]{:S(2)}, u32[]{:S(2)}) collective-permute-start(bf16[224,768]{1,0:T(8,128)(2,1)S(1)} %collective-permute-done.8.refs_11_.refs_12_), channel_id=1, source_target_pairs={{0,8},{1,9},{2,10},{3,11},{4,0},{5,1},{6,2},{7,3},{8,12},{9,13},{1... | collective-permute-start | bytes 1032200 | tf_op jit(solution)/shard_map/ppermute | solution.py:145
  48.3 13.2 %collective-permute-start.21 = (bf16[384,768]{1,0:T(8,128)(2,1)S(1)}, bf16[384,768]{1,0:T(8,128)(2,1)S(1)}, u32[]{:S(2)}, u32[]{:S(2)}) collective-permute-start(bf16[384,768]{1,0:T(8,128)(2,1)S(1)} %collective-permute-done.20.refs_26_.refs_27_), channel_id=1, source_target_pairs={{0,1},{1,0},{2,3},{3,2},{4,5},{5,4},{6,7},{7,6},{8,9},{9,8},{10,11... | collective-permute-start | bytes 1769480 | tf_op jit(solution)/shard_map/ppermute | solution.py:145
  56.3 15.2 %collective-permute-start.24 = (bf16[384,768]{1,0:T(8,128)(2,1)}, bf16[384,768]{1,0:T(8,128)(2,1)}, u32[]{:S(2)}, u32[]{:S(2)}) collective-permute-start(bf16[384,768]{1,0:T(8,128)(2,1)} %constant_dynamic-update-slice_fusion.4), channel_id=1, source_target_pairs={{0,16},{1,17},{2,18},{3,19},{4,20},{5,21},{6,22},{7,23},{8,24},{9,... | collective-permute-start | bytes 1769480 | tf_op jit(solution)/shard_map/ppermute | solution.py:145
  59.9 21.1 %collective-permute-start.15 = (bf16[672,768]{1,0:T(8,128)(2,1)}, bf16[672,768]{1,0:T(8,128)(2,1)}, u32[]{:S(2)}, u32[]{:S(2)}) collective-permute-start(bf16[672,768]{1,0:T(8,128)(2,1)} %pad_maximum_fusion.1), channel_id=1, source_target_pairs={{0,1},{1,0},{2,3},{3,2},{4,5},{5,4},{6,7},{7,6},{8,9},{9,8},{10,11... | collective-permute-start | bytes 3096584 | tf_op jit(solution)/shard_map/ppermute | solution.py:145
  60.0 9.9 %collective-permute-start.27 = (bf16[192,768]{1,0:T(8,128)(2,1)S(1)}, bf16[192,768]{1,0:T(8,128)(2,1)S(1)}, u32[]{:S(2)}, u32[]{:S(2)}) collective-permute-start(bf16[192,768]{1,0:T(8,128)(2,1)S(1)} %collective-permute-done.6.refs_34_.refs_35_), channel_id=1, source_target_pairs={{0,2},{1,3},{2,0},{3,1},{4,6},{5,7},{6,4},{7,5},{8,10},{9,11},{10,... | collective-permute-start | bytes 884744 | tf_op jit(solution)/shard_map/ppermute | solution.py:145
  61.6 15.3 %collective-permute-start.22 = (bf16[224,768]{1,0:T(8,128)(2,1)S(1)}, bf16[224,768]{1,0:T(8,128)(2,1)}, u32[]{:S(2)}, u32[]{:S(2)}) collective-permute-start(bf16[224,768]{1,0:T(8,128)(2,1)S(1)} %collective-permute-done.9.refs_14_.refs_15_), channel_id=1, source_target_pairs={{0,2},{1,3},{2,0},{3,1},{4,6},{5,7},{6,4},{7,5},{8,10},{9,11},{10,... | collective-permute-start | bytes 1032200 | tf_op jit(solution)/shard_map/ppermute | solution.py:145
  69.8 8.4 %collective-permute-start.28 = (bf16[192,768]{1,0:T(8,128)(2,1)S(1)}, bf16[192,768]{1,0:T(8,128)(2,1)}, u32[]{:S(2)}, u32[]{:S(2)}) collective-permute-start(bf16[192,768]{1,0:T(8,128)(2,1)S(1)} %collective-permute-done.27.refs_35_.refs_36_), channel_id=1, source_target_pairs={{0,16},{1,17},{2,18},{3,19},{4,20},{5,21},{6,22},{7,23},{8,24},{9,... | collective-permute-start | bytes 884744 | tf_op jit(solution)/shard_map/ppermute | solution.py:145
  71.3 9.7 %collective-permute-start.25 = (bf16[384,768]{1,0:T(8,128)(2,1)}, bf16[384,768]{1,0:T(8,128)(2,1)}, u32[]{:S(2)}, u32[]{:S(2)}) collective-permute-start(bf16[384,768]{1,0:T(8,128)(2,1)} %constant_dynamic-update-slice_fusion.4), channel_id=1, source_target_pairs={{0,1},{1,0},{2,3},{3,2},{4,5},{5,4},{6,7},{7,6},{8,9},{9,8},{10,11... | collective-permute-start | bytes 1769480 | tf_op jit(solution)/shard_map/ppermute | solution.py:145
  (53 other events, 625.3 us)

commit v4 on v3

--- a/solution.py
+++ b/solution.py
@@ -398,8 +398,8 @@
     def landed():
         for one in soon:
             one.ready()
-        for one in later:
-            one.begin()
+        while later:
+            later.pop(0).begin()
 
     by_name = dict(zip(names, fetched))
     state, scales, patch, place, out, terms = (
@@ -410,6 +410,7 @@
     if terms is None:
         flat = results[2]
         own_terms(packs, flat, samples)
+        landed()
     else:
         flat = terms.ready()
     spread_terms(flat, mods, nb, samples)

time: 138 us -> 137 us (level)
  transfers between devices with their start and end apart: 43 -> 43, of which waited for: 24 -> 23; matrix products, arithmetic and copies ran while one was open for 4% -> 4% of each run, Pallas kernels for 2% -> 2%
where the time goes in v4:
time: 137 us
  waiting for transfers between devices  55.2 us (40%)
  starting transfers between devices  39 us (28%)
  Pallas kernels  33.2 us (24%)
  local copies, waits for them, and re-layouts  5.31 us (4%)
  other arithmetic  2.38 us (2%)
    ppermute x31, waiting for transfers between devices, _send(): value = lax.ppermute(value, ('group', 'tm'), pairs)  43.4 us
    pallas_call x2, Pallas kernels, run_network(): pl.pallas_call(functools.partial(network_kernel, names, keys, len(buffers...  30.1 us
    ppermute x31, starting transfers between devices, _send(): value = lax.ppermute(value, ('group', 'tm'), pairs)  26.1 us
    ppermute x12, starting transfers between devices, earlier_sum(): lax.ppermute(narrow, 'tm', [(i, i ^ far) for i in range(count)])  12.9 us
    ppermute x12, waiting for transfers between devices, earlier_sum(): lax.ppermute(narrow, 'tm', [(i, i ^ far) for i in range(count)])  11.8 us
    pallas_call x1, Pallas kernels, conditioning(): pl.pallas_call(functools.partial(conditioning_kernel, steps, samples), ou...  3.13 us
  transfers between devices with their start and end apart: 43, of which 23 were waited for; matrix products, arithmetic and copies ran while one was open for 4% of the time, Pallas kernels for 2%

profile of v4, /device:TPU:0, one launch (start us, length us, event | category | flops | bytes accessed | tf_op | source)
XLA Modules:
  0.0 137.2 jit_solution(7939407305577924064)
XLA Ops:
  1.6 4.1 %collective-permute-start = (bf16[192,768]{1,0:T(8,128)(2,1)S(1)}, bf16[192,768]{1,0:T(8,128)(2,1)S(1)}, u32[]{:S(2)}, u32[]{:S(2)}) collective-permute-start(bf16[192,768]{1,0:T(8,128)(2,1)S(1)} %get-tuple-element.78.refs_17_.refs_18_), channel_id=1, source_target_pairs={{0,8},{1,9},{2,10},{3,11},{4,0},{5,1},{6,2},{7,3},{8,12},{9,13},{1... | collective-permute-start | bytes 884744 | tf_op jit(solution)/shard_map/ppermute | solution.py:145
  8.8 3.1 %shard_map.163 = (f32[64,384]{1,0:T(8,128)}, f32[32,128]{1,0:T(8,128)}) custom-call(s32[25]{0:T(128)} %times.1, s32[1]{0:T(128)S(6)} %copy.30.window, f32[1000]{0:T(1024)} %constant.26.clone.levels, bf16[256,768]{1,0:T(8,128)(2,1)} %w_in.1, bf16[768,768]{1,0:T(8,128)(2,1)} %w_out.1, f32[4,768]{1,0:T(4,128)} %fusion.5.classes, bf16[288,768]{1,0:T(8,128)(2,1)} %bitcast.38, ...), custom_call_target="tpu_custom_call" | custom-call | tf_op jit(solution)/shard_map/pallas_call | solution.py:86
  13.5 1.6 %collective-permute-start.3 = (bf16[224,768]{1,0:T(8,128)(2,1)S(1)}, bf16[224,768]{1,0:T(8,128)(2,1)S(1)}, u32[]{:S(2)}, u32[]{:S(2)}) collective-permute-start(bf16[224,768]{1,0:T(8,128)(2,1)S(1)} %maximum_maximum_fusion.refs_5_.refs_6_), channel_id=1, source_target_pairs={{0,8},{1,9},{2,10},{3,11},{4,0},{5,1},{6,2},{7,3},{8,12},{9,13},{1... | collective-permute-start | bytes 1032200 | tf_op jit(solution)/shard_map/ppermute | solution.py:145
  17.1 5.1 %collective-permute-done.2.refs_7_.refs_8_ = bf16[224,768]{1,0:T(8,128)(2,1)S(1)} collective-permute-done((bf16[224,768]{1,0:T(8,128)(2,1)S(1)}, bf16[224,768]{1,0:T(8,128)(2,1)S(1)}, u32[]{:S(2)}, u32[]{:S(2)}) %collective-permute-start.2) | collective-permute-done | bytes 344096 | tf_op jit(solution)/shard_map/ppermute | solution.py:145
  24.5 4.3 %collective-permute-done.5.refs_29_.refs_30_ = bf16[192,768]{1,0:T(8,128)(2,1)S(1)} collective-permute-done((bf16[192,768]{1,0:T(8,128)(2,1)S(1)}, bf16[192,768]{1,0:T(8,128)(2,1)S(1)}, u32[]{:S(2)}, u32[]{:S(2)}) %collective-permute-start.5) | collective-permute-done | bytes 294944 | tf_op jit(solution)/shard_map/ppermute | solution.py:145
  30.3 2.5 %collective-permute-start.6 = (bf16[192,768]{1,0:T(8,128)(2,1)S(1)}, bf16[192,768]{1,0:T(8,128)(2,1)S(1)}, u32[]{:S(2)}, u32[]{:S(2)}) collective-permute-start(bf16[192,768]{1,0:T(8,128)(2,1)S(1)} %collective-permute-done.5.refs_29_.refs_30_), channel_id=1, source_target_pairs={{0,8},{1,9},{2,10},{3,11},{4,0},{5,1},{6,2},{7,3},{8,12},{9,13},{1... | collective-permute-start | bytes 884744 | tf_op jit(solution)/shard_map/ppermute | solution.py:145
  34.5 2.3 %collective-permute-done.4.refs_10_.refs_11_ = bf16[224,768]{1,0:T(8,128)(2,1)S(1)} collective-permute-done((bf16[224,768]{1,0:T(8,128)(2,1)S(1)}, bf16[224,768]{1,0:T(8,128)(2,1)S(1)}, u32[]{:S(2)}, u32[]{:S(2)}) %collective-permute-start.4) | collective-permute-done | bytes 344096 | tf_op jit(solution)/shard_map/ppermute | solution.py:145
  37.1 3.2 %collective-permute-done.6.refs_34_.refs_35_ = bf16[192,768]{1,0:T(8,128)(2,1)S(1)} collective-permute-done((bf16[192,768]{1,0:T(8,128)(2,1)S(1)}, bf16[192,768]{1,0:T(8,128)(2,1)S(1)}, u32[]{:S(2)}, u32[]{:S(2)}) %collective-permute-start.6) | collective-permute-done | bytes 294944 | tf_op jit(solution)/shard_map/ppermute | solution.py:145
  40.2 4.1 %collective-permute-done.8.refs_11_.refs_12_ = bf16[224,768]{1,0:T(8,128)(2,1)S(1)} collective-permute-done((bf16[224,768]{1,0:T(8,128)(2,1)S(1)}, bf16[224,768]{1,0:T(8,128)(2,1)S(1)}, u32[]{:S(2)}, u32[]{:S(2)}) %collective-permute-start.8) | collective-permute-done | bytes 344096 | tf_op jit(solution)/shard_map/ppermute | solution.py:145
  45.8 2.7 %collective-permute-start.9 = (bf16[224,768]{1,0:T(8,128)(2,1)S(1)}, bf16[224,768]{1,0:T(8,128)(2,1)S(1)}, u32[]{:S(2)}, u32[]{:S(2)}) collective-permute-start(bf16[224,768]{1,0:T(8,128)(2,1)S(1)} %collective-permute-done.8.refs_11_.refs_12_), channel_id=1, source_target_pairs={{0,8},{1,9},{2,10},{3,11},{4,0},{5,1},{6,2},{7,3},{8,12},{9,13},{1... | collective-permute-start | bytes 1032200 | tf_op jit(solution)/shard_map/ppermute | solution.py:145
  48.5 2.6 %collective-permute-done.17.refs_30_.refs_31_ = bf16[192,768]{1,0:T(8,128)(2,1)S(1)} collective-permute-done((bf16[192,768]{1,0:T(8,128)(2,1)S(1)}, bf16[192,768]{1,0:T(8,128)(2,1)S(1)}, u32[]{:S(2)}, u32[]{:S(2)}) %collective-permute-start.17) | collective-permute-done | bytes 294944 | tf_op jit(solution)/shard_map/ppermute | solution.py:145
  53.1 3.1 %collective-permute-done.9.refs_14_.refs_15_ = bf16[224,768]{1,0:T(8,128)(2,1)S(1)} collective-permute-done((bf16[224,768]{1,0:T(8,128)(2,1)S(1)}, bf16[224,768]{1,0:T(8,128)(2,1)S(1)}, u32[]{:S(2)}, u32[]{:S(2)}) %collective-permute-start.9) | collective-permute-done | bytes 344096 | tf_op jit(solution)/shard_map/ppermute | solution.py:145
  60.1 1.6 %collective-permute-start.27 = (bf16[192,768]{1,0:T(8,128)(2,1)S(1)}, bf16[192,768]{1,0:T(8,128)(2,1)S(1)}, u32[]{:S(2)}, u32[]{:S(2)}) collective-permute-start(bf16[192,768]{1,0:T(8,128)(2,1)S(1)} %collective-permute-done.6.refs_34_.refs_35_), channel_id=1, source_target_pairs={{0,2},{1,3},{2,0},{3,1},{4,6},{5,7},{6,4},{7,5},{8,10},{9,11},{10,... | collective-permute-start | bytes 884744 | tf_op jit(solution)/shard_map/ppermute | solution.py:145
  62.3 7.7 %collective-permute-done.27.refs_35_.refs_36_ = bf16[192,768]{1,0:T(8,128)(2,1)S(1)} collective-permute-done((bf16[192,768]{1,0:T(8,128)(2,1)S(1)}, bf16[192,768]{1,0:T(8,128)(2,1)S(1)}, u32[]{:S(2)}, u32[]{:S(2)}) %collective-permute-start.27) | collective-permute-done | bytes 294944 | tf_op jit(solution)/shard_map/ppermute | solution.py:145
  72.0 5.1 %collective-permute-done.22.refs_15_.refs_16_ = bf16[224,768]{1,0:T(8,128)(2,1)} collective-permute-done((bf16[224,768]{1,0:T(8,128)(2,1)S(1)}, bf16[224,768]{1,0:T(8,128)(2,1)}, u32[]{:S(2)}, u32[]{:S(2)}) %collective-permute-start.22) | collective-permute-done | bytes 344096 | tf_op jit(solution)/shard_map/ppermute | solution.py:145
  81.3 15.8 %shard_map.164 = (f32[64,256]{1,0:T(8,128)S(1)}, bf16[64,256]{1,0:T(8,128)(2,1)S(1)}, f32[128,384]{1,0:T(8,128)S(1)}) custom-call(f32[64,256]{1,0:T(8,128)S(1)} %reshape.14.refs_0_, bf16[768,64]{1,0:T(8,128)(2,1)S(1)} %bitcast.31, f32[768,256]{1,0:T(8,128)} %constant.25.clone.refs_2_.refs_3_, bf16[64,768]{1,0:T(8,128)(2,1)S(1)} %bitcast.33, ...), custom_call_target="tpu_custom_call" | custom-call | flops 3623878656 | bytes 14155776 | tf_op jit(solution)/shard_map/pallas_call | solution.py:463
  100.5 2.1 %collective-permute-done.32 = bf16[64,256]{1,0:T(8,128)(2,1)S(1)} collective-permute-done((bf16[64,256]{1,0:T(8,128)(2,1)S(1)}, bf16[64,256]{1,0:T(8,128)(2,1)S(1)}, u32[]{:S(2)}, u32[]{:S(2)}) %collective-permute-start.32) | collective-permute-done | bytes 32800 | tf_op jit(solution)/shard_map/ppermute | solution.py:487
  102.6 1.7 %collective-permute-start.36 = (bf16[64,256]{1,0:T(8,128)(2,1)S(1)}, bf16[64,256]{1,0:T(8,128)(2,1)S(1)}, u32[]{:S(2)}, u32[]{:S(2)}) collective-permute-start(bf16[64,256]{1,0:T(8,128)(2,1)S(1)} %fusion), channel_id=1, source_target_pairs={{0,12},{1,13},{2,14},{3,15},{4,8},{5,9},{6,10},{7,11},{8,4},{9,5},... | collective-permute-start | bytes 98312 | tf_op jit(solution)/shard_map/ppermute | solution.py:487
  104.3 1.8 %collective-permute-start.35 = (bf16[64,256]{1,0:T(8,128)(2,1)S(1)}, bf16[64,256]{1,0:T(8,128)(2,1)S(1)}, u32[]{:S(2)}, u32[]{:S(2)}) collective-permute-start(bf16[64,256]{1,0:T(8,128)(2,1)S(1)} %fusion), channel_id=1, source_target_pairs={{0,8},{1,9},{2,10},{3,11},{4,12},{5,13},{6,14},{7,15},{8,0},{9,1},... | collective-permute-start | bytes 98312 | tf_op jit(solution)/shard_map/ppermute | solution.py:487
  110.0 14.3 %shard_map.165 = (f32[64,256]{1,0:T(8,128)S(1)}, bf16[64,256]{1,0:T(8,128)(2,1)S(1)}) custom-call(f32[128,384]{1,0:T(8,128)S(1)} %get-tuple-element.72.refs_0_, f32[64,256]{1,0:T(8,128)S(1)} %fusion.2.refs_1_, bf16[768,64]{1,0:T(8,128)(2,1)S(1)} %bitcast.32, f32[768,256]{1,0:T(8,128)} %constant.25.clone.refs_2_.refs_3_, bf16[64,768]{1,0:T(8,128)(2,1)S(1)} %bitcast.34, ...), custom_call_target="tpu_custom_call" | custom-call | flops 3623878656 | bytes 14155776 | tf_op jit(solution)/shard_map/pallas_call | solution.py:463
  124.4 1.6 %collective-permute-start.38 = (bf16[64,256]{1,0:T(8,128)(2,1)S(1)}, bf16[64,256]{1,0:T(8,128)(2,1)S(1)}, u32[]{:S(2)}, u32[]{:S(2)}) collective-permute-start(bf16[64,256]{1,0:T(8,128)(2,1)S(1)} %get-tuple-element.75), channel_id=1, source_target_pairs={{0,2},{1,3},{2,0},{3,1},{4,6},{5,7},{6,4},{7,5},{8,10},{9,11},{10,... | collective-permute-start | bytes 98312 | tf_op jit(solution)/shard_map/ppermute | solution.py:487
  126.3 1.8 %collective-permute-done.39 = bf16[64,256]{1,0:T(8,128)(2,1)S(1)} collective-permute-done((bf16[64,256]{1,0:T(8,128)(2,1)S(1)}, bf16[64,256]{1,0:T(8,128)(2,1)S(1)}, u32[]{:S(2)}, u32[]{:S(2)}) %collective-permute-start.39) | collective-permute-done | bytes 32800 | tf_op jit(solution)/shard_map/ppermute | solution.py:487
  128.5 2.9 %collective-permute-start.42 = (bf16[64,256]{1,0:T(8,128)(2,1)S(1)}, bf16[64,256]{1,0:T(8,128)(2,1)S(1)}, u32[]{:S(2)}, u32[]{:S(2)}) collective-permute-start(bf16[64,256]{1,0:T(8,128)(2,1)S(1)} %fusion.1), channel_id=1, source_target_pairs={{0,12},{1,13},{2,14},{3,15},{4,8},{5,9},{6,10},{7,11},{8,4},{9,5},... | collective-permute-start | bytes 98312 | tf_op jit(solution)/shard_map/ppermute | solution.py:487
  132.9 1.7 %collective-permute-done.42 = bf16[64,256]{1,0:T(8,128)(2,1)S(1)} collective-permute-done((bf16[64,256]{1,0:T(8,128)(2,1)S(1)}, bf16[64,256]{1,0:T(8,128)(2,1)S(1)}, u32[]{:S(2)}, u32[]{:S(2)}) %collective-permute-start.42) | collective-permute-done | bytes 32800 | tf_op jit(solution)/shard_map/ppermute | solution.py:487
  (162 shorter events, 39.5 us)
Async XLA Ops:
  1.6 13.5 %collective-permute-start = (bf16[192,768]{1,0:T(8,128)(2,1)S(1)}, bf16[192,768]{1,0:T(8,128)(2,1)S(1)}, u32[]{:S(2)}, u32[]{:S(2)}) collective-permute-start(bf16[192,768]{1,0:T(8,128)(2,1)S(1)} %get-tuple-element.78.refs_17_.refs_18_), channel_id=1, source_target_pairs={{0,8},{1,9},{2,10},{3,11},{4,0},{5,1},{6,2},{7,3},{8,12},{9,13},{1... | collective-permute-start | bytes 884744 | tf_op jit(solution)/shard_map/ppermute | solution.py:145
  5.7 9.8 %collective-permute-start.10 = (bf16[192,768]{1,0:T(8,128)(2,1)S(1)}, bf16[192,768]{1,0:T(8,128)(2,1)S(1)}, u32[]{:S(2)}, u32[]{:S(2)}) collective-permute-start(bf16[192,768]{1,0:T(8,128)(2,1)S(1)} %get-tuple-element.78.refs_17_.refs_18_), channel_id=1, source_target_pairs={{0,2},{1,3},{2,0},{3,1},{4,6},{5,7},{6,4},{7,5},{8,10},{9,11},{10,... | collective-permute-start | bytes 884744 | tf_op jit(solution)/shard_map/ppermute | solution.py:145
  12.9 9.3 %collective-permute-start.2 = (bf16[224,768]{1,0:T(8,128)(2,1)S(1)}, bf16[224,768]{1,0:T(8,128)(2,1)S(1)}, u32[]{:S(2)}, u32[]{:S(2)}) collective-permute-start(bf16[224,768]{1,0:T(8,128)(2,1)S(1)} %maximum_maximum_fusion.refs_5_.refs_6_), channel_id=1, source_target_pairs={{0,2},{1,3},{2,0},{3,1},{4,6},{5,7},{6,4},{7,5},{8,10},{9,11},{10,... | collective-permute-start | bytes 1032200 | tf_op jit(solution)/shard_map/ppermute | solution.py:145
  13.5 11.0 %collective-permute-start.3 = (bf16[224,768]{1,0:T(8,128)(2,1)S(1)}, bf16[224,768]{1,0:T(8,128)(2,1)S(1)}, u32[]{:S(2)}, u32[]{:S(2)}) collective-permute-start(bf16[224,768]{1,0:T(8,128)(2,1)S(1)} %maximum_maximum_fusion.refs_5_.refs_6_), channel_id=1, source_target_pairs={{0,8},{1,9},{2,10},{3,11},{4,0},{5,1},{6,2},{7,3},{8,12},{9,13},{1... | collective-permute-start | bytes 1032200 | tf_op jit(solution)/shard_map/ppermute | solution.py:145
  15.1 13.7 %collective-permute-start.5 = (bf16[192,768]{1,0:T(8,128)(2,1)S(1)}, bf16[192,768]{1,0:T(8,128)(2,1)S(1)}, u32[]{:S(2)}, u32[]{:S(2)}) collective-permute-start(bf16[192,768]{1,0:T(8,128)(2,1)S(1)} %collective-permute-done.refs_24_.refs_25_), channel_id=1, source_target_pairs={{0,8},{1,9},{2,10},{3,11},{4,0},{5,1},{6,2},{7,3},{8,12},{9,13},{1... | collective-permute-start | bytes 884744 | tf_op jit(solution)/shard_map/ppermute | solution.py:145
  15.5 17.3 %collective-permute-start.12 = (bf16[384,768]{1,0:T(8,128)(2,1)S(1)}, bf16[384,768]{1,0:T(8,128)(2,1)S(1)}, u32[]{:S(2)}, u32[]{:S(2)}) collective-permute-start(bf16[384,768]{1,0:T(8,128)(2,1)S(1)} %constant_dynamic-update-slice_fusion), channel_id=1, source_target_pairs={{0,16},{1,17},{2,18},{3,19},{4,20},{5,21},{6,22},{7,23},{8,24},{9,... | collective-permute-start | bytes 1769480 | tf_op jit(solution)/shard_map/ppermute | solution.py:145
  17.1 15.9 %collective-permute-start.19 = (bf16[384,768]{1,0:T(8,128)(2,1)S(1)}, bf16[384,768]{1,0:T(8,128)(2,1)S(1)}, u32[]{:S(2)}, u32[]{:S(2)}) collective-permute-start(bf16[384,768]{1,0:T(8,128)(2,1)S(1)} %pad_maximum_fusion.2), channel_id=1, source_target_pairs={{0,1},{1,0},{2,3},{3,2},{4,5},{5,4},{6,7},{7,6},{8,9},{9,8},{10,11... | collective-permute-start | bytes 1769480 | tf_op jit(solution)/shard_map/ppermute | solution.py:145
  24.5 8.4 %collective-permute-start.1 = (bf16[224,768]{1,0:T(8,128)(2,1)S(1)}, bf16[224,768]{1,0:T(8,128)(2,1)S(1)}, u32[]{:S(2)}, u32[]{:S(2)}) collective-permute-start(bf16[224,768]{1,0:T(8,128)(2,1)S(1)} %maximum_maximum_fusion.refs_5_.refs_6_), channel_id=1, source_target_pairs={{0,1},{1,0},{2,3},{3,2},{4,5},{5,4},{6,7},{7,6},{8,9},{9,8},{10,11... | collective-permute-start | bytes 1032200 | tf_op jit(solution)/shard_map/ppermute | solution.py:145
  28.8 8.1 %collective-permute-start.4 = (bf16[224,768]{1,0:T(8,128)(2,1)S(1)}, bf16[224,768]{1,0:T(8,128)(2,1)S(1)}, u32[]{:S(2)}, u32[]{:S(2)}) collective-permute-start(bf16[224,768]{1,0:T(8,128)(2,1)S(1)} %collective-permute-done.3.refs_9_.refs_10_), channel_id=1, source_target_pairs={{0,2},{1,3},{2,0},{3,1},{4,6},{5,7},{6,4},{7,5},{8,10},{9,11},{10,... | collective-permute-start | bytes 1032200 | tf_op jit(solution)/shard_map/ppermute | solution.py:145
  30.3 9.9 %collective-permute-start.6 = (bf16[192,768]{1,0:T(8,128)(2,1)S(1)}, bf16[192,768]{1,0:T(8,128)(2,1)S(1)}, u32[]{:S(2)}, u32[]{:S(2)}) collective-permute-start(bf16[192,768]{1,0:T(8,128)(2,1)S(1)} %collective-permute-done.5.refs_29_.refs_30_), channel_id=1, source_target_pairs={{0,8},{1,9},{2,10},{3,11},{4,0},{5,1},{6,2},{7,3},{8,12},{9,13},{1... | collective-permute-start | bytes 884744 | tf_op jit(solution)/shard_map/ppermute | solution.py:145
  32.8 11.6 %collective-permute-start.8 = (bf16[224,768]{1,0:T(8,128)(2,1)S(1)}, bf16[224,768]{1,0:T(8,128)(2,1)S(1)}, u32[]{:S(2)}, u32[]{:S(2)}) collective-permute-start(bf16[224,768]{1,0:T(8,128)(2,1)S(1)} %collective-permute-done.3.refs_9_.refs_10_), channel_id=1, source_target_pairs={{0,8},{1,9},{2,10},{3,11},{4,0},{5,1},{6,2},{7,3},{8,12},{9,13},{1... | collective-permute-start | bytes 1032200 | tf_op jit(solution)/shard_map/ppermute | solution.py:145
  33.0 12.8 %collective-permute-start.20 = (bf16[384,768]{1,0:T(8,128)(2,1)S(1)}, bf16[384,768]{1,0:T(8,128)(2,1)S(1)}, u32[]{:S(2)}, u32[]{:S(2)}) collective-permute-start(bf16[384,768]{1,0:T(8,128)(2,1)S(1)} %constant_dynamic-update-slice_fusion.2), channel_id=1, source_target_pairs={{0,16},{1,17},{2,18},{3,19},{4,20},{5,21},{6,22},{7,23},{8,24},{9,... | collective-permute-start | bytes 1769480 | tf_op jit(solution)/shard_map/ppermute | solution.py:145
  34.5 11.3 %collective-permute-start.11 = (bf16[384,768]{1,0:T(8,128)(2,1)S(1)}, bf16[384,768]{1,0:T(8,128)(2,1)S(1)}, u32[]{:S(2)}, u32[]{:S(2)}) collective-permute-start(bf16[384,768]{1,0:T(8,128)(2,1)S(1)} %constant_dynamic-update-slice_fusion), channel_id=1, source_target_pairs={{0,1},{1,0},{2,3},{3,2},{4,5},{5,4},{6,7},{7,6},{8,9},{9,8},{10,11... | collective-permute-start | bytes 1769480 | tf_op jit(solution)/shard_map/ppermute | solution.py:145
  36.8 11.7 %collective-permute-start.13 = (bf16[384,768]{1,0:T(8,128)(2,1)S(1)}, bf16[384,768]{1,0:T(8,128)(2,1)S(1)}, u32[]{:S(2)}, u32[]{:S(2)}) collective-permute-start(bf16[384,768]{1,0:T(8,128)(2,1)S(1)} %collective-permute-done.12.refs_21_.refs_22_), channel_id=1, source_target_pairs={{0,1},{1,0},{2,3},{3,2},{4,5},{5,4},{6,7},{7,6},{8,9},{9,8},{10,11... | collective-permute-start | bytes 1769480 | tf_op jit(solution)/shard_map/ppermute | solution.py:145
  40.2 21.5 %collective-permute-start.7 = (bf16[672,768]{1,0:T(8,128)(2,1)S(1)}, bf16[672,768]{1,0:T(8,128)(2,1)S(1)}, u32[]{:S(2)}, u32[]{:S(2)}) collective-permute-start(bf16[672,768]{1,0:T(8,128)(2,1)S(1)} %pad_maximum_fusion), channel_id=1, source_target_pairs={{0,1},{1,0},{2,3},{3,2},{4,5},{5,4},{6,7},{7,6},{8,9},{9,8},{10,11... | collective-permute-start | bytes 3096584 | tf_op jit(solution)/shard_map/ppermute | solution.py:145
  45.8 14.3 %collective-permute-start.18 = (bf16[384,768]{1,0:T(8,128)(2,1)S(1)}, bf16[384,768]{1,0:T(8,128)(2,1)S(1)}, u32[]{:S(2)}, u32[]{:S(2)}) collective-permute-start(bf16[384,768]{1,0:T(8,128)(2,1)S(1)} %constant_dynamic-update-slice_fusion.2), channel_id=1, source_target_pairs={{0,1},{1,0},{2,3},{3,2},{4,5},{5,4},{6,7},{7,6},{8,9},{9,8},{10,11... | collective-permute-start | bytes 1769480 | tf_op jit(solution)/shard_map/ppermute | solution.py:145
  45.8 10.5 %collective-permute-start.9 = (bf16[224,768]{1,0:T(8,128)(2,1)S(1)}, bf16[224,768]{1,0:T(8,128)(2,1)S(1)}, u32[]{:S(2)}, u32[]{:S(2)}) collective-permute-start(bf16[224,768]{1,0:T(8,128)(2,1)S(1)} %collective-permute-done.8.refs_11_.refs_12_), channel_id=1, source_target_pairs={{0,8},{1,9},{2,10},{3,11},{4,0},{5,1},{6,2},{7,3},{8,12},{9,13},{1... | collective-permute-start | bytes 1032200 | tf_op jit(solution)/shard_map/ppermute | solution.py:145
  48.5 13.2 %collective-permute-start.21 = (bf16[384,768]{1,0:T(8,128)(2,1)S(1)}, bf16[384,768]{1,0:T(8,128)(2,1)S(1)}, u32[]{:S(2)}, u32[]{:S(2)}) collective-permute-start(bf16[384,768]{1,0:T(8,128)(2,1)S(1)} %collective-permute-done.20.refs_26_.refs_27_), channel_id=1, source_target_pairs={{0,1},{1,0},{2,3},{3,2},{4,5},{5,4},{6,7},{7,6},{8,9},{9,8},{10,11... | collective-permute-start | bytes 1769480 | tf_op jit(solution)/shard_map/ppermute | solution.py:145
  56.3 15.3 %collective-permute-start.24 = (bf16[384,768]{1,0:T(8,128)(2,1)}, bf16[384,768]{1,0:T(8,128)(2,1)}, u32[]{:S(2)}, u32[]{:S(2)}) collective-permute-start(bf16[384,768]{1,0:T(8,128)(2,1)} %constant_dynamic-update-slice_fusion.4), channel_id=1, source_target_pairs={{0,16},{1,17},{2,18},{3,19},{4,20},{5,21},{6,22},{7,23},{8,24},{9,... | collective-permute-start | bytes 1769480 | tf_op jit(solution)/shard_map/ppermute | solution.py:145
  60.1 21.1 %collective-permute-start.15 = (bf16[672,768]{1,0:T(8,128)(2,1)}, bf16[672,768]{1,0:T(8,128)(2,1)}, u32[]{:S(2)}, u32[]{:S(2)}) collective-permute-start(bf16[672,768]{1,0:T(8,128)(2,1)} %pad_maximum_fusion.1), channel_id=1, source_target_pairs={{0,1},{1,0},{2,3},{3,2},{4,5},{5,4},{6,7},{7,6},{8,9},{9,8},{10,11... | collective-permute-start | bytes 3096584 | tf_op jit(solution)/shard_map/ppermute | solution.py:145
  60.1 9.9 %collective-permute-start.27 = (bf16[192,768]{1,0:T(8,128)(2,1)S(1)}, bf16[192,768]{1,0:T(8,128)(2,1)S(1)}, u32[]{:S(2)}, u32[]{:S(2)}) collective-permute-start(bf16[192,768]{1,0:T(8,128)(2,1)S(1)} %collective-permute-done.6.refs_34_.refs_35_), channel_id=1, source_target_pairs={{0,2},{1,3},{2,0},{3,1},{4,6},{5,7},{6,4},{7,5},{8,10},{9,11},{10,... | collective-permute-start | bytes 884744 | tf_op jit(solution)/shard_map/ppermute | solution.py:145
  61.8 15.3 %collective-permute-start.22 = (bf16[224,768]{1,0:T(8,128)(2,1)S(1)}, bf16[224,768]{1,0:T(8,128)(2,1)}, u32[]{:S(2)}, u32[]{:S(2)}) collective-permute-start(bf16[224,768]{1,0:T(8,128)(2,1)S(1)} %collective-permute-done.9.refs_14_.refs_15_), channel_id=1, source_target_pairs={{0,2},{1,3},{2,0},{3,1},{4,6},{5,7},{6,4},{7,5},{8,10},{9,11},{10,... | collective-permute-start | bytes 1032200 | tf_op jit(solution)/shard_map/ppermute | solution.py:145
  70.0 8.4 %collective-permute-start.28 = (bf16[192,768]{1,0:T(8,128)(2,1)S(1)}, bf16[192,768]{1,0:T(8,128)(2,1)}, u32[]{:S(2)}, u32[]{:S(2)}) collective-permute-start(bf16[192,768]{1,0:T(8,128)(2,1)S(1)} %collective-permute-done.27.refs_35_.refs_36_), channel_id=1, source_target_pairs={{0,16},{1,17},{2,18},{3,19},{4,20},{5,21},{6,22},{7,23},{8,24},{9,... | collective-permute-start | bytes 884744 | tf_op jit(solution)/shard_map/ppermute | solution.py:145
  71.5 9.7 %collective-permute-start.25 = (bf16[384,768]{1,0:T(8,128)(2,1)}, bf16[384,768]{1,0:T(8,128)(2,1)}, u32[]{:S(2)}, u32[]{:S(2)}) collective-permute-start(bf16[384,768]{1,0:T(8,128)(2,1)} %constant_dynamic-update-slice_fusion.4), channel_id=1, source_target_pairs={{0,1},{1,0},{2,3},{3,2},{4,5},{5,4},{6,7},{7,6},{8,9},{9,8},{10,11... | collective-permute-start | bytes 1769480 | tf_op jit(solution)/shard_map/ppermute | solution.py:145
  (53 other events, 627.3 us)
